TPU v7x, 32 devices: a whole 2x2x4 slice. The times are simulated.
32 devices in a mesh: replica: 4 (over x, core), shard: 8 (over z, y).
Axes of the slice: x: 2, y: 2, z: 4, core: 2. Of those that a mesh axis runs over, the one named last changes fastest.
Arguments:
- images: bfloat16 [128, 197, 768], P(('replica', 'shard')), may hold values from -6 to 6
- routes: int32 [128, 197, 2], P(('replica', 'shard')), may hold values from 0 to 7, all different within a row; in each aligned block of 788 rows (0 to 787, 788 to 1575, ..., all dimensions but the last counted through in order) at most 275 rows name the same one
- cotangent: bfloat16 [128, 197, 768], P(('replica', 'shard')), may hold values from -6 to 6
- ln1_gain: bfloat16 [768], P('shard'), may hold values from 0.5 to 1.5
- ln1_bias: bfloat16 [768], P('shard'), may hold values from -1.75 to 1.75
- qkv_weight: bfloat16 [768, 2304], P('shard'), may hold values from -0.21875 to 0.21875
- q_bias: bfloat16 [768], P('shard'), may hold values from -1.75 to 1.75
- v_bias: bfloat16 [768], P('shard'), may hold values from -1.75 to 1.75
- out_weight: bfloat16 [768, 768], P('shard'), may hold values from -1.25 to 1.25
- out_bias: bfloat16 [768], P('shard'), may hold values from -1.75 to 1.75
- ln2_gain: bfloat16 [768], P('shard'), may hold values from 0.5 to 1.5
- ln2_bias: bfloat16 [768], P('shard'), may hold values from -1.75 to 1.75
- router_weight: bfloat16 [768, 8], P('shard'), may hold values from -0.15625 to 0.15625
- expert_in: bfloat16 [8, 768, 3072], P('shard'), may hold values from -0.21875 to 0.21875
- expert_in_bias: bfloat16 [8, 3072], P('shard'), may hold values from -0.625 to 0.625
- expert_out: bfloat16 [8, 3072, 768], P('shard'), may hold values from -1.75 to 1.75
- expert_out_bias: bfloat16 [8, 768], P('shard'), may hold values from -6 to 6
Outputs:
- output: bfloat16 [128, 197, 768], P(('replica', 'shard'))
- input_grad: bfloat16 [128, 197, 768], P(('replica', 'shard'))
- ln1_gain_grad: float32 [768], P('shard')
- ln1_bias_grad: float32 [768], P('shard')
- qkv_weight_grad: float32 [768, 2304], P('shard')
- q_bias_grad: float32 [768], P('shard')
- v_bias_grad: float32 [768], P('shard')
- out_weight_grad: float32 [768, 768], P('shard')
- out_bias_grad: float32 [768], P('shard')
- ln2_gain_grad: float32 [768], P('shard')
- ln2_bias_grad: float32 [768], P('shard')
- router_weight_grad: float32 [768, 8], P('shard')
- expert_in_grad: float32 [8, 768, 3072], P('shard')
- expert_in_bias_grad: float32 [8, 3072], P('shard')
- expert_out_grad: float32 [8, 3072, 768], P('shard')
- expert_out_bias_grad: float32 [8, 768], P('shard')
Inputs may be any that keep to these rules, and one draw needn't show every extreme that they name: `routes`: each token names two different experts. Within the rows of one device (aligned blocks of 788 tokens in image order) no expert is named by more than 275 copies, a bound that some block reaches.
All inputs are finite; a program needn't handle non-finite values.
Results may differ from a plain program's by a relative error of at most 0.022.
Values may be sent and summed in bfloat16 or wider, within the bound.
No kernel may reach another device: no remote copies, remote signals or barrier semaphores. Data moves between devices by JAX's collectives and lax.ppermute only.
A program may use at most 256 MiB of HBM per device.

v0:
```python
import jax
import jax.numpy as jnp
from jax import lax
from jax.sharding import PartitionSpec as P

HEADS = 12
HEAD_DIM = 64


eps_norm = 1e-06


def normalize(values):
    average = jnp.mean(values, -1, keepdims=True)
    centred = values - average
    variance = jnp.mean(centred * centred, -1, keepdims=True)
    inverse = lax.rsqrt(variance + eps_norm)
    return (centred * inverse, inverse)


def norm_back(grad_out, scaled, inverse, gain_vec):
    gain_grad = jnp.sum(grad_out * scaled, 0)
    shift_grad = jnp.sum(grad_out, 0)
    grad_scaled = grad_out * gain_vec
    first_term = jnp.mean(grad_scaled, -1, keepdims=True)
    second_term = jnp.mean(grad_scaled * scaled, -1, keepdims=True)
    return (inverse * (grad_scaled - first_term - scaled * second_term), gain_grad, shift_grad)


def slot_index(route_ids, experts, capacity):
    flat_ids = route_ids.reshape(-1)
    onehot = (flat_ids[:, None] == jnp.arange(experts, dtype=jnp.int32)[None, :]).astype(jnp.int32)
    ranking = jnp.sum((jnp.cumsum(onehot, 0) - 1) * onehot, 1)
    return flat_ids * capacity + ranking


def per_device(
    images,
    routes,
    cotangent,
    ln1_gain,
    ln1_bias,
    qkv_weight,
    q_bias,
    v_bias,
    out_weight,
    out_bias,
    ln2_gain,
    ln2_bias,
    router_weight,
    expert_in,
    expert_in_bias,
    expert_out,
    expert_out_bias,
):
    highest = lax.Precision.HIGHEST
    experts = lax.axis_size("shard")
    images_here, seq_len, model_width = images.shape
    tokens_here = images_here * seq_len
    capacity = 14 * tokens_here // (5 * experts)
    factor = HEAD_DIM ** (-0.5)
    gathered = (
        lax.all_gather(ln1_gain, "shard", axis=0, tiled=True),
        lax.all_gather(ln1_bias, "shard", axis=0, tiled=True),
        lax.all_gather(qkv_weight, "shard", axis=0, tiled=True),
        lax.all_gather(q_bias, "shard", axis=0, tiled=True),
        lax.all_gather(v_bias, "shard", axis=0, tiled=True),
        lax.all_gather(out_weight, "shard", axis=0, tiled=True),
        lax.all_gather(out_bias, "shard", axis=0, tiled=True),
        lax.all_gather(ln2_gain, "shard", axis=0, tiled=True),
        lax.all_gather(ln2_bias, "shard", axis=0, tiled=True),
        lax.all_gather(router_weight, "shard", axis=0, tiled=True),
    )
    (
        gain_one,
        shift_one,
        qkv_full,
        query_bias,
        value_bias,
        out_full,
        out_shift,
        gain_two,
        shift_two,
        router_full,
    ) = gathered
    row_values = images.reshape(tokens_here, model_width).astype(jnp.float32)
    scaled_one, inverse_one = normalize(row_values)
    normed = (scaled_one * gain_one.astype(jnp.float32) + shift_one.astype(jnp.float32)).astype(
        jnp.bfloat16
    )
    key_zeros = jnp.zeros((model_width,), jnp.float32)
    qkv_shift = jnp.concatenate(
        [query_bias.astype(jnp.float32), key_zeros, value_bias.astype(jnp.float32)]
    )
    projected = (jnp.dot(normed, qkv_full, preferred_element_type=jnp.float32) + qkv_shift).astype(
        jnp.bfloat16
    )
    heads_view = projected.reshape(images_here, seq_len, 3, HEADS, HEAD_DIM)
    queries = heads_view[:, :, 0]
    keys_all = heads_view[:, :, 1]
    values_all = heads_view[:, :, 2]
    scores = (
        jnp.einsum("ishd,ithd->ihst", queries, keys_all, preferred_element_type=jnp.float32)
        * factor
    )
    row_max = jnp.max(scores, -1, keepdims=True)
    exp_scores = jnp.exp(scores - row_max)
    row_total = jnp.sum(exp_scores, -1, keepdims=True)
    attn_probs = exp_scores / row_total
    log_total = row_max + jnp.log(row_total)
    attended = jnp.einsum(
        "ihst,ithd->ishd",
        attn_probs.astype(jnp.bfloat16),
        values_all,
        preferred_element_type=jnp.float32,
    )
    attended = attended.reshape(tokens_here, model_width).astype(jnp.bfloat16)
    branch = jnp.dot(attended, out_full, preferred_element_type=jnp.float32) + out_shift.astype(
        jnp.float32
    )
    middle = row_values + branch
    scaled_two, inverse_two = normalize(middle)
    normed_two = (scaled_two * gain_two.astype(jnp.float32) + shift_two.astype(jnp.float32)).astype(
        jnp.bfloat16
    )
    logits = jnp.dot(normed_two, router_full, preferred_element_type=jnp.float32)
    router_probs = jax.nn.softmax(logits, axis=-1)
    route_rows = routes.reshape(tokens_here, 2)
    chosen = (route_rows[:, :, None] == jnp.arange(experts, dtype=jnp.int32)[None, None, :]).astype(
        jnp.float32
    )
    gate_values = jnp.sum(router_probs[:, None, :] * chosen, -1)
    slot_ids = slot_index(route_rows, experts, capacity)
    copies = jnp.broadcast_to(normed_two[:, None, :], (tokens_here, 2, model_width)).reshape(
        tokens_here * 2, model_width
    )
    outgoing = jnp.zeros((experts * capacity, model_width), jnp.bfloat16).at[slot_ids].set(copies)
    arrived = lax.all_to_all(
        outgoing.reshape(experts, capacity, model_width),
        "shard",
        split_axis=0,
        concat_axis=0,
        tiled=True,
    )
    arrived = arrived.reshape(experts * capacity, model_width)
    inner_act = jnp.dot(arrived, expert_in[0], preferred_element_type=jnp.float32) + expert_in_bias[
        0
    ].astype(jnp.float32)
    hidden = jax.nn.gelu(inner_act).astype(jnp.bfloat16)
    outer_act = (
        jnp.dot(hidden, expert_out[0], preferred_element_type=jnp.float32)
        + expert_out_bias[0].astype(jnp.float32)
    ).astype(jnp.bfloat16)
    returned = lax.all_to_all(
        outer_act.reshape(experts, capacity, model_width),
        "shard",
        split_axis=0,
        concat_axis=0,
        tiled=True,
    )
    returned = returned.reshape(experts * capacity, model_width)[slot_ids].reshape(
        tokens_here, 2, model_width
    )
    mixed_rows = middle + jnp.sum(gate_values[:, :, None] * returned.astype(jnp.float32), 1)
    output = mixed_rows.reshape(images.shape).astype(jnp.bfloat16)
    regathered = (
        lax.all_gather(ln1_gain, "shard", axis=0, tiled=True),
        lax.all_gather(qkv_weight, "shard", axis=0, tiled=True),
        lax.all_gather(out_weight, "shard", axis=0, tiled=True),
        lax.all_gather(ln2_gain, "shard", axis=0, tiled=True),
        lax.all_gather(router_weight, "shard", axis=0, tiled=True),
    )
    gain_back_one, qkv_back, out_back, gain_back_two, router_back = regathered
    grad_out = cotangent.reshape(tokens_here, model_width).astype(jnp.float32)
    gate_grads = jnp.sum(grad_out[:, None, :] * returned.astype(jnp.float32), -1)
    sent_grads = (
        (gate_values[:, :, None] * grad_out[:, None, :])
        .astype(jnp.bfloat16)
        .reshape(tokens_here * 2, model_width)
    )
    grad_buffer = (
        jnp.zeros((experts * capacity, model_width), jnp.bfloat16).at[slot_ids].set(sent_grads)
    )
    outer_grad = lax.all_to_all(
        grad_buffer.reshape(experts, capacity, model_width),
        "shard",
        split_axis=0,
        concat_axis=0,
        tiled=True,
    )
    outer_grad = outer_grad.reshape(experts * capacity, model_width)
    expert_out_grad = jnp.einsum(
        "rf,rd->fd", hidden, outer_grad, preferred_element_type=jnp.float32
    )[None]
    expert_out_bias_grad = jnp.sum(outer_grad.astype(jnp.float32), 0)[None]
    hidden_grad = jnp.einsum(
        "rd,fd->rf", outer_grad, expert_out[0], preferred_element_type=jnp.float32
    )
    gelu_pull = jax.vjp(jax.nn.gelu, inner_act)[1]
    inner_grad = gelu_pull(hidden_grad)[0].astype(jnp.bfloat16)
    expert_in_grad = jnp.einsum(
        "rd,rf->df", arrived, inner_grad, preferred_element_type=jnp.float32
    )[None]
    expert_in_bias_grad = jnp.sum(inner_grad.astype(jnp.float32), 0)[None]
    arrived_grad = jnp.einsum(
        "rf,df->rd", inner_grad, expert_in[0], preferred_element_type=jnp.float32
    ).astype(jnp.bfloat16)
    back_grads = lax.all_to_all(
        arrived_grad.reshape(experts, capacity, model_width),
        "shard",
        split_axis=0,
        concat_axis=0,
        tiled=True,
    )
    back_grads = back_grads.reshape(experts * capacity, model_width)[slot_ids].reshape(
        tokens_here, 2, model_width
    )
    prob_grads = jnp.sum(gate_grads[:, :, None] * chosen, 1)
    logit_grads = router_probs * (
        prob_grads - jnp.sum(router_probs * prob_grads, -1, keepdims=True)
    )
    router_grad = jnp.einsum(
        "td,te->de", normed_two.astype(jnp.float32), logit_grads, precision=highest
    )
    normed_two_grad = jnp.einsum(
        "te,de->td", logit_grads, router_back.astype(jnp.float32), precision=highest
    )
    normed_two_grad = normed_two_grad + jnp.sum(back_grads.astype(jnp.float32), 1)
    middle_norm_grad, gain_two_grad, shift_two_grad = norm_back(
        normed_two_grad, scaled_two, inverse_two, gain_back_two.astype(jnp.float32)
    )
    middle_grad = grad_out + middle_norm_grad
    branch_grad = middle_grad.astype(jnp.bfloat16)
    out_shift_grad = jnp.sum(branch_grad.astype(jnp.float32), 0)
    out_full_grad = jnp.einsum(
        "td,te->de", attended, branch_grad, preferred_element_type=jnp.float32
    )
    attended_grad = jnp.einsum(
        "te,de->td", branch_grad, out_back, preferred_element_type=jnp.float32
    ).astype(jnp.bfloat16)
    grad_heads = attended_grad.reshape(images_here, seq_len, HEADS, HEAD_DIM)
    scores_back = (
        jnp.einsum("ishd,ithd->ihst", queries, keys_all, preferred_element_type=jnp.float32)
        * factor
    )
    probs_back = jnp.exp(scores_back - log_total)
    values_grad = jnp.einsum(
        "ihst,ishd->ithd",
        probs_back.astype(jnp.bfloat16),
        grad_heads,
        preferred_element_type=jnp.float32,
    )
    prob_back_grad = jnp.einsum(
        "ishd,ithd->ihst", grad_heads, values_all, preferred_element_type=jnp.float32
    )
    score_grad = (
        probs_back * (prob_back_grad - jnp.sum(probs_back * prob_back_grad, -1, keepdims=True))
    ).astype(jnp.bfloat16)
    query_grad = (
        jnp.einsum("ihst,ithd->ishd", score_grad, keys_all, preferred_element_type=jnp.float32)
        * factor
    )
    key_grad = (
        jnp.einsum("ihst,ishd->ithd", score_grad, queries, preferred_element_type=jnp.float32)
        * factor
    )
    projected_grad = (
        jnp.stack([query_grad, key_grad, values_grad], 2)
        .reshape(tokens_here, 3 * model_width)
        .astype(jnp.bfloat16)
    )
    qkv_full_grad = jnp.einsum(
        "td,te->de", normed, projected_grad, preferred_element_type=jnp.float32
    )
    projected_sums = jnp.sum(projected_grad.astype(jnp.float32), 0)
    query_bias_grad = projected_sums[:model_width]
    value_bias_grad = projected_sums[2 * model_width :]
    normed_grad = jnp.einsum(
        "te,de->td", projected_grad, qkv_back, preferred_element_type=jnp.float32
    )
    rows_norm_grad, gain_one_grad, shift_one_grad = norm_back(
        normed_grad, scaled_one, inverse_one, gain_back_one.astype(jnp.float32)
    )
    input_grad = (middle_grad + rows_norm_grad).astype(jnp.bfloat16).reshape(images.shape)
    owned = (
        lax.psum_scatter(
            gain_one_grad.astype(jnp.bfloat16), "shard", scatter_dimension=0, tiled=True
        ).astype(jnp.float32),
        lax.psum_scatter(
            shift_one_grad.astype(jnp.bfloat16), "shard", scatter_dimension=0, tiled=True
        ).astype(jnp.float32),
        lax.psum_scatter(
            qkv_full_grad.astype(jnp.bfloat16), "shard", scatter_dimension=0, tiled=True
        ).astype(jnp.float32),
        lax.psum_scatter(
            query_bias_grad.astype(jnp.bfloat16), "shard", scatter_dimension=0, tiled=True
        ).astype(jnp.float32),
        lax.psum_scatter(
            value_bias_grad.astype(jnp.bfloat16), "shard", scatter_dimension=0, tiled=True
        ).astype(jnp.float32),
        lax.psum_scatter(
            out_full_grad.astype(jnp.bfloat16), "shard", scatter_dimension=0, tiled=True
        ).astype(jnp.float32),
        lax.psum_scatter(
            out_shift_grad.astype(jnp.bfloat16), "shard", scatter_dimension=0, tiled=True
        ).astype(jnp.float32),
        lax.psum_scatter(
            gain_two_grad.astype(jnp.bfloat16), "shard", scatter_dimension=0, tiled=True
        ).astype(jnp.float32),
        lax.psum_scatter(
            shift_two_grad.astype(jnp.bfloat16), "shard", scatter_dimension=0, tiled=True
        ).astype(jnp.float32),
        lax.psum_scatter(
            router_grad.astype(jnp.bfloat16), "shard", scatter_dimension=0, tiled=True
        ).astype(jnp.float32),
    )
    (
        gain_one_part,
        shift_one_part,
        qkv_part,
        query_part,
        value_part,
        out_part,
        out_shift_part,
        gain_two_part,
        shift_two_part,
        router_part,
    ) = owned
    summed = (
        lax.psum(gain_one_part.astype(jnp.bfloat16), "replica").astype(jnp.float32),
        lax.psum(shift_one_part.astype(jnp.bfloat16), "replica").astype(jnp.float32),
        lax.psum(qkv_part.astype(jnp.bfloat16), "replica").astype(jnp.float32),
        lax.psum(query_part.astype(jnp.bfloat16), "replica").astype(jnp.float32),
        lax.psum(value_part.astype(jnp.bfloat16), "replica").astype(jnp.float32),
        lax.psum(out_part.astype(jnp.bfloat16), "replica").astype(jnp.float32),
        lax.psum(out_shift_part.astype(jnp.bfloat16), "replica").astype(jnp.float32),
        lax.psum(gain_two_part.astype(jnp.bfloat16), "replica").astype(jnp.float32),
        lax.psum(shift_two_part.astype(jnp.bfloat16), "replica").astype(jnp.float32),
        lax.psum(router_part.astype(jnp.bfloat16), "replica").astype(jnp.float32),
        lax.psum(expert_in_grad.astype(jnp.bfloat16), "replica").astype(jnp.float32),
        lax.psum(expert_in_bias_grad.astype(jnp.bfloat16), "replica").astype(jnp.float32),
        lax.psum(expert_out_grad.astype(jnp.bfloat16), "replica").astype(jnp.float32),
        lax.psum(expert_out_bias_grad.astype(jnp.bfloat16), "replica").astype(jnp.float32),
    )
    (
        gain_one_part,
        shift_one_part,
        qkv_part,
        query_part,
        value_part,
        out_part,
        out_shift_part,
        gain_two_part,
        shift_two_part,
        router_part,
        expert_in_grad,
        expert_in_bias_grad,
        expert_out_grad,
        expert_out_bias_grad,
    ) = summed
    return (
        output,
        input_grad,
        gain_one_part,
        shift_one_part,
        qkv_part,
        query_part,
        value_part,
        out_part,
        out_shift_part,
        gain_two_part,
        shift_two_part,
        router_part,
        expert_in_grad,
        expert_in_bias_grad,
        expert_out_grad,
        expert_out_bias_grad,
    )


def solution(mesh):
    return jax.shard_map(
        per_device,
        mesh=mesh,
        in_specs=(
            P(("replica", "shard"), None, None),
            P(("replica", "shard"), None, None),
            P(("replica", "shard"), None, None),
            P("shard"),
            P("shard"),
            P("shard", None),
            P("shard"),
            P("shard"),
            P("shard", None),
            P("shard"),
            P("shard"),
            P("shard"),
            P("shard", None),
            P("shard", None, None),
            P("shard", None),
            P("shard", None, None),
            P("shard", None),
        ),
        out_specs=(
            P(("replica", "shard"), None, None),
            P(("replica", "shard"), None, None),
            P("shard"),
            P("shard"),
            P("shard", None),
            P("shard"),
            P("shard"),
            P("shard", None),
            P("shard"),
            P("shard"),
            P("shard"),
            P("shard", None),
            P("shard", None, None),
            P("shard", None),
            P("shard", None, None),
            P("shard", None),
        ),
        check_vma=False,
    )
```

profile of v0, /device:TPU:0, one launch (start us, length us, event | category | flops | bytes accessed | tf_op | source)
XLA Modules:
  0.0 986.1 jit_solution(5788097186460516979)
XLA Ops:
  10.7 2.5 multiply_reduce_fusion.9
  18.0 40.0 %all-reduce.16 = (bf16[768]{0:T(1024)(128)(2,1)S(1)}, bf16[768]{0:T(1024)(128)(2,1)S(1)}, bf16[768]{0:T(1024)(128)(2,1)S(1)}, bf16[768]{0:T(1024)(128)(2,1)S(1)}...) all-reduce(bf16[768]{0:T(1024)(128)(2,1)S(1)} %dynamic-update-slice, ...), channel_id=1, replica_groups=mesh['replica'=4,'shard'=8] {'shard'}, use_global_device_ids=true, to_apply=%add.4 | all-reduce | flops 5376 | bytes 21504
  64.5 14.2 %all-gather.4.cloned.1.call-done = bf16[768,2304]{1,0:T(8,128)(2,1)} async-done(((bf16[96,2304]{1,0:T(8,128)(2,1)}), bf16[768,2304]{1,0:T(8,128)(2,1)}) %all-gather.4.cloned.1.call-update) | async-done | bytes 3538960 | tf_op jit(solution)/shard_map/all_gather | solution.py:65
  78.7 6.8 add_convert_fusion
  85.5 11.9 %reshape.380 = bf16[4,197,3,12,64]{4,3,2,1,0:T(8,128)(2,1)} reshape(bf16[788,2304]{1,0:T(8,128)(2,1)} %add_convert_fusion) | data formatting | bytes 7262208 | tf_op jit(solution)/shard_map/reshape | solution.py:98
  97.4 6.9 fusion.55
  104.2 3.9 copy.197
  108.2 4.5 copy.198
  112.7 5.5 copy.196
  123.5 3.0 fusion.38
  128.9 4.2 convert_element_type.295
  133.1 3.0 fusion.58
  142.6 12.4 %scatter_custom_fusion = bf16[2200,768]{1,0:T(8,128)(2,1)S(1)} fusion(s32[1576]{0:T(1024)S(1)} %fusion.49, bf16[1576,768]{1,0:T(8,128)(2,1)} %reshape.322, bf16[]{:T(256)} %constant.44.clone.1), kind=kCustom, calls=%fused_computation.69 | custom fusion | bytes 3379712 | tf_op jit(solution)/shard_map/scatter | solution.py:137
  155.0 2.8 reshape.285
  157.8 4.6 all-to-all-start
  162.5 94.6 %all-gather = bf16[8,96,8]{1,2,0:T(8,128)(2,1)S(1)} all-gather(bf16[1,96,8]{1,2,0:T(8,128)(2,1)S(1)} %bitcast.108), channel_id=1, replica_groups=mesh['replica'=4,'shard'=8] {'shard'}, dimensions={0}, use_global_device_ids=true | all-gather | bytes 13824 | tf_op jit(solution)/shard_map/all_gather | solution.py:72
  260.9 3.9 mul.270
  264.7 7.1 mul.278
  276.1 18.9 %scatter_custom_fusion.1 = bf16[2200,768]{1,0:T(8,128)(2,1)S(1)} fusion(s32[1576]{0:T(1024)S(1)} %fusion.49, f32[1576,768]{1,0:T(8,128)} %mul.278, f32[1576]{0:T(1024)S(1)} %mul.276, bf16[]{:T(256)} %constant.44.clone.1), kind=kCustom, calls=%fused_computation.57 | custom fusion | flops 2420736 | bytes 8228866 | tf_op jit(solution)/shard_map/scatter | solution.py:182
  295.0 2.8 reshape.289
  297.8 3.7 all-to-all-start.2
  301.5 4.7 reshape.286
  306.2 26.5 %multiply_convert_fusion = (bf16[2200,3072]{1,0:T(8,128)(2,1)}, f32[2200,3072]{1,0:T(8,128)}) fusion(f32[3072]{0:T(1024)S(1)} %bitcast.106, bf16[2200,768]{1,0:T(8,128)(2,1)} %reshape.286, bf16[1,768,3072]{2,1,0:T(8,128)(2,1)} %param.30), kind=kOutput, calls=%fused_computation.13 | convolution fusion | flops 10448486400 | bytes 48660480 | tf_op jit(solution)/shard_map/dot_general | solution.py:146
  332.7 16.4 %add_convert_fusion.1 = bf16[2200,768]{1,0:T(8,128)(2,1)} fusion(bf16[2200,3072]{1,0:T(8,128)(2,1)} %get-tuple-element.168, bf16[1,3072,768]{2,1,0:T(8,128)(2,1)} %param.32, f32[768]{0:T(1024)S(1)} %convert_reduce_fusion.1), kind=kOutput, calls=%fused_computation.23 | convolution fusion | flops 10384281600 | bytes 21617664 | tf_op jit(solution)/shard_map/dot_general | solution.py:151
  349.0 4.7 reshape.287
  353.7 20.4 %all-to-all-done.2 = bf16[8,275,768]{2,1,0:T(8,128)(2,1)S(1)} async-done(((bf16[8,275,768]{2,1,0:T(8,128)(2,1)}), bf16[8,275,768]{2,1,0:T(8,128)(2,1)S(1)}, u32[]{:S(2)}, u32[]{:S(2)}) %all-to-all-start.2) | async-done | bytes 3379232 | tf_op jit(solution)/shard_map/all_to_all | solution.py:184
  374.1 4.6 all-to-all-start.1
  378.8 2.9 reshape.290
  381.7 35.3 %fusion.60 = (bf16[3072]{0:T(1024)(128)(2,1)S(1)}, bf16[2200,3072]{1,0:T(8,128)(2,1)}) fusion(f32[2200,3072]{1,0:T(8,128)} %get-tuple-element.169, f32[3072]{0:T(1024)S(1)} %bitcast.107, bf16[2200,768]{1,0:T(8,128)(2,1)} %reshape.290, bf16[1,3072,768]{2,1,0:T(8,128)(2,1)} %param.32), kind=kOutput, calls=%fused_computation.130 | convolution fusion | flops 10529584128 | bytes 48666624 | tf_op jit(solution)/shard_map/rd,fd->rf/dot_general | solution.py:196
  417.0 15.5 %convolution_convert_fusion.3 = bf16[2200,768]{1,0:T(8,128)(2,1)S(1)} fusion(bf16[2200,3072]{1,0:T(8,128)(2,1)} %get-tuple-element.175, bf16[1,768,3072]{2,1,0:T(8,128)(2,1)} %param.30), kind=kOutput, calls=%fused_computation.28 | convolution fusion | flops 10382592000 | bytes 21614592 | tf_op jit(solution)/shard_map/rf,df->rd/dot_general | solution.py:205
  432.5 2.8 reshape.291
  435.2 19.8 %all-to-all-done.1 = bf16[8,275,768]{2,1,0:T(8,128)(2,1)} async-done(((bf16[8,275,768]{2,1,0:T(8,128)(2,1)}), bf16[8,275,768]{2,1,0:T(8,128)(2,1)}, u32[]{:S(2)}, u32[]{:S(2)}) %all-to-all-start.1) | async-done | bytes 3379232 | tf_op jit(solution)/shard_map/all_to_all | solution.py:154
  455.1 4.5 all-to-all-start.3
  462.4 3.0 reshape.288
  465.4 6.2 gather_fusion
  471.7 6.5 reshape.299
  478.2 13.7 %multiply_reduce_fusion.2 = (f32[788,2]{1,0:T(8,128)S(1)}, f32[788,768]{1,0:T(8,128)}) fusion(f32[788,2,768]{2,1,0:T(2,128)} %reshape.299, f32[788,768]{1,0:T(8,128)S(1)} %copy-done.3, f32[788,2]{1,0:T(8,128)S(1)} %copy-done.26), kind=kLoop, calls=%fused_computation.34 | loop fusion | flops 4234712 | bytes 9695552 | tf_op jit(solution)/shard_map/reduce_sum | solution.py:175
  492.2 43.8 %all-to-all-done.3 = bf16[8,275,768]{2,1,0:T(8,128)(2,1)} async-done(((bf16[8,275,768]{2,1,0:T(8,128)(2,1)}), bf16[8,275,768]{2,1,0:T(8,128)(2,1)}, u32[]{:S(2)}, u32[]{:S(2)}) %all-to-all-start.3) | async-done | bytes 3379232 | tf_op jit(solution)/shard_map/all_to_all | solution.py:208
  536.0 3.0 reshape.292
  539.0 6.2 gather_fusion.1
  545.2 6.8 reshape.301
  552.1 9.7 reduce_sum.258
  561.8 5.8 multiply_reduce_fusion.4
  572.8 2.9 convolution_convert_fusion.4
  575.7 3.5 reshape.381
  579.3 4.0 copy.176
  583.3 7.5 multiply_reduce_fusion
  590.8 11.9 %multiply_convert_fusion.1 = bf16[4,12,197,197]{2,3,1,0:T(8,128)(2,1)} fusion(f32[4,12,197,197]{2,3,1,0:T(8,128)} %get-tuple-element.172, f32[4,12,197,197]{2,3,1,0:T(8,128)} %copy-done, f32[4,12,197]{2,1,0:T(8,128)S(1)} %get-tuple-element.171, f32[4,12,197]{2,1,0:T(8,128)S(1)} %log_add_fusion), kind=kLoop, calls=%fused_computation.14 | loop fusion | flops 9314160 | bytes 18703968 | tf_op jit(solution)/shard_map/convert_element_type | solution.py:258
  602.7 3.6 multiply_bitcast_fusion.1
  608.8 5.8 fusion.23
  616.0 6.7 copy.181
  622.7 9.7 convert_element_type.318
  632.4 7.5 convolution_convert_fusion.2
  640.0 16.5 %fusion.20 = bf16[1,3072,768]{2,1,0:T(8,128)(2,1)} fusion(bf16[2200,3072]{1,0:T(8,128)(2,1)} %get-tuple-element.168, bf16[2200,768]{1,0:T(8,128)(2,1)} %reshape.290), kind=kOutput, calls=%fused_computation.42 | convolution fusion | flops 10383261696 | bytes 21614592 | tf_op jit(solution)/shard_map/rf,rd->fd/dot_general | solution.py:192
  658.0 17.3 %fusion.19 = bf16[1,768,3072]{2,1,0:T(8,128)(2,1)} fusion(bf16[2200,768]{1,0:T(8,128)(2,1)} %reshape.286, bf16[2200,3072]{1,0:T(8,128)(2,1)} %get-tuple-element.175), kind=kOutput, calls=%fused_computation.41 | convolution fusion | flops 10383261696 | bytes 21614592 | tf_op jit(solution)/shard_map/rd,rf->df/dot_general | solution.py:201
  675.3 42.9 %reduce-scatter.6.cloned.1.call-done = bf16[96,2304]{1,0:T(8,128)(2,1)} async-done(((bf16[768,2304]{1,0:T(8,128)(2,1)}), bf16[96,2304]{1,0:T(8,128)(2,1)}) %reduce-scatter.6.cloned.1.call-update) | async-done | bytes 442384 | tf_op jit(solution)/shard_map/reduce_scatter | solution.py:292
  720.9 9.6 multiply_reduce_fusion.5
  730.5 36.0 %all-reduce.15 = (bf16[768]{0:T(1024)(128)(2,1)S(1)}, bf16[768]{0:T(1024)(128)(2,1)S(1)}, bf16[768]{0:T(1024)(128)(2,1)S(1)}, bf16[768]{0:T(1024)(128)(2,1)S(1)}...) all-reduce(bf16[768]{0:T(1024)(128)(2,1)S(1)} %get-tuple-element.11, ...), channel_id=2, replica_groups=mesh['replica'=4,'shard'=8] {'shard'}, use_global_device_ids=true, to_apply=%region_25.26.clone | all-reduce | flops 5376 | bytes 21504
  767.0 3.7 add_convert_fusion.2
  775.7 6.8 reduce-scatter.10.cloned.1.call-done
  783.3 10.8 %all-reduce.17 = (bf16[96]{0:T(256)(128)(2,1)S(1)}, bf16[96]{0:T(256)(128)(2,1)S(1)}, bf16[96]{0:T(256)(128)(2,1)S(1)}, bf16[96]{0:T(256)(128)(2,1)S(1)}, bf16[9...) all-reduce(bf16[96]{0:T(256)(128)(2,1)S(1)} %dynamic-slice.8, ...), channel_id=1, replica_groups=mesh['replica'=4,'shard'=8] {'replica'}, use_global_device_ids=true, to_apply=%region_26.27 | all-reduce | flops 5280 | bytes 21120 | tf_op jit(solution)/shard_map/psum | solution.py:330
  799.4 165.9 %all-reduce.21.cloned.1.call-done = (bf16[96,2304]{1,0:T(8,128)(2,1)}, bf16[96,768]{1,0:T(8,128)(2,1)}, bf16[1,768,3072]{2,1,0:T(8,128)(2,1)}, bf16[1,3072,768]{2,1,0:T(8,128)(2,1)}) async-done(((bf16[96,2304]{1,0:T(8,128)(2,1)}, bf16[96,768]{1,0:T(8,128)(2,1)}, bf16[1,768,3072]{2,1,0:T(8,128)(2,1)}, bf16[1,3072,768]{2,1,0:T(8,128)(2,1)}), (bf16[96,2304]{1,0:T(8,128)(2,1)}, bf16[96,768]{1,0:T(8,128)(2,1)}, ...) | async-done | bytes 10027024 | tf_op jit(solution)/shard_map/psum | solution.py:332
  965.3 7.5 convert_element_type.344
  972.9 4.5 convert_element_type.349
  (295 shorter events, 65.0 us)
Async XLA Ops:
  7.2 6.0 copy-start.11
  7.2 71.5 %all-gather.4.cloned.1.call-start = ((), (), s32[]{:S(2)}) async-start(), calls=%async_computation.7 | async-start | bytes 3981312 | tf_op jit(solution)/shard_map/all_gather | solution.py:65
  7.9 125.2 %all-gather.6.cloned.1.call-start = ((), (), s32[]{:S(2)}) async-start(), calls=%async_computation.8 | async-start | bytes 1327104 | tf_op jit(solution)/shard_map/all_gather | solution.py:68
  8.7 6.1 copy-start.48
  10.5 4.5 copy-start.72
  10.5 5.8 copy-start.74
  10.6 6.0 copy-start.75
  10.6 6.2 copy-start.76
  10.6 6.5 copy-start.77
  10.6 6.7 copy-start.78
  10.6 6.9 copy-start.79
  10.6 7.1 copy-start.80
  10.6 47.6 %copy-start.27 = (f32[4,197]{0,1:T(8,128)}, f32[4,197]{0,1:T(8,128)S(1)}, u32[]{:S(2)}) copy-start(f32[4,197]{0,1:T(8,128)S(1)} %broadcast_multiply_fusion) | copy-start | bytes 9460
  58.0 20.7 %copy-start.57 = (f32[768]{0:T(1024)}, f32[768]{0:T(1024)S(1)}, u32[]{:S(2)}) copy-start(f32[768]{0:T(1024)S(1)} %convert_element_type.286) | copy-start | bytes 9220
  58.0 20.6 %copy-start.67 = (f32[768]{0:T(1024)}, f32[768]{0:T(1024)S(1)}, u32[]{:S(2)}) copy-start(f32[768]{0:T(1024)S(1)} %convert_element_type.287) | copy-start | bytes 9220
  58.7 20.0 %copy-start.63 = (f32[788]{0:T(1024)}, f32[788]{0:T(1024)S(1)}, u32[]{:S(2)}) copy-start(f32[788]{0:T(1024)S(1)} %rsqrt.21) | copy-start | bytes 9460
  58.8 19.9 %copy-start.65 = (f32[788]{0:T(1024)}, f32[788]{0:T(1024)S(1)}, u32[]{:S(2)}) copy-start(f32[788]{0:T(1024)S(1)} %div.43) | copy-start | bytes 9460
  60.8 24.7 %copy-start.19 = (f32[788,768]{1,0:T(8,128)}, f32[788,768]{1,0:T(8,128)S(1)}, u32[]{:S(2)}) copy-start(f32[788,768]{1,0:T(8,128)S(1)} %reshape.295) | copy-start | bytes 7262212
  60.8 75.8 %copy-start.49 = (f32[768]{0:T(1024)}, f32[768]{0:T(1024)S(1)}, u32[]{:S(2)}) copy-start(f32[768]{0:T(1024)S(1)} %convert_element_type.297) | copy-start | bytes 9220
  64.5 211.6 %copy-start.61 = (s32[1576]{0:T(1024)}, s32[1576]{0:T(1024)S(1)}, u32[]{:S(2)}) copy-start(s32[1576]{0:T(1024)S(1)} %fusion.49) | copy-start | bytes 18916
  108.1 10.0 %copy-start.13 = (bf16[4,197,1,12,64]{1,4,3,0,2:T(8,128)(2,1)}, bf16[4,197,1,12,64]{1,4,3,0,2:T(8,128)(2,1)S(1)}, u32[]{:S(2)}) copy-start(bf16[4,197,1,12,64]{1,4,3,0,2:T(8,128)(2,1)S(1)} %copy.197) | copy-start | bytes 3631108
  112.6 7.0 copy-start.15
  126.5 6.6 copy-start.20
  157.8 4.6 copy-start.71
  157.8 99.4 %copy-start.31 = (bf16[4,197,768]{2,0,1:T(4,128)(2,1)S(1)}, bf16[4,197,768]{2,0,1:T(4,128)(2,1)}, u32[]{:S(2)}) copy-start(bf16[4,197,768]{2,0,1:T(4,128)(2,1)} %param.19) | copy-start | bytes 3631108
  157.8 140.0 %all-to-all-start = ((bf16[8,275,768]{2,1,0:T(8,128)(2,1)}), bf16[8,275,768]{2,1,0:T(8,128)(2,1)}, u32[]{:S(2)}, u32[]{:S(2)}) async-start(bf16[8,275,768]{2,1,0:T(8,128)(2,1)} %reshape.285), calls=%async_computation | async-start | bytes 6881280 | tf_op jit(solution)/shard_map/all_to_all | solution.py:138
  257.1 14.7 %copy-start.44 = (bf16[768,8]{0,1:T(8,128)(2,1)}, bf16[768,8]{0,1:T(8,128)(2,1)S(1)}, u32[]{:S(2)}) copy-start(bf16[768,8]{0,1:T(8,128)(2,1)S(1)} %reshape.356) | copy-start | bytes 36868
  257.2 16.5 %copy-start.55 = (s32[788,2]{0,1:T(2,128)}, s32[788,2]{0,1:T(2,128)S(1)}, u32[]{:S(2)}) copy-start(s32[788,2]{0,1:T(2,128)S(1)} %eq.37) | copy-start | bytes 18916
  264.7 7.1 copy-start.69
  264.7 7.1 copy-start.70
  297.8 76.3 %all-to-all-start.2 = ((bf16[8,275,768]{2,1,0:T(8,128)(2,1)}), bf16[8,275,768]{2,1,0:T(8,128)(2,1)S(1)}, u32[]{:S(2)}, u32[]{:S(2)}) async-start(bf16[8,275,768]{2,1,0:T(8,128)(2,1)} %reshape.289), calls=%async_computation.2 | async-start | bytes 6881280 | tf_op jit(solution)/shard_map/all_to_all | solution.py:184
  374.1 4.7 copy-start.7
  374.1 80.9 %all-to-all-start.1 = ((bf16[8,275,768]{2,1,0:T(8,128)(2,1)}), bf16[8,275,768]{2,1,0:T(8,128)(2,1)}, u32[]{:S(2)}, u32[]{:S(2)}) async-start(bf16[8,275,768]{2,1,0:T(8,128)(2,1)} %reshape.287), calls=%async_computation.1 | async-start | bytes 6881280 | tf_op jit(solution)/shard_map/all_to_all | solution.py:154
  435.2 24.4 %copy-start.12 = (bf16[4,197,768]{2,0,1:T(4,128)(2,1)S(1)}, bf16[4,197,768]{2,0,1:T(4,128)(2,1)}, u32[]{:S(2)}) copy-start(bf16[4,197,768]{2,0,1:T(4,128)(2,1)} %param.17) | copy-start | bytes 3631108
  435.2 24.4 %copy-start.28 = (f32[4,197]{0,1:T(8,128)S(1)}, f32[4,197]{0,1:T(8,128)}, u32[]{:S(2)}) copy-start(f32[4,197]{0,1:T(8,128)} %copy-done.27) | copy-start | bytes 9460
  435.2 24.4 %copy-start.33 = (f32[4,197]{0,1:T(8,128)S(1)}, f32[4,197]{0,1:T(8,128)}, u32[]{:S(2)}) copy-start(f32[4,197]{0,1:T(8,128)} %copy-done.32) | copy-start | bytes 9460
  435.2 24.4 %copy-start.58 = (f32[768]{0:T(1024)S(1)}, f32[768]{0:T(1024)}, u32[]{:S(2)}) copy-start(f32[768]{0:T(1024)} %copy-done.57) | copy-start | bytes 9220
  435.2 24.4 %copy-start.68 = (f32[768]{0:T(1024)S(1)}, f32[768]{0:T(1024)}, u32[]{:S(2)}) copy-start(f32[768]{0:T(1024)} %copy-done.67) | copy-start | bytes 9220
  455.1 81.0 %all-to-all-start.3 = ((bf16[8,275,768]{2,1,0:T(8,128)(2,1)}), bf16[8,275,768]{2,1,0:T(8,128)(2,1)}, u32[]{:S(2)}, u32[]{:S(2)}) async-start(bf16[8,275,768]{2,1,0:T(8,128)(2,1)} %reshape.291), calls=%async_computation.3 | async-start | bytes 6881280 | tf_op jit(solution)/shard_map/all_to_all | solution.py:208
  459.6 215.7 %reduce-scatter.8.cloned.1.call-start = ((), (), s32[]{:S(2)}) async-start(), calls=%async_computation.10 | async-start | bytes 1327104 | tf_op jit(solution)/shard_map/reduce_scatter | solution.py:301
  471.7 6.5 copy-start.3
  471.7 6.5 copy-start.26
  478.2 13.9 %copy-start.56 = (s32[788,2]{0,1:T(2,128)S(1)}, s32[788,2]{0,1:T(2,128)}, u32[]{:S(2)}) copy-start(s32[788,2]{0,1:T(2,128)} %copy-done.55) | copy-start | bytes 18916
  478.2 13.9 %copy-start.39 = (f32[788,8]{0,1:T(8,128)S(1)}, f32[788,8]{0,1:T(8,128)}, u32[]{:S(2)}) copy-start(f32[788,8]{0,1:T(8,128)} %copy-done.38) | copy-start | bytes 75652
  478.2 13.9 %copy-start.54 = (f32[788]{0:T(1024)S(1)}, f32[788]{0:T(1024)}, u32[]{:S(2)}) copy-start(f32[788]{0:T(1024)} %copy-done.53) | copy-start | bytes 9460
  478.2 13.9 %copy-start.60 = (f32[788]{0:T(1024)S(1)}, f32[788]{0:T(1024)}, u32[]{:S(2)}) copy-start(f32[788]{0:T(1024)} %copy-done.59) | copy-start | bytes 9460
  552.0 9.8 copy-start.6
  552.1 9.7 copy-start.37
  552.1 9.7 copy-start.45
  552.1 9.7 copy-start.47
  552.1 9.7 copy-start.50
  552.1 9.7 copy-start.52
  561.8 5.8 copy-start.4
  572.6 145.6 %reduce-scatter.6.cloned.1.call-start = ((), (), s32[]{:S(2)}) async-start(), calls=%async_computation.9 | async-start | bytes 3981312 | tf_op jit(solution)/shard_map/reduce_scatter | solution.py:292
  590.8 11.9 %copy-start.16 = (bf16[4,197,1,12,64]{1,4,3,0,2:T(8,128)(2,1)S(1)}, bf16[4,197,1,12,64]{1,4,3,0,2:T(8,128)(2,1)}, u32[]{:S(2)}) copy-start(bf16[4,197,1,12,64]{1,4,3,0,2:T(8,128)(2,1)} %copy-done.15) | copy-start | bytes 3631108
  602.7 4.4 copy-start.14
  622.7 9.7 copy-start.30
  639.9 16.6 %copy-start.10 = (bf16[788,768]{1,0:T(8,128)(2,1)S(1)}, bf16[788,768]{1,0:T(8,128)(2,1)}, u32[]{:S(2)}) copy-start(bf16[788,768]{1,0:T(8,128)(2,1)} %copy-done.9) | copy-start | bytes 3631108
  639.9 142.6 %reduce-scatter.10.cloned.1.call-start = ((), (), s32[]{:S(2)}) async-start(), calls=%async_computation.11 | async-start | bytes 221184
  657.9 307.4 %all-reduce.21.cloned.1.call-start = ((), (), s32[]{:S(2)}) async-start(), calls=%async_computation.12 | async-start | bytes 20054016 | tf_op jit(solution)/shard_map/psum | solution.py:332
  720.9 46.1 %copy-start.18 = (f32[788,768]{1,0:T(8,128)S(1)}, f32[788,768]{1,0:T(8,128)}, u32[]{:S(2)}) copy-start(f32[788,768]{1,0:T(8,128)} %copy-done.17) | copy-start | bytes 7262212
  965.3 7.5 copy-start.24
  972.9 4.5 copy-start.40
  972.9 5.5 copy-start.43
  (27 other events, 62.6 us)
Sparse Core Ops, SparseCore 0:
  10.2 68.4 all-gather.3
  80.9 39.6 all-gather.5
  572.7 62.9 reduce-scatter.7
  640.0 78.1 reduce-scatter.5
  721.9 60.6 reduce-scatter.9
  785.7 179.5 all-reduce.20
where the time goes:
time: 992 us; the launch traced here: 986 us
  waiting for transfers between devices  315 us (32%)
  matrix products  191 us (19%)
  blocking collectives  181 us (18%)
  local copies, waits for them, and re-layouts  173 us (17%)
  other arithmetic  91.4 us (9%)
  starting transfers between devices  17.8 us (2%)
  between operations  17 us (2%)
    psum x1, waiting for transfers between devices, per_device(): lax.psum(qkv_part.astype(jnp.bfloat16), 'replica').astype(jnp.float32)  166 us
    all_gather x1, blocking collectives, per_device(): lax.all_gather(router_weight, 'shard', axis=0, tiled=True)  94.6 us
    unnamed x2, blocking collectives  76.1 us
    all_to_all x1, waiting for transfers between devices, per_device(): lax.all_to_all(arrived_grad.reshape(experts, capacity, model_width), 'sha...  43.8 us
    reduce_scatter x1, waiting for transfers between devices, per_device(): lax.psum_scatter(qkv_full_grad.astype(jnp.bfloat16), 'shard', scatter_dim...  42.9 us
    dot_general x1, matrix products, per_device(): jnp.einsum('rd,fd->rf', outer_grad, expert_out[0], preferred_element_type...  35.3 us
    unnamed x197, local copies, waits for them, and re-layouts  31.3 us
    dot_general x1, matrix products, per_device(): jnp.dot(arrived, expert_in[0], preferred_element_type=jnp.float32)  26.5 us
  transfers between devices with their start and end apart: 10, of which 7 were waited for; matrix products, arithmetic and copies ran while one was open for 38% of the time, Pallas kernels for 0%

commit v1 on v0

v1 whole, which is shorter than its diff:
```python
import jax
import jax.numpy as jnp
from jax import lax
from jax.sharding import PartitionSpec as P

HEADS = 12
HEAD_DIM = 64
LANES = 128


eps_norm = 1e-06
f32 = jnp.float32
bf16 = jnp.bfloat16


def normalize(values):
    average = jnp.mean(values, -1, keepdims=True)
    centred = values - average
    variance = jnp.mean(centred * centred, -1, keepdims=True)
    inverse = lax.rsqrt(variance + eps_norm)
    return (centred * inverse, inverse)


def norm_back(grad_out, scaled, inverse, gain_vec):
    gain_grad = jnp.sum(grad_out * scaled, 0)
    shift_grad = jnp.sum(grad_out, 0)
    grad_scaled = grad_out * gain_vec
    first_term = jnp.mean(grad_scaled, -1, keepdims=True)
    second_term = jnp.mean(grad_scaled * scaled, -1, keepdims=True)
    return (inverse * (grad_scaled - first_term - scaled * second_term), gain_grad, shift_grad)


def slot_index(route_ids, experts, stride):
    flat_ids = route_ids.reshape(-1)
    onehot = (flat_ids[:, None] == jnp.arange(experts, dtype=jnp.int32)[None, :]).astype(jnp.int32)
    ranking = jnp.sum((jnp.cumsum(onehot, 0) - 1) * onehot, 1)
    return (flat_ids * stride + ranking).reshape(route_ids.shape)


def exchange(rows, experts):
    width = rows.shape[-1]
    blocks = rows.reshape(experts, rows.shape[0] // experts, width)
    moved = lax.all_to_all(blocks, "shard", split_axis=0, concat_axis=0, tiled=True)
    return moved.reshape(rows.shape)


def replica_sum(value):
    count = lax.axis_size("replica")
    me = lax.axis_index("replica")
    core = me % 2
    half = value.shape[0] // 2
    mine = lax.dynamic_slice_in_dim(value, core * half, half, 0)
    other = lax.dynamic_slice_in_dim(value, (1 - core) * half, half, 0)
    mine = mine.astype(f32) + lax.ppermute(
        other, "replica", [(i, i ^ 1) for i in range(count)]
    ).astype(f32)
    mine = mine.astype(bf16)
    step = 2
    while step < count:
        theirs = lax.ppermute(mine, "replica", [(i, i ^ step) for i in range(count)])
        mine = (mine.astype(f32) + theirs.astype(f32)).astype(bf16)
        step *= 2
    theirs = lax.ppermute(mine, "replica", [(i, i ^ 1) for i in range(count)])
    first = jnp.where(core == 0, mine, theirs).astype(f32)
    second = jnp.where(core == 0, theirs, mine).astype(f32)
    return jnp.concatenate([first, second], 0)


def per_device(
    images,
    routes,
    cotangent,
    ln1_gain,
    ln1_bias,
    qkv_weight,
    q_bias,
    v_bias,
    out_weight,
    out_bias,
    ln2_gain,
    ln2_bias,
    router_weight,
    expert_in,
    expert_in_bias,
    expert_out,
    expert_out_bias,
):
    experts = lax.axis_size("shard")
    expert_here = lax.axis_index("shard")
    images_here, seq_len, model_width = images.shape
    tokens_here = images_here * seq_len
    capacity = 14 * tokens_here // (5 * experts)
    stride = -(-capacity // 8) * 8
    slots = experts * stride
    factor = HEAD_DIM ** (-0.5)

    columns = [ln1_gain, ln1_bias, q_bias, v_bias, out_bias, ln2_gain, ln2_bias]
    small = jnp.concatenate([router_weight, jnp.stack(columns, 1)], 1)
    width_small = -(-small.shape[1] // LANES) * LANES
    small = jnp.pad(small, ((0, 0), (0, width_small - small.shape[1])))
    packed = lax.all_gather(
        jnp.concatenate([qkv_weight, out_weight, small], 1), "shard", axis=0, tiled=True
    )
    qkv_full = packed[:, : 3 * model_width]
    out_full = packed[:, 3 * model_width : 4 * model_width]
    small_full = packed[:, 4 * model_width :]
    router_full = small_full[:, :experts]
    vectors = small_full[:, experts : experts + len(columns)].T.astype(f32)
    gain_one, shift_one, query_bias, value_bias, out_shift, gain_two, shift_two = vectors

    route_rows = routes.reshape(tokens_here, 2)
    slot_ids = slot_index(route_rows, experts, stride)
    slot_row = jnp.arange(slots, dtype=jnp.int32)
    send = (
        (slot_row[:, None] == slot_ids[None, :, 0]) | (slot_row[:, None] == slot_ids[None, :, 1])
    ).astype(bf16)
    collect = (
        (slot_ids[:, 0, None] == slot_row[None, :]) | (slot_ids[:, 1, None] == slot_row[None, :])
    ).astype(bf16)

    cot_rows = cotangent.reshape(tokens_here, model_width)
    cot_sent = jnp.dot(send, cot_rows, preferred_element_type=f32).astype(bf16)
    cot_there = exchange(cot_sent, experts)

    row_values = images.reshape(tokens_here, model_width).astype(f32)
    scaled_one, inverse_one = normalize(row_values)
    normed = (scaled_one * gain_one + shift_one).astype(bf16)
    qkv_shift = jnp.concatenate([query_bias, jnp.zeros((model_width,), f32), value_bias])
    projected = (jnp.dot(normed, qkv_full, preferred_element_type=f32) + qkv_shift).astype(bf16)
    heads_view = projected.reshape(images_here, seq_len, 3, HEADS, HEAD_DIM)
    queries = heads_view[:, :, 0]
    keys_all = heads_view[:, :, 1]
    values_all = heads_view[:, :, 2]
    scores = (
        jnp.einsum("ishd,ithd->ihst", queries, keys_all, preferred_element_type=f32) * factor
    )
    row_max = jnp.max(scores, -1, keepdims=True)
    exp_scores = jnp.exp(scores - row_max)
    row_total = jnp.sum(exp_scores, -1, keepdims=True)
    attn_probs = exp_scores / row_total
    log_total = row_max + jnp.log(row_total)
    attended = jnp.einsum(
        "ihst,ithd->ishd", attn_probs.astype(bf16), values_all, preferred_element_type=f32
    )
    attended = attended.reshape(tokens_here, model_width).astype(bf16)
    middle = row_values + jnp.dot(attended, out_full, preferred_element_type=f32) + out_shift
    scaled_two, inverse_two = normalize(middle)
    normed_two = (scaled_two * gain_two + shift_two).astype(bf16)

    sent = jnp.dot(send, normed_two, preferred_element_type=f32).astype(bf16)
    arrived = exchange(sent, experts)

    probs = jax.nn.softmax(jnp.dot(arrived, router_full, preferred_element_type=f32), axis=-1)
    is_here = (jnp.arange(experts, dtype=jnp.int32) == expert_here).astype(f32)[None, :]
    gate = jnp.sum(probs * is_here, -1, keepdims=True)
    weight_in = expert_in[0]
    weight_out = expert_out[0]
    inner_act = jnp.dot(arrived, weight_in, preferred_element_type=f32) + expert_in_bias[0].astype(
        f32
    )
    hidden = jax.nn.gelu(inner_act).astype(bf16)
    outer_act = jnp.dot(hidden, weight_out, preferred_element_type=f32) + expert_out_bias[0].astype(
        f32
    )
    gated = (gate * outer_act).astype(bf16)
    cot_wide = cot_there.astype(f32)
    gate_grad = jnp.sum(cot_wide * outer_act, -1, keepdims=True)
    outer_grad = (gate * cot_wide).astype(bf16)
    logit_grads = gate_grad * gate * (is_here - probs)
    hidden_grad = jnp.einsum("rd,fd->rf", outer_grad, weight_out, preferred_element_type=f32)
    gelu_pull = jax.vjp(jax.nn.gelu, inner_act)[1]
    inner_grad = gelu_pull(hidden_grad)[0].astype(bf16)
    arrived_grad = (
        jnp.einsum("rf,df->rd", inner_grad, weight_in, preferred_element_type=f32)
        + jnp.einsum("re,de->rd", logit_grads, router_full.astype(f32))
    ).astype(bf16)
    back = exchange(arrived_grad, experts)
    returned = exchange(gated, experts)

    expert_out_part = jnp.einsum("rf,rd->fd", hidden, outer_grad, preferred_element_type=f32)
    expert_out_grad = replica_sum(expert_out_part.astype(bf16))[None]
    expert_in_part = jnp.einsum("rd,rf->df", arrived, inner_grad, preferred_element_type=f32)
    expert_in_grad = replica_sum(expert_in_part.astype(bf16))[None]
    expert_out_bias_part = jnp.sum(outer_grad.astype(f32), 0)
    expert_in_bias_part = jnp.sum(inner_grad.astype(f32), 0)
    router_grad = jnp.einsum("rd,re->de", arrived.astype(f32), logit_grads)

    grad_out = cot_rows.astype(f32)
    normed_two_grad = jnp.dot(collect, back, preferred_element_type=f32)
    middle_norm_grad, gain_two_grad, shift_two_grad = norm_back(
        normed_two_grad, scaled_two, inverse_two, gain_two
    )
    middle_grad = grad_out + middle_norm_grad
    branch_grad = middle_grad.astype(bf16)
    out_shift_grad = jnp.sum(branch_grad.astype(f32), 0)
    out_full_grad = jnp.einsum("td,te->de", attended, branch_grad, preferred_element_type=f32)
    attended_grad = jnp.einsum(
        "te,de->td", branch_grad, out_full, preferred_element_type=f32
    ).astype(bf16)
    grad_heads = attended_grad.reshape(images_here, seq_len, HEADS, HEAD_DIM)
    scores_back = (
        jnp.einsum("ishd,ithd->ihst", queries, keys_all, preferred_element_type=f32) * factor
    )
    probs_back = jnp.exp(scores_back - log_total)
    values_grad = jnp.einsum(
        "ihst,ishd->ithd", probs_back.astype(bf16), grad_heads, preferred_element_type=f32
    )
    prob_back_grad = jnp.einsum(
        "ishd,ithd->ihst", grad_heads, values_all, preferred_element_type=f32
    )
    score_grad = (
        probs_back * (prob_back_grad - jnp.sum(probs_back * prob_back_grad, -1, keepdims=True))
    ).astype(bf16)
    query_grad = (
        jnp.einsum("ihst,ithd->ishd", score_grad, keys_all, preferred_element_type=f32) * factor
    )
    key_grad = (
        jnp.einsum("ihst,ishd->ithd", score_grad, queries, preferred_element_type=f32) * factor
    )
    projected_grad = (
        jnp.stack([query_grad, key_grad, values_grad], 2)
        .reshape(tokens_here, 3 * model_width)
        .astype(bf16)
    )
    qkv_full_grad = jnp.einsum("td,te->de", normed, projected_grad, preferred_element_type=f32)
    projected_sums = jnp.sum(projected_grad.astype(f32), 0)
    query_bias_grad = projected_sums[:model_width]
    value_bias_grad = projected_sums[2 * model_width :]
    normed_grad = jnp.einsum("te,de->td", projected_grad, qkv_full, preferred_element_type=f32)
    rows_norm_grad, gain_one_grad, shift_one_grad = norm_back(
        normed_grad, scaled_one, inverse_one, gain_one
    )
    output = (
        (middle + jnp.dot(collect, returned, preferred_element_type=f32))
        .reshape(images.shape)
        .astype(bf16)
    )
    input_grad = (middle_grad + rows_norm_grad).astype(bf16).reshape(images.shape)

    vector_grads = [
        gain_one_grad,
        shift_one_grad,
        query_bias_grad,
        value_bias_grad,
        out_shift_grad,
        gain_two_grad,
        shift_two_grad,
    ]
    small_grad = jnp.concatenate([router_grad.T, jnp.stack(vector_grads, 0)], 0)
    small_grad = jnp.pad(small_grad, ((0, width_small - small_grad.shape[0]), (0, 0)))
    packed_grad = jnp.concatenate(
        [qkv_full_grad.astype(bf16), out_full_grad.astype(bf16), small_grad.T.astype(bf16)], 1
    )
    owned = lax.psum_scatter(packed_grad, "shard", scatter_dimension=0, tiled=True)
    bias_parts = jnp.concatenate([expert_in_bias_part, expert_out_bias_part]).astype(bf16)
    width_all = owned.shape[1]
    bias_rows = -(-bias_parts.shape[0] // width_all)
    bias_parts = jnp.pad(bias_parts, (0, bias_rows * width_all - bias_parts.shape[0]))
    owned = jnp.concatenate([owned, bias_parts.reshape(bias_rows, width_all)], 0)
    summed = lax.psum(owned, "replica").astype(f32)
    rows = qkv_weight.shape[0]
    biases = summed[rows:].reshape(-1)
    hidden_width = expert_in_bias.shape[1]
    summed = summed[:rows]
    small_sum = summed[:, 4 * model_width :]
    vector_sums = small_sum[:, experts : experts + len(columns)].T
    return (
        output,
        input_grad,
        vector_sums[0],
        vector_sums[1],
        summed[:, : 3 * model_width],
        vector_sums[2],
        vector_sums[3],
        summed[:, 3 * model_width : 4 * model_width],
        vector_sums[4],
        vector_sums[5],
        vector_sums[6],
        small_sum[:, :experts],
        expert_in_grad,
        biases[None, :hidden_width],
        expert_out_grad,
        biases[None, hidden_width : hidden_width + model_width],
    )


def solution(mesh):
    return jax.shard_map(
        per_device,
        mesh=mesh,
        in_specs=(
            P(("replica", "shard"), None, None),
            P(("replica", "shard"), None, None),
            P(("replica", "shard"), None, None),
            P("shard"),
            P("shard"),
            P("shard", None),
            P("shard"),
            P("shard"),
            P("shard", None),
            P("shard"),
            P("shard"),
            P("shard"),
            P("shard", None),
            P("shard", None, None),
            P("shard", None),
            P("shard", None, None),
            P("shard", None),
        ),
        out_specs=(
            P(("replica", "shard"), None, None),
            P(("replica", "shard"), None, None),
            P("shard"),
            P("shard"),
            P("shard", None),
            P("shard"),
            P("shard"),
            P("shard", None),
            P("shard"),
            P("shard"),
            P("shard"),
            P("shard", None),
            P("shard", None, None),
            P("shard", None),
            P("shard", None, None),
            P("shard", None),
        ),
        check_vma=False,
    )
```

time: 992 us -> 789 us (0.80)
  blocking collectives: 181 us -> 0 us
  local copies, waits for them, and re-layouts: 173 us -> 110 us
  waiting for transfers between devices: 315 us -> 349 us
  matrix products: 191 us -> 212 us
  other arithmetic: 91.4 us -> 77.6 us
    psum x1, waiting for transfers between devices: 166 us -> 27.9 us  [per_device(): summed = lax.psum(owned, 'replica').astype(f32)]
    all_gather x1 -> x0, blocking collectives: 94.6 us -> none  [per_device(): lax.all_gather(router_weight, 'shard', axis=0, tiled=True)]
    ppermute x0 -> x6, waiting for transfers between devices: none -> 91.4 us  [the longest x2 91.3 us: replica_sum(): lax.ppermute(mine, 'replica', [(i, i ^ step) for i in range(count)])]
    unnamed x2 -> x0, blocking collectives: 76.1 us -> none
    all_gather x2 -> x1, waiting for transfers between devices: 14.2 us -> 73.4 us  [per_device(): lax.all_gather(jnp.concatenate([qkv_weight, out_weight, small], 1), 'shar...]
    all_to_all x4, waiting for transfers between devices: 84 us -> 141 us  [exchange(): lax.all_to_all(blocks, 'shard', split_axis=0, concat_axis=0, tiled=True)]
    reduce_scatter x2 -> x1, waiting for transfers between devices: 42.9 us -> 15.7 us  [per_device(): lax.psum_scatter(packed_grad, 'shard', scatter_dimension=0, tiled=True)]
    reshape x10 -> x4, local copies, waits for them, and re-layouts: 30.6 us -> 5.51 us  [the longest x1 2.81 us: per_device(): (middle_grad + rows_norm_grad).astype(bf16).reshape(images.shape)]
  transfers between devices with their start and end apart: 10 -> 13, of which waited for: 7 -> 8; matrix products, arithmetic and copies ran while one was open for 38% -> 30% of each run, Pallas kernels for 0% -> 0%
where the time goes in v1:
time: 789 us; the launch traced here: 784 us
  waiting for transfers between devices  349 us (44%)
  matrix products  212 us (27%)
  local copies, waits for them, and re-layouts  110 us (14%)
  other arithmetic  77.6 us (10%)
  starting transfers between devices  19.9 us (3%)
  between operations  15 us (2%)
    all_to_all x4, waiting for transfers between devices, exchange(): lax.all_to_all(blocks, 'shard', split_axis=0, concat_axis=0, tiled=True)  141 us
    ppermute x2, waiting for transfers between devices, replica_sum(): lax.ppermute(mine, 'replica', [(i, i ^ step) for i in range(count)])  91.3 us
    all_gather x1, waiting for transfers between devices, per_device(): lax.all_gather(jnp.concatenate([qkv_weight, out_weight, small], 1), 'shar...  73.4 us
    dot_general x1, matrix products, per_device(): jnp.einsum('rd,fd->rf', outer_grad, weight_out, preferred_element_type=f32)  32.9 us
    unnamed x122, local copies, waits for them, and re-layouts  28.5 us
    psum x1, waiting for transfers between devices, per_device(): summed = lax.psum(owned, 'replica').astype(f32)  27.9 us
    dot_general x1, matrix products, per_device(): jnp.dot(arrived, weight_in, preferred_element_type=f32)  24.2 us
    dot_general x1, matrix products, per_device(): jnp.dot(hidden, weight_out, preferred_element_type=f32)  19.4 us
  transfers between devices with their start and end apart: 13, of which 8 were waited for; matrix products, arithmetic and copies ran while one was open for 30% of the time, Pallas kernels for 0%

profile of v1, /device:TPU:0, one launch (start us, length us, event | category | flops | bytes accessed | tf_op | source)
XLA Modules:
  0.0 783.9 jit_solution(16884600131491742331)
XLA Ops:
  10.9 2.9 copy.113
  18.9 2.5 reduce-window.6
  22.6 73.4 %all-gather.2.cloned.1.call-done = bf16[768,3200]{1,0:T(8,128)(2,1)} async-done(((bf16[96,3200]{1,0:T(8,128)(2,1)}), bf16[768,3200]{1,0:T(8,128)(2,1)}) %all-gather.2.cloned.1.call-update) | async-done | bytes 4915216 | tf_op jit(solution)/shard_map/all_gather | solution.py:101
  98.6 6.8 add_convert_fusion
  105.4 11.9 %reshape.252 = bf16[4,197,3,12,64]{4,3,2,1,0:T(8,128)(2,1)} reshape(bf16[788,2304]{1,0:T(8,128)(2,1)} %add_convert_fusion) | data formatting | bytes 7262208 | tf_op jit(solution)/shard_map/reshape | solution.py:130
  117.3 6.9 fusion.102
  124.2 3.9 copy.153
  128.1 4.5 copy.154
  132.6 5.4 copy.152
  143.4 2.7 fusion.65
  146.1 2.4 copy.123
  148.5 4.2 convert_element_type.225
  152.7 3.0 fusion.104
  156.2 6.6 fusion.19
  162.9 3.7 all-to-all-start
  166.6 2.4 copy.128
  169.0 2.7 reshape.237
  171.7 7.0 fusion.22
  178.7 64.1 %all-to-all-done = bf16[8,280,768]{2,1,0:T(8,128)(2,1)S(1)} async-done(((bf16[8,280,768]{2,1,0:T(8,128)(2,1)}), bf16[8,280,768]{2,1,0:T(8,128)(2,1)S(1)}, u32[]{:S(2)}, u32[]{:S(2)}) %all-to-all-start) | async-done | bytes 3440672 | tf_op jit(solution)/shard_map/all_to_all | solution.py:43
  242.8 4.9 all-to-all-start.2
  250.4 2.3 add_convert_fusion.10
  253.8 2.7 convert_element_type.250
  260.7 24.2 %multiply_convert_fusion = (bf16[2240,3072]{1,0:T(8,128)(2,1)}, f32[2240,3072]{1,0:T(8,128)}) fusion(f32[3072]{0:T(1024)} %bitcast.137, bf16[2240,768]{1,0:T(8,128)(2,1)S(1)} %bitcast.127, bf16[1,768,3072]{2,1,0:T(8,128)(2,1)} %param.30), kind=kOutput, calls=%fused_computation.9 | convolution fusion | flops 10638458880 | bytes 49459200 | tf_op jit(solution)/shard_map/dot_general | solution.py:158
  285.0 39.2 %all-to-all-done.2 = bf16[8,280,768]{2,1,0:T(8,128)(2,1)} async-done(((bf16[8,280,768]{2,1,0:T(8,128)(2,1)}), bf16[8,280,768]{2,1,0:T(8,128)(2,1)}, u32[]{:S(2)}, u32[]{:S(2)}) %all-to-all-start.2) | async-done | bytes 3440672 | tf_op jit(solution)/shard_map/all_to_all | solution.py:43
  324.2 19.4 %multiply_reduce_fusion.2 = (f32[2240]{0:T(1024)S(1)}, f32[2240,768]{1,0:T(8,128)}, bf16[2240,768]{1,0:T(8,128)(2,1)}) fusion(f32[768]{0:T(1024)} %convert_reduce_fusion.1, bf16[2240,768]{1,0:T(8,128)(2,1)} %bitcast.86, f32[2240]{0:T(1024)S(1)} %multiply_reduce_fusion.11, bf16[2240,3072]{1,0:T(8,128)(2,1)} %get-tuple-element.126, ...), kind=kOutput, calls=%fused_computation.27 | convolution fusion | flops 10579965952 | bytes 32264704 | tf_op jit(solution)/shard_map/dot_general | solution.py:162
  343.6 3.0 fusion.101
  346.7 32.9 %fusion.106 = (bf16[3072]{0:T(1024)(128)(2,1)}, bf16[2240,3072]{1,0:T(8,128)(2,1)}) fusion(f32[2240,3072]{1,0:T(8,128)} %get-tuple-element.127, f32[3072]{0:T(1024)S(1)} %bitcast.138, bf16[2240,768]{1,0:T(8,128)(2,1)S(1)} %bitcast.134, bf16[1,3072,768]{2,1,0:T(8,128)(2,1)} %param.32), kind=kOutput, calls=%fused_computation.194 | convolution fusion | flops 10721031168 | bytes 49465344 | tf_op jit(solution)/shard_map/rd,fd->rf/dot_general | solution.py:170
  379.6 15.5 %fusion.35 = f32[2240,768]{1,0:T(8,128)S(1)} fusion(bf16[2240,3072]{1,0:T(8,128)(2,1)} %get-tuple-element.135, bf16[1,768,3072]{2,1,0:T(8,128)(2,1)} %param.30), kind=kOutput, calls=%fused_computation.52 | convolution fusion | flops 10569646080 | bytes 25362432 | tf_op jit(solution)/shard_map/rf,df->rd/dot_general | solution.py:174
  395.1 3.9 add_convert_fusion.1
  399.0 4.5 all-to-all-start.3
  403.6 17.1 %convolution_convert_fusion.1 = bf16[3072,768]{1,0:T(8,128)(2,1)S(1)} fusion(bf16[2240,3072]{1,0:T(8,128)(2,1)} %get-tuple-element.126, f32[2240,768]{1,0:T(8,128)} %get-tuple-element.111, f32[2240]{0:T(1024)S(1)} %multiply_reduce_fusion.11), kind=kOutput, calls=%fused_computation.38 | convolution fusion | flops 10575446016 | bytes 25371392 | tf_op jit(solution)/shard_map/rf,rd->fd/dot_general | solution.py:180
  422.5 15.4 %convolution_convert_fusion = bf16[768,3072]{1,0:T(8,128)(2,1)S(1)} fusion(bf16[2240,768]{1,0:T(8,128)(2,1)S(1)} %bitcast.128, bf16[2240,3072]{1,0:T(8,128)(2,1)} %get-tuple-element.135), kind=kOutput, calls=%fused_computation.37 | convolution fusion | flops 10572005376 | bytes 21921792 | tf_op jit(solution)/shard_map/rd,rf->df/dot_general | solution.py:182
  437.9 2.2 copy-done.19
  442.3 37.7 %all-to-all-done.3 = bf16[8,280,768]{2,1,0:T(8,128)(2,1)} async-done(((bf16[8,280,768]{2,1,0:T(8,128)(2,1)}), bf16[8,280,768]{2,1,0:T(8,128)(2,1)}, u32[]{:S(2)}, u32[]{:S(2)}) %all-to-all-start.3) | async-done | bytes 3440672 | tf_op jit(solution)/shard_map/all_to_all | solution.py:43
  480.0 7.2 multiply_reduce_fusion.3
  489.9 2.5 convolution_convert_fusion.3
  492.3 3.5 reshape.253
  495.9 4.0 copy.130
  499.9 7.6 multiply_reduce_fusion
  507.6 11.7 %multiply_convert_fusion.1 = bf16[4,12,197,197]{2,3,1,0:T(8,128)(2,1)} fusion(f32[4,12,197,197]{2,3,1,0:T(8,128)} %get-tuple-element.132, f32[4,12,197,197]{2,3,1,0:T(8,128)} %copy-done, f32[4,12,197]{2,1,0:T(8,128)S(1)} %get-tuple-element.131, f32[4,12,197]{2,1,0:T(8,128)S(1)} %copy-done.25), kind=kLoop, calls=%fused_computation.10 | loop fusion | flops 9314160 | bytes 18703968 | tf_op jit(solution)/shard_map/convert_element_type | solution.py:213
  519.3 3.6 multiply_bitcast_fusion.1
  525.3 5.7 fusion.51
  532.3 6.7 copy.135
  538.9 9.9 %convert_element_type.247 = bf16[788,2304]{0,1:T(8,128)(2,1)} reshape(bf16[4,197,3,12,64]{1,0,4,3,2:T(4,128)(2,1)} %copy.135) | data formatting | bytes 7262208 | tf_op jit(solution)/shard_map/convert_element_type | solution.py:223
  548.8 7.7 convolution_convert_fusion.2
  556.6 7.7 multiply_reduce_fusion.4
  564.8 2.9 convolution_convert_fusion.4
  567.7 2.4 pad_maximum_fusion
  570.2 4.5 all-to-all-start.1
  575.0 4.8 add_convert_fusion.3
  581.2 4.7 add_convert_fusion.5
  586.5 47.8 %collective-permute-done.4 = bf16[1536,768]{1,0:T(8,128)(2,1)} collective-permute-done((bf16[1536,768]{1,0:T(8,128)(2,1)}, bf16[1536,768]{1,0:T(8,128)(2,1)}, u32[]{:S(2)}, u32[]{:S(2)}) %collective-permute-start.4) | collective-permute-done | bytes 2359328 | tf_op jit(solution)/shard_map/ppermute | solution.py:60
  634.3 4.4 add_convert_fusion.2
  638.7 43.6 %collective-permute-done.1 = bf16[384,3072]{1,0:T(8,128)(2,1)} collective-permute-done((bf16[384,3072]{1,0:T(8,128)(2,1)}, bf16[384,3072]{1,0:T(8,128)(2,1)}, u32[]{:S(2)}, u32[]{:S(2)}) %collective-permute-start.1) | collective-permute-done | bytes 2359328 | tf_op jit(solution)/shard_map/ppermute | solution.py:60
  682.3 4.7 add_convert_fusion.4
  688.8 2.8 reshape.242
  691.6 2.8 copy.141
  694.4 6.8 add_convert_fusion.7
  704.4 2.7 broadcast_select_fusion.1
  707.1 4.5 fusion.31
  711.5 4.1 broadcast_select_fusion.3
  715.6 15.7 %reduce-scatter.2.cloned.1.call-done = bf16[96,3200]{1,0:T(8,128)(2,1)} async-done(((bf16[768,3200]{1,0:T(8,128)(2,1)}), bf16[96,3200]{1,0:T(8,128)(2,1)}) %reduce-scatter.2.cloned.1.call-update) | async-done | bytes 614416 | tf_op jit(solution)/shard_map/reduce_scatter | solution.py:254
  733.3 6.7 fusion.30
  740.0 27.9 %all-reduce.6.cloned.1.call-done = bf16[98,3200]{1,0:T(8,128)(2,1)} async-done(((bf16[98,3200]{1,0:T(8,128)(2,1)}), bf16[98,3200]{1,0:T(8,128)(2,1)}) %all-reduce.6.cloned.1.call-update) | async-done | bytes 627216 | tf_op jit(solution)/shard_map/psum | solution.py:260
  (212 shorter events, 55.5 us)
Async XLA Ops:
  7.2 6.6 copy-start.2
  7.2 88.9 %all-gather.2.cloned.1.call-start = ((), (), s32[]{:S(2)}) async-start(), calls=%async_computation.5 | async-start | bytes 5529600 | tf_op jit(solution)/shard_map/all_gather | solution.py:101
  14.3 4.0 copy-start.37
  16.3 82.3 %copy-start.40 = (f32[788]{0:T(1024)}, f32[788]{0:T(1024)S(1)}, u32[]{:S(2)}) copy-start(f32[788]{0:T(1024)S(1)} %rsqrt.21) | copy-start | bytes 9460
  16.4 82.2 %copy-start.42 = (f32[788]{0:T(1024)}, f32[788]{0:T(1024)S(1)}, u32[]{:S(2)}) copy-start(f32[788]{0:T(1024)S(1)} %div.43) | copy-start | bytes 9460
  18.4 87.0 %copy-start.12 = (f32[788,768]{1,0:T(8,128)}, f32[788,768]{1,0:T(8,128)S(1)}, u32[]{:S(2)}) copy-start(f32[788,768]{1,0:T(8,128)S(1)} %reshape.245) | copy-start | bytes 7262212
  22.6 133.6 %copy-start.53 = (s32[788]{0:T(1024)}, s32[788]{0:T(1024)S(1)}, u32[]{:S(2)}) copy-start(s32[788]{0:T(1024)S(1)} %get-tuple-element.103) | copy-start | bytes 9460
  22.6 149.0 %copy-start.51 = (s32[788]{0:T(1024)}, s32[788]{0:T(1024)S(1)}, u32[]{:S(2)}) copy-start(s32[788]{0:T(1024)S(1)} %get-tuple-element.102) | copy-start | bytes 9460
  98.5 57.7 %copy-start.38 = (f32[768]{0:T(1024)}, f32[768]{0:T(1024)S(1)}, u32[]{:S(2)}) copy-start(f32[768]{0:T(1024)S(1)} %get-tuple-element.88) | copy-start | bytes 9220
  98.6 151.8 %copy-start.33 = (f32[768]{0:T(1024)}, f32[768]{0:T(1024)S(1)}, u32[]{:S(2)}) copy-start(f32[768]{0:T(1024)S(1)} %get-tuple-element.94) | copy-start | bytes 9220
  128.1 9.9 %copy-start.3 = (bf16[4,197,1,12,64]{1,4,3,0,2:T(8,128)(2,1)}, bf16[4,197,1,12,64]{1,4,3,0,2:T(8,128)(2,1)S(1)}, u32[]{:S(2)}) copy-start(bf16[4,197,1,12,64]{1,4,3,0,2:T(8,128)(2,1)S(1)} %copy.153) | copy-start | bytes 3631108
  132.6 7.0 copy-start.5
  139.6 3.8 copy-start
  139.6 3.9 copy-start.27
  139.6 3.8 copy-start.16
  143.4 2.7 copy-start.29
  146.1 6.6 copy-start.13
  155.7 7.2 copy-start.7
  155.7 7.2 copy-start.35
  156.2 6.7 copy-start.44
  162.9 79.9 %all-to-all-start = ((bf16[8,280,768]{2,1,0:T(8,128)(2,1)}), bf16[8,280,768]{2,1,0:T(8,128)(2,1)S(1)}, u32[]{:S(2)}, u32[]{:S(2)}) async-start(bf16[8,280,768]{2,1,0:T(8,128)(2,1)} %bitcast.133), calls=%async_computation | async-start | bytes 6881280 | tf_op jit(solution)/shard_map/all_to_all | solution.py:43
  242.8 81.4 %all-to-all-start.2 = ((bf16[8,280,768]{2,1,0:T(8,128)(2,1)}), bf16[8,280,768]{2,1,0:T(8,128)(2,1)}, u32[]{:S(2)}, u32[]{:S(2)}) async-start(bf16[8,280,768]{2,1,0:T(8,128)(2,1)} %bitcast.132), calls=%async_computation.2 | async-start | bytes 6881280 | tf_op jit(solution)/shard_map/all_to_all | solution.py:43
  249.1 146.1 %copy-start.49 = (f32[8]{0:T(128)}, f32[8]{0:T(128)S(1)}, u32[]{:S(2)}) copy-start(f32[8]{0:T(128)S(1)} %compare_convert_fusion) | copy-start | bytes 100
  252.6 3.8 copy-start.28
  324.2 19.4 %copy-start.32 = (f32[8,280]{1,0:T(8,128)S(1)}, f32[8,280]{1,0:T(8,128)}, u32[]{:S(2)}) copy-start(f32[8,280]{1,0:T(8,128)} %mul.273) | copy-start | bytes 26884
  343.6 51.5 %copy-start.30 = (f32[2240]{0:T(1024)}, f32[2240]{0:T(1024)S(1)}, u32[]{:S(2)}) copy-start(f32[2240]{0:T(1024)S(1)} %mul.288) | copy-start | bytes 26884
  343.6 3.1 copy-start.46
  399.0 80.9 %all-to-all-start.3 = ((bf16[8,280,768]{2,1,0:T(8,128)(2,1)}), bf16[8,280,768]{2,1,0:T(8,128)(2,1)}, u32[]{:S(2)}, u32[]{:S(2)}) async-start(bf16[8,280,768]{2,1,0:T(8,128)(2,1)} %bitcast.130), calls=%async_computation.3 | async-start | bytes 6881280 | tf_op jit(solution)/shard_map/all_to_all | solution.py:43
  403.5 327.8 %reduce-scatter.2.cloned.1.call-start = ((), (), s32[]{:S(2)}) async-start(), calls=%async_computation.6 | async-start | bytes 5529600 | tf_op jit(solution)/shard_map/reduce_scatter | solution.py:254
  420.7 17.1 %copy-start.20 = (bf16[3072,768]{1,0:T(8,128)(2,1)}, bf16[3072,768]{1,0:T(8,128)(2,1)S(1)}, u32[]{:S(2)}) copy-start(bf16[3072,768]{1,0:T(8,128)(2,1)S(1)} %convolution_convert_fusion.1) | copy-start | bytes 14155780
  422.5 152.5 %collective-permute-start.3 = (bf16[1536,768]{1,0:T(8,128)(2,1)}, bf16[1536,768]{1,0:T(8,128)(2,1)}, u32[]{:S(2)}, u32[]{:S(2)}) collective-permute-start(bf16[1536,768]{1,0:T(8,128)(2,1)} %constant_dynamic-slice_fusion), channel_id=1, source_target_pairs={{0,8},{8,0},{16,24},{24,16},{1,9},{9,1},{17,25},{25,17},{2,10},{10... | collective-permute-start | bytes 7077896 | tf_op jit(solution)/shard_map/ppermute | solution.py:54
  437.8 2.2 copy-start.19
  440.1 39.9 %copy-start.36 = (f32[788]{0:T(1024)S(1)}, f32[788]{0:T(1024)}, u32[]{:S(2)}) copy-start(f32[788]{0:T(1024)} %copy-done.35) | copy-start | bytes 9460
  441.7 139.6 %collective-permute-start = (bf16[384,3072]{1,0:T(8,128)(2,1)}, bf16[384,3072]{1,0:T(8,128)(2,1)}, u32[]{:S(2)}, u32[]{:S(2)}) collective-permute-start(bf16[384,3072]{1,0:T(8,128)(2,1)} %constant_dynamic-slice_fusion.1), channel_id=1, source_target_pairs={{0,8},{8,0},{16,24},{24,16},{1,9},{9,1},{17,25},{25,17},{2,10},{10... | collective-permute-start | bytes 7077896 | tf_op jit(solution)/shard_map/ppermute | solution.py:54
  480.0 7.3 copy-start.8
  480.0 7.3 copy-start.18
  480.0 7.3 copy-start.39
  480.0 7.3 copy-start.45
  495.9 4.0 copy-start.17
  495.9 4.0 copy-start.25
  507.6 11.7 %copy-start.6 = (bf16[4,197,1,12,64]{1,4,3,0,2:T(8,128)(2,1)S(1)}, bf16[4,197,1,12,64]{1,4,3,0,2:T(8,128)(2,1)}, u32[]{:S(2)}) copy-start(bf16[4,197,1,12,64]{1,4,3,0,2:T(8,128)(2,1)} %copy-done.5) | copy-start | bytes 3631108
  519.3 3.9 copy-start.1
  519.3 4.4 copy-start.4
  538.9 9.9 %copy-start.24 = (bf16[788,768]{1,0:T(8,128)(2,1)S(1)}, bf16[788,768]{1,0:T(8,128)(2,1)}, u32[]{:S(2)}) copy-start(bf16[788,768]{1,0:T(8,128)(2,1)} %convert_element_type.250) | copy-start | bytes 3631108
  548.8 7.7 copy-start.14
  548.8 7.7 copy-start.21
  548.8 7.7 copy-start.34
  548.8 7.7 copy-start.41
  548.8 7.7 copy-start.43
  556.5 8.2 %copy-start.11 = (f32[788,768]{1,0:T(8,128)S(1)}, f32[788,768]{1,0:T(8,128)}, u32[]{:S(2)}) copy-start(f32[788,768]{1,0:T(8,128)} %copy-done.10) | copy-start | bytes 7262212
  564.8 2.9 copy-start.22
  570.2 124.2 %all-to-all-start.1 = ((bf16[8,280,768]{2,1,0:T(8,128)(2,1)}), bf16[8,280,768]{2,1,0:T(8,128)(2,1)}, u32[]{:S(2)}, u32[]{:S(2)}) async-start(bf16[8,280,768]{2,1,0:T(8,128)(2,1)} %bitcast.131), calls=%async_computation.1 | async-start | bytes 6881280 | tf_op jit(solution)/shard_map/all_to_all | solution.py:43
  574.7 193.2 %all-reduce.6.cloned.1.call-start = ((), (), s32[]{:S(2)}) async-start(), calls=%async_computation.7 | async-start | bytes 1331200 | tf_op jit(solution)/shard_map/psum | solution.py:260
  579.8 6.7 copy-start.47
  579.8 6.7 copy-start.48
  579.8 54.5 %collective-permute-start.4 = (bf16[1536,768]{1,0:T(8,128)(2,1)}, bf16[1536,768]{1,0:T(8,128)(2,1)}, u32[]{:S(2)}, u32[]{:S(2)}) collective-permute-start(bf16[1536,768]{1,0:T(8,128)(2,1)} %add_convert_fusion.3), channel_id=1, source_target_pairs={{0,16},{8,24},{16,0},{24,8},{1,17},{9,25},{17,1},{25,9},{2,18},{10... | collective-permute-start | bytes 7077896 | tf_op jit(solution)/shard_map/ppermute | solution.py:60
  585.9 96.4 %collective-permute-start.1 = (bf16[384,3072]{1,0:T(8,128)(2,1)}, bf16[384,3072]{1,0:T(8,128)(2,1)}, u32[]{:S(2)}, u32[]{:S(2)}) collective-permute-start(bf16[384,3072]{1,0:T(8,128)(2,1)} %add_convert_fusion.5), channel_id=1, source_target_pairs={{0,16},{8,24},{16,0},{24,8},{1,17},{9,25},{17,1},{25,9},{2,18},{10... | collective-permute-start | bytes 7077896 | tf_op jit(solution)/shard_map/ppermute | solution.py:60
  638.7 48.3 %copy-start.15 = (f32[788,768]{1,0:T(8,128)S(1)}, f32[788,768]{1,0:T(8,128)}, u32[]{:S(2)}) copy-start(f32[788,768]{1,0:T(8,128)} %copy-done.12) | copy-start | bytes 7262212
  638.7 48.3 %copy-start.23 = (f32[788,768]{1,0:T(8,128)S(1)}, f32[788,768]{1,0:T(8,128)}, u32[]{:S(2)}) copy-start(f32[788,768]{1,0:T(8,128)} %get-tuple-element.133) | copy-start | bytes 7262212
  638.7 65.7 %collective-permute-start.5 = (bf16[1536,768]{1,0:T(8,128)(2,1)}, bf16[1536,768]{1,0:T(8,128)(2,1)}, u32[]{:S(2)}, u32[]{:S(2)}) collective-permute-start(bf16[1536,768]{1,0:T(8,128)(2,1)} %add_convert_fusion.2), channel_id=1, source_target_pairs={{0,8},{8,0},{16,24},{24,16},{1,9},{9,1},{17,25},{25,17},{2,10},{10... | collective-permute-start | bytes 7077896 | tf_op jit(solution)/shard_map/ppermute | solution.py:63
  686.9 24.6 %collective-permute-start.2 = (bf16[384,3072]{1,0:T(8,128)(2,1)}, bf16[384,3072]{1,0:T(8,128)(2,1)}, u32[]{:S(2)}, u32[]{:S(2)}) collective-permute-start(bf16[384,3072]{1,0:T(8,128)(2,1)} %add_convert_fusion.4), channel_id=1, source_target_pairs={{0,8},{8,0},{16,24},{24,16},{1,9},{9,1},{17,25},{25,17},{2,10},{10... | collective-permute-start | bytes 7077896 | tf_op jit(solution)/shard_map/ppermute | solution.py:63
  688.8 5.6 copy-start.9
  688.8 5.6 copy-start.52
  688.8 5.6 copy-start.54
  (4 other events, 5.2 us)
Sparse Core Ops, SparseCore 0:
  11.0 85.0 all-gather.1
  570.3 161.0 reduce-scatter.1
  734.4 33.4 all-reduce.5

commit v2 on v1

v2 whole, which is shorter than its diff:
```python
import functools

import jax
import jax.numpy as jnp
from jax import lax
from jax.experimental import pallas as pl
from jax.experimental.pallas import tpu as pltpu
from jax.sharding import PartitionSpec as P

HEADS = 12
HEAD_DIM = 64
LANES = 128
VMEM_BYTES = 56 * 1024 * 1024


eps_norm = 1e-06
f32 = jnp.float32
bf16 = jnp.bfloat16

GAIN_ONE, SHIFT_ONE, QUERY_BIAS, VALUE_BIAS, OUT_SHIFT, GAIN_TWO, SHIFT_TWO = range(7)
VECTORS = 7


def round_up(value, multiple):
    return -(-value // multiple) * multiple


def normalize(values):
    average = jnp.mean(values, -1, keepdims=True)
    centred = values - average
    variance = jnp.mean(centred * centred, -1, keepdims=True)
    inverse = lax.rsqrt(variance + eps_norm)
    return (centred * inverse, inverse)


def norm_back(grad_out, scaled, inverse, gain_vec):
    gain_grad = jnp.sum(grad_out * scaled, 0, keepdims=True)
    shift_grad = jnp.sum(grad_out, 0, keepdims=True)
    grad_scaled = grad_out * gain_vec
    first_term = jnp.mean(grad_scaled, -1, keepdims=True)
    second_term = jnp.mean(grad_scaled * scaled, -1, keepdims=True)
    return (inverse * (grad_scaled - first_term - scaled * second_term), gain_grad, shift_grad)


def dot(left, right):
    return jnp.dot(left, right, preferred_element_type=f32)


def dot_last(left, right):
    return lax.dot_general(left, right, (((1,), (1,)), ((), ())), preferred_element_type=f32)


def dot_first(left, right):
    return lax.dot_general(left, right, (((0,), (0,)), ((), ())), preferred_element_type=f32)


def params(steps=0):
    return pltpu.CompilerParams(
        vmem_limit_bytes=VMEM_BYTES,
        dimension_semantics=("arbitrary",) * steps if steps else None,
    )


def cost():
    return pl.CostEstimate(flops=1 << 20, bytes_accessed=1 << 16, transcendentals=0)


def whole(shape):
    return pl.BlockSpec(shape, lambda *_: (0,) * len(shape))


def scalar_spec():
    return pl.BlockSpec(memory_space=pltpu.SMEM)


def forward_kernel(seq_len, width, x_ref, w_ref, vec_ref, h1_ref, qkv_ref, o_ref, mid_ref, h2_ref):
    vec = vec_ref[...]

    def row(index):
        return vec[index : index + 1]

    x = x_ref[0].astype(f32)
    scaled, _ = normalize(x)
    h1 = (scaled * row(GAIN_ONE) + row(SHIFT_ONE)).astype(bf16)
    h1_ref[0] = h1
    for part, bias in ((0, QUERY_BIAS), (1, None), (2, VALUE_BIAS)):
        block = dot(h1, w_ref[:, part * width : (part + 1) * width])
        if bias is not None:
            block = block + row(bias)
        qkv_ref[0, :, part * width : (part + 1) * width] = block.astype(bf16)
    rows = x.shape[0]
    lane = lax.broadcasted_iota(jnp.int32, (1, LANES), 1)
    key_there = lax.broadcasted_iota(jnp.int32, (1, rows), 1) < seq_len
    factor = HEAD_DIM ** (-0.5)
    for pair in range(width // LANES):
        at = pair * LANES
        queries = qkv_ref[0, :, at : at + LANES] * jnp.asarray(factor, bf16)
        keys = qkv_ref[0, :, width + at : width + at + LANES]
        values = qkv_ref[0, :, 2 * width + at : 2 * width + at + LANES]
        total = None
        for half in range(LANES // HEAD_DIM):
            mine = (lane // HEAD_DIM) == half
            scores = dot_last(jnp.where(mine, queries, jnp.zeros_like(queries)), keys)
            scores = jnp.where(key_there, scores, -1e30)
            powers = jnp.exp(scores - jnp.max(scores, -1, keepdims=True))
            probs = (powers * (1.0 / jnp.sum(powers, -1, keepdims=True))).astype(bf16)
            part = dot(probs, jnp.where(mine, values, jnp.zeros_like(values)))
            total = part if total is None else total + part
        o_ref[0, :, at : at + LANES] = total.astype(bf16)
    middle = x + (dot(o_ref[0], w_ref[:, 3 * width : 4 * width]) + row(OUT_SHIFT))
    mid_ref[0] = middle
    scaled, _ = normalize(middle)
    h2_ref[0] = (scaled * row(GAIN_TWO) + row(SHIFT_TWO)).astype(bf16)


def attention_forward(x, packed, vec, seq_len):
    images, rows, width = x.shape

    def spec(columns):
        return pl.BlockSpec((1, rows, columns), lambda i: (i, 0, 0))

    def shape(columns, dtype):
        return jax.ShapeDtypeStruct((images, rows, columns), dtype)

    return pl.pallas_call(
        functools.partial(forward_kernel, seq_len, width),
        grid=(images,),
        in_specs=[spec(width), whole(packed.shape), whole(vec.shape)],
        out_specs=[spec(width), spec(3 * width), spec(width), spec(width), spec(width)],
        out_shape=[
            shape(width, bf16),
            shape(3 * width, bf16),
            shape(width, bf16),
            shape(width, f32),
            shape(width, bf16),
        ],
        compiler_params=params(1),
        cost_estimate=cost(),
        name="attention_forward",
    )(x, packed, vec)


def dispatch_kernel(slot_ref, rows_ref, out_ref):
    slots = slot_ref[...]
    high = out_ref.shape[0]
    slot = lax.broadcasted_iota(jnp.int32, (high, rows_ref.shape[0]), 0) + pl.program_id(0) * high
    hot = jnp.where((slot == slots[0:1]) | (slot == slots[1:2]), 1.0, 0.0).astype(bf16)
    out_ref[...] = dot(hot, rows_ref[...]).astype(bf16)


def dispatch(slots, rows, places, steps):
    width = rows.shape[1]
    return pl.pallas_call(
        dispatch_kernel,
        in_specs=[whole(slots.shape), whole(rows.shape)],
        out_specs=pl.BlockSpec((places // steps, width), lambda e: (e, 0)),
        grid=(steps,),
        out_shape=jax.ShapeDtypeStruct((places, width), bf16),
        compiler_params=params(1),
        cost_estimate=cost(),
        name="dispatch",
    )(slots, rows)


def expert_kernel(
    experts,
    tiles,
    here_ref,
    rows_ref,
    cot_ref,
    in_ref,
    in_bias_ref,
    out_ref,
    out_bias_ref,
    router_ref,
    back_ref,
    gated_ref,
    hidden_ref,
    inner_ref,
    outer_ref,
    logit_ref,
    in_sum_ref,
    out_sum_ref,
    slope_ref,
    total_ref,
):
    phase, tile = pl.program_id(0), pl.program_id(1)

    @pl.when(phase == 0)
    def _():
        act = dot(rows_ref[...], in_ref[0]) + in_bias_ref[...].astype(f32)
        square = act * act
        slant = 0.7978845608028654
        bend = jnp.tanh(act * (slant + (slant * 0.044715) * square))
        half = 0.5 + 0.5 * bend
        hidden = (act * half).astype(bf16)
        hidden_ref[...] = hidden
        slope_ref[tile] = half + (0.5 * act) * (1.0 - bend * bend) * (
            slant + (3.0 * slant * 0.044715) * square
        )
        part = dot(hidden, out_ref[0])

        @pl.when(tile == 0)
        def _():
            total_ref[...] = part

        @pl.when(tile > 0)
        def _():
            total_ref[...] += part

    @pl.when((phase == 0) & (tile == tiles - 1))
    def _():
        outer = total_ref[...] + out_bias_ref[...].astype(f32)
        logits = dot(rows_ref[...], router_ref[...])
        lane = lax.broadcasted_iota(jnp.int32, (1, LANES), 1)
        logits = jnp.where(lane < experts, logits, -1e30)
        powers = jnp.exp(logits - jnp.max(logits, -1, keepdims=True))
        probs = powers / jnp.sum(powers, -1, keepdims=True)
        is_here = jnp.where(lane == here_ref[0], 1.0, 0.0)
        gate = jnp.sum(probs * is_here, -1, keepdims=True)
        gated_ref[...] = (gate * outer).astype(bf16)
        cot = cot_ref[...].astype(f32)
        gate_grad = jnp.sum(cot * outer, -1, keepdims=True)
        outer_grad = (gate * cot).astype(bf16)
        outer_ref[...] = outer_grad
        out_sum_ref[...] = jnp.sum(outer_grad.astype(f32), 0, keepdims=True)
        logit_ref[...] = ((gate_grad * gate) * (is_here - probs)).astype(bf16)

    @pl.when(phase == 1)
    def _():
        hidden_grad = dot_last(outer_ref[...], out_ref[0])
        inner = (hidden_grad * slope_ref[tile]).astype(bf16)
        inner_ref[...] = inner
        in_sum_ref[...] = jnp.sum(inner.astype(f32), 0, keepdims=True)
        part = dot_last(inner, in_ref[0])

        @pl.when(tile == 0)
        def _():
            total_ref[...] = part + dot_last(logit_ref[...], router_ref[...])

        @pl.when(tile > 0)
        def _():
            total_ref[...] += part

    @pl.when((phase == 1) & (tile == tiles - 1))
    def _():
        back_ref[...] = total_ref[...].astype(bf16)


def expert_chunk(here, rows_in, cots, weights, router, experts):
    rows, width = rows_in.shape
    weight_in, bias_in, weight_out, bias_out = weights
    hidden = weight_in.shape[2]
    depth = 512
    tiles = hidden // depth

    def first_phase(p, f, _):
        return (0, jnp.where(p == 0, f, tiles - 1))

    def second_phase(p, f, _):
        return (0, jnp.where(p == 0, 0, f))

    every = whole((rows, width))

    def shape(columns):
        return jax.ShapeDtypeStruct((rows, columns), bf16)

    return pl.pallas_call(
        functools.partial(expert_kernel, experts, tiles),
        grid_spec=pltpu.PrefetchScalarGridSpec(
            num_scalar_prefetch=1,
            grid=(2, tiles),
            in_specs=[
                every,
                every,
                pl.BlockSpec((1, width, depth), lambda p, f, _: (0, 0, f)),
                pl.BlockSpec((1, depth), lambda p, f, _: (0, f)),
                pl.BlockSpec((1, depth, width), lambda p, f, _: (0, f, 0)),
                whole((1, width)),
                whole(router.shape),
            ],
            out_specs=[
                every,
                every,
                pl.BlockSpec((rows, depth), first_phase),
                pl.BlockSpec((rows, depth), second_phase),
                every,
                whole((rows, LANES)),
                pl.BlockSpec((1, depth), second_phase),
                whole((1, width)),
            ],
            scratch_shapes=[
                pltpu.VMEM((tiles, rows, depth), f32),
                pltpu.VMEM((rows, width), f32),
            ],
        ),
        out_shape=[
            shape(width),
            shape(width),
            shape(hidden),
            shape(hidden),
            shape(width),
            shape(LANES),
            jax.ShapeDtypeStruct((1, hidden), f32),
            jax.ShapeDtypeStruct((1, width), f32),
        ],
        compiler_params=params(2),
        cost_estimate=cost(),
        name="expert_chunk",
    )(here, rows_in, cots, weight_in, bias_in, weight_out, bias_out, router)


def out_grad_kernel(parts, core_ref, *refs):
    hidden_refs, outer_refs = refs[:parts], refs[parts : 2 * parts]
    mine_ref, other_ref = refs[2 * parts : 2 * parts + 2]
    turned_refs = refs[2 * parts + 2 :]
    step = pl.program_id(0)

    @pl.when(step == 0)
    def _():
        for outer_ref, turned_ref in zip(outer_refs, turned_refs):
            turned_ref[...] = outer_ref[...].T

    total = sum(dot(turned[...], hidden[...]) for turned, hidden in zip(turned_refs, hidden_refs))
    block = total.astype(bf16).T

    @pl.when(step < pl.num_programs(0) // 2)
    def _():
        other_ref[...] = block

    @pl.when(step >= pl.num_programs(0) // 2)
    def _():
        mine_ref[...] = block


def out_grad(core, hiddens, outers):
    parts = len(hiddens)
    high, wide = hiddens[0].shape[1], outers[0].shape[1]
    tile = 512
    half = high // 2 // tile

    def place(i, core_ref):
        own = i >= half
        return (0, jnp.where(own, core_ref[0], 1 - core_ref[0]) * half + i - own * half)

    return pl.pallas_call(
        functools.partial(out_grad_kernel, parts),
        grid_spec=pltpu.PrefetchScalarGridSpec(
            num_scalar_prefetch=1,
            grid=(2 * half,),
            in_specs=[pl.BlockSpec((rows.shape[0], tile), place) for rows in hiddens]
            + [whole(rows.shape) for rows in outers],
            out_specs=[
                pl.BlockSpec((tile, wide), lambda i, _: (jnp.maximum(i - half, 0), 0)),
                pl.BlockSpec((tile, wide), lambda i, _: (jnp.minimum(i, half - 1), 0)),
            ],
            scratch_shapes=[pltpu.VMEM((wide, rows.shape[0]), bf16) for rows in outers],
        ),
        out_shape=[jax.ShapeDtypeStruct((high // 2, wide), bf16)] * 2,
        compiler_params=params(1),
        cost_estimate=cost(),
        name="out_grad",
    )(core, *hiddens, *outers)


def in_grad_kernel(parts, core_ref, *refs):
    arrived_refs, inner_refs, logit_refs = (refs[i * parts : (i + 1) * parts] for i in range(3))
    mine_ref, other_ref, router_ref = refs[3 * parts : 3 * parts + 3]
    turned_refs = refs[3 * parts + 3 :]
    half = mine_ref.shape[0]

    @pl.when(pl.program_id(0) == 0)
    def _():
        for arrived_ref, turned_ref in zip(arrived_refs, turned_refs):
            turned = arrived_ref[...].T
            turned_ref[0] = turned[:half]
            turned_ref[1] = turned[half:]
        for h in range(2):
            router_ref[h * half : (h + 1) * half, :] = sum(
                dot(turned[h], logit[...]) for turned, logit in zip(turned_refs, logit_refs)
            )

    core = core_ref[0]
    mine_ref[...] = sum(
        dot(turned[core], inner[...]) for turned, inner in zip(turned_refs, inner_refs)
    ).astype(bf16)
    other_ref[...] = sum(
        dot(turned[1 - core], inner[...]) for turned, inner in zip(turned_refs, inner_refs)
    ).astype(bf16)


def in_grad(core, arrived, inners, logits):
    parts = len(inners)
    high, wide = arrived[0].shape[1], inners[0].shape[1]
    tile = 512
    spec = pl.BlockSpec((high // 2, tile), lambda i, _: (0, i))
    return pl.pallas_call(
        functools.partial(in_grad_kernel, parts),
        grid_spec=pltpu.PrefetchScalarGridSpec(
            num_scalar_prefetch=1,
            grid=(wide // tile,),
            in_specs=[whole(rows.shape) for rows in arrived]
            + [pl.BlockSpec((rows.shape[0], tile), lambda i, _: (0, i)) for rows in inners]
            + [whole(rows.shape) for rows in logits],
            out_specs=[spec, spec, whole((high, LANES))],
            scratch_shapes=[pltpu.VMEM((2, high // 2, rows.shape[0]), bf16) for rows in arrived],
        ),
        out_shape=[jax.ShapeDtypeStruct((high // 2, wide), bf16)] * 2
        + [jax.ShapeDtypeStruct((high, LANES), f32)],
        compiler_params=params(1),
        cost_estimate=cost(),
        name="in_grad",
    )(core, *arrived, *inners, *logits)


def widen_kernel(core_ref, mine_ref, theirs_ref, out_ref):
    own = pl.program_id(0) == core_ref[0]

    @pl.when(own)
    def _():
        out_ref[...] = mine_ref[...].astype(f32)

    @pl.when(jnp.logical_not(own))
    def _():
        out_ref[...] = theirs_ref[...].astype(f32)


def widen(core, mine, theirs):
    high, wide = mine.shape
    tile = high // 4

    def block(is_mine):
        def index(h, i, core_ref):
            used = (h == core_ref[0]) == is_mine
            return (jnp.where(used, i, 0), 0)

        return pl.BlockSpec((tile, wide), index)

    return pl.pallas_call(
        widen_kernel,
        grid_spec=pltpu.PrefetchScalarGridSpec(
            num_scalar_prefetch=1,
            grid=(2, 4),
            in_specs=[block(True), block(False)],
            out_specs=pl.BlockSpec((tile, wide), lambda h, i, _: (h * 4 + i, 0)),
        ),
        out_shape=jax.ShapeDtypeStruct((2 * high, wide), f32),
        compiler_params=params(2),
        cost_estimate=cost(),
        name="widen",
    )(core, mine, theirs)


def collect(slots, rows):
    slot = lax.broadcasted_iota(jnp.int32, (1, rows.shape[0]), 1)
    hot = (slots[:, 0:1] == slot) | (slots[:, 1:2] == slot)
    return dot(jnp.where(hot, 1.0, 0.0).astype(bf16), rows)


def collect_parts(slots, part_refs):
    return sum(
        collect(slots[:, 2 * part : 2 * part + 2], part_ref[...])
        for part, part_ref in enumerate(part_refs)
    )


def output_kernel(slot_ref, mid_ref, *refs):
    refs[-1][0] = (mid_ref[0] + collect_parts(slot_ref[0].T, refs[:-1])).astype(bf16)


def combine_output(image_slots, middle, returned):
    images, rows, width = middle.shape
    spec = pl.BlockSpec((1, rows, width), lambda i: (i, 0, 0))
    return pl.pallas_call(
        output_kernel,
        grid=(images,),
        in_specs=[pl.BlockSpec((1, *image_slots.shape[1:]), lambda i: (i, 0, 0)), spec]
        + [whole(part.shape) for part in returned],
        out_specs=spec,
        out_shape=jax.ShapeDtypeStruct((images, rows, width), bf16),
        compiler_params=params(1),
        cost_estimate=cost(),
        name="combine_output",
    )(image_slots, middle, *returned)


def backward_kernel(seq_len, width, experts, parts, core_ref, *refs):
    slot_ref, x_ref, cot_ref, mid_ref, qkv_ref, w_ref, vec_ref = refs[:7]
    h1_ref, o_ref, router_ref = refs[7:10]
    part_refs = refs[10 : 10 + parts]
    grad_ref, mine_ref, other_ref, dqkv_ref, sums_ref, total_ref = refs[10 + parts :]
    vec = vec_ref[...]

    def row(index):
        return vec[index : index + 1]

    h2_grad = collect_parts(slot_ref[0].T, part_refs)
    scaled, inverse = normalize(mid_ref[0])
    norm_grad, gain_two_grad, shift_two_grad = norm_back(h2_grad, scaled, inverse, row(GAIN_TWO))
    mid_grad = cot_ref[0].astype(f32) + norm_grad
    branch = mid_grad.astype(bf16)
    out_shift_grad = jnp.sum(branch.astype(f32), 0, keepdims=True)
    o_grad = dot_last(branch, w_ref[:, 3 * width : 4 * width]).astype(bf16)

    rows = branch.shape[0]
    lane = lax.broadcasted_iota(jnp.int32, (1, LANES), 1)
    key_there = lax.broadcasted_iota(jnp.int32, (rows, 1), 0) < seq_len
    factor = HEAD_DIM ** (-0.5)
    for pair in range(width // LANES):
        at = pair * LANES
        queries = qkv_ref[0, :, at : at + LANES] * jnp.asarray(factor, bf16)
        keys = qkv_ref[0, :, width + at : width + at + LANES]
        values = qkv_ref[0, :, 2 * width + at : 2 * width + at + LANES]
        grads = o_grad[:, at : at + LANES]
        query_grad = key_grad = value_grad = None
        for half in range(LANES // HEAD_DIM):
            mine = (lane // HEAD_DIM) == half

            def only(slab):
                return jnp.where(mine, slab, jnp.zeros_like(slab))

            own_queries, own_keys, own_grads = only(queries), only(keys), only(grads)
            scores = dot_last(own_keys, queries)
            scores = jnp.where(key_there, scores, -1e30)
            powers = jnp.exp(scores - jnp.max(scores, 0, keepdims=True))
            probs = powers * (1.0 / jnp.sum(powers, 0, keepdims=True))
            prob_grad = dot_last(values, own_grads)
            spread = jnp.sum(probs * prob_grad, 0, keepdims=True)
            score_grad = (probs * (prob_grad - spread)).astype(bf16)
            value_part = dot(probs.astype(bf16), own_grads)
            key_part = dot(score_grad, own_queries)
            query_part = dot_first(score_grad, own_keys)
            if half == 0:
                query_grad, key_grad, value_grad = query_part, key_part, value_part
            else:
                query_grad += query_part
                key_grad += key_part
                value_grad += value_part
        dqkv_ref[:, at : at + LANES] = (query_grad * factor).astype(bf16)
        dqkv_ref[:, width + at : width + at + LANES] = key_grad.astype(bf16)
        dqkv_ref[:, 2 * width + at : 2 * width + at + LANES] = value_grad.astype(bf16)

    h1_grad = dot_last(dqkv_ref[...], w_ref[:, : 3 * width])
    query_sum = jnp.sum(dqkv_ref[:, :width].astype(f32), 0, keepdims=True)
    value_sum = jnp.sum(dqkv_ref[:, 2 * width :].astype(f32), 0, keepdims=True)
    scaled, inverse = normalize(x_ref[0].astype(f32))
    norm_grad, gain_one_grad, shift_one_grad = norm_back(h1_grad, scaled, inverse, row(GAIN_ONE))
    grad_ref[0] = (mid_grad + norm_grad).astype(bf16)
    sums = [
        gain_one_grad,
        shift_one_grad,
        query_sum,
        value_sum,
        out_shift_grad,
        gain_two_grad,
        shift_two_grad,
        jnp.zeros((sums_ref.shape[0] - VECTORS, width), f32),
    ]
    sums = jnp.concatenate(sums, 0)

    image = pl.program_id(0)
    qkv_part = dot_first(h1_ref[0], dqkv_ref[...])
    out_part = dot_first(o_ref[0], branch)

    @pl.when(image == 0)
    def _():
        sums_ref[...] = sums
        total_ref[:, : 3 * width] = qkv_part
        total_ref[:, 3 * width : 4 * width] = out_part

    @pl.when(image > 0)
    def _():
        sums_ref[...] += sums
        total_ref[:, : 3 * width] += qkv_part
        total_ref[:, 3 * width : 4 * width] += out_part

    @pl.when(image == pl.num_programs(0) - 1)
    def _():
        small = total_ref.shape[1] - 4 * width
        column = lax.broadcasted_iota(jnp.int32, (8, small), 1)
        pick = jnp.where(column == experts + lax.broadcasted_iota(jnp.int32, (8, small), 0), 1.0, 0.0)
        total_ref[:, 4 * width :] = dot_first(sums_ref[...].astype(bf16), pick.astype(bf16))
        own = lax.broadcasted_iota(jnp.int32, (1, LANES), 1) < experts
        total_ref[:, 4 * width : 4 * width + LANES] += jnp.where(own, router_ref[...], 0.0)
        half = total_ref.shape[1] // 2

        @pl.when(core_ref[0] == 0)
        def _():
            mine_ref[...] = total_ref[:, :half].astype(bf16)
            other_ref[...] = total_ref[:, half:].astype(bf16)

        @pl.when(core_ref[0] != 0)
        def _():
            other_ref[...] = total_ref[:, :half].astype(bf16)
            mine_ref[...] = total_ref[:, half:].astype(bf16)


def attention_backward(
    core, image_slots, x, cot, middle, qkv, packed, vec, h1, attended, router_grad, back, experts, seq_len
):
    images, rows, width = x.shape
    columns = 4 * width + round_up(experts + VECTORS, 2 * LANES)

    def spec(columns):
        return pl.BlockSpec((1, rows, columns), lambda i: (i, 0, 0))

    half = jax.ShapeDtypeStruct((width, columns // 2), bf16)
    return pl.pallas_call(
        functools.partial(backward_kernel, seq_len, width, experts, len(back)),
        grid=(images,),
        in_specs=[
            scalar_spec(),
            pl.BlockSpec((1, *image_slots.shape[1:]), lambda i: (i, 0, 0)),
            spec(width),
            spec(width),
            spec(width),
            spec(3 * width),
            whole(packed.shape),
            whole(vec.shape),
            spec(width),
            spec(width),
            whole(router_grad.shape),
        ]
        + [whole(part.shape) for part in back],
        out_specs=[spec(width), whole(half.shape), whole(half.shape)],
        out_shape=[jax.ShapeDtypeStruct(x.shape, bf16), half, half],
        scratch_shapes=[
            pltpu.VMEM((rows, 3 * width), bf16),
            pltpu.VMEM((8, width), f32),
            pltpu.VMEM((width, columns), f32),
        ],
        compiler_params=params(1),
        cost_estimate=cost(),
        name="attention_backward",
    )(core, image_slots, x, cot, middle, qkv, packed, vec, h1, attended, router_grad, *back)


def swap(value, axis, distance):
    count = lax.axis_size(axis)
    return lax.ppermute(value, axis, [(i, i ^ distance) for i in range(count)])


def exchange(rows):
    experts = lax.axis_size("shard")
    blocks = rows.reshape(experts, rows.shape[0] // experts, rows.shape[1])
    moved = lax.all_to_all(blocks, "shard", split_axis=0, concat_axis=0, tiled=True)
    return moved.reshape(rows.shape)


def add(left, right):
    return (left.astype(f32) + right.astype(f32)).astype(bf16)


def halves(value, core, axis):
    half = value.shape[axis] // 2
    mine = lax.dynamic_slice_in_dim(value, core * half, half, axis)
    other = lax.dynamic_slice_in_dim(value, (1 - core) * half, half, axis)
    return mine, other


def join(mine, theirs, core, axis):
    first = jnp.where(core == 0, mine, theirs)
    second = jnp.where(core == 0, theirs, mine)
    return jnp.concatenate([first, second], axis)


def over_chips(value):
    step = 2
    while step < lax.axis_size("replica"):
        value = add(value, swap(value, "replica", step))
        step *= 2
    return value


def tie(*values):
    return lax.optimization_barrier(values)


def per_device(
    images,
    routes,
    cotangent,
    ln1_gain,
    ln1_bias,
    qkv_weight,
    q_bias,
    v_bias,
    out_weight,
    out_bias,
    ln2_gain,
    ln2_bias,
    router_weight,
    expert_in,
    expert_in_bias,
    expert_out,
    expert_out_bias,
):
    experts = lax.axis_size("shard")
    here = lax.axis_index("shard").reshape(1).astype(jnp.int32)
    core = lax.axis_index("replica") % 2
    images_here, seq_len, width = images.shape
    tokens_here = images_here * seq_len
    capacity = 14 * tokens_here // (5 * experts)
    first_part = round_up(-(-capacity // 2), 16)
    parts = [(0, first_part), (first_part, round_up(capacity - first_part, 8))]
    rows = round_up(seq_len, 16)
    tokens = images_here * rows

    columns = [ln1_gain, ln1_bias, q_bias, v_bias, out_bias, ln2_gain, ln2_bias]
    small = jnp.concatenate([router_weight, jnp.stack(columns, 1)], 1)
    small_width = round_up(small.shape[1], LANES)
    small = jnp.pad(small, ((0, 0), (0, small_width - small.shape[1])))
    shard = jnp.concatenate([qkv_weight, out_weight, small], 1)
    mine, _ = halves(shard, core, 0)
    mine = lax.all_gather(mine, "shard", axis=0, tiled=False)

    pad_rows = ((0, 0), (0, rows - seq_len), (0, 0))
    route_rows = jnp.pad(routes, pad_rows, constant_values=-1).reshape(tokens, 2).T
    expert_ids = jnp.arange(experts, dtype=jnp.int32)[:, None]
    named = (route_rows[0:1] == expert_ids) | (route_rows[1:2] == expert_ids)
    token = jnp.arange(tokens, dtype=jnp.int32)
    earlier = (token[:, None] < token[None, :]).astype(bf16)
    ranking = dot(named.astype(bf16), earlier).astype(jnp.int32)
    ranks = [
        jnp.sum(jnp.where(route_rows[j][None] == expert_ids, ranking, 0), 0) for j in range(2)
    ]
    there = route_rows[0] >= 0
    part_slots = [
        jnp.where(
            there & (ranks[j] >= first) & (ranks[j] < first + size),
            route_rows[j] * size + ranks[j] - first,
            -1,
        )
        for first, size in parts
        for j in range(2)
    ]
    part_rows = [jnp.stack(part_slots[2 * i : 2 * i + 2], 0) for i in range(len(parts))]
    image_slots = part_slots + part_slots[:1] * (8 - len(part_slots))
    image_slots = jnp.stack(image_slots, 0).reshape(8, images_here, rows).swapaxes(0, 1)

    def place(values):
        return [
            dispatch(part_rows[i], values, experts * size, 4) for i, (_, size) in enumerate(parts)
        ]

    x = jnp.pad(images, pad_rows)
    cot = jnp.pad(cotangent, pad_rows)
    cot_sent = place(cot.reshape(tokens, width))
    cot_there = [exchange(cot_sent[0])]
    mine, cot_there[0], cot_sent[1], x, cot, image_slots = tie(
        mine, cot_there[0], cot_sent[1], x, cot, image_slots
    )
    cot_there.append(exchange(cot_sent[1]))
    packed = join(mine, swap(mine, "replica", 1), core, 1).reshape(width, shard.shape[1])
    small_full = packed[:, 4 * width :]
    lane = jnp.arange(small_width, dtype=jnp.int32)[None, :]
    router = jnp.where(lane < experts, small_full, jnp.zeros_like(small_full))[:, :LANES]
    pick = (lane == experts + jnp.arange(8, dtype=jnp.int32)[:, None]).astype(bf16)
    vec = dot_last(pick, small_full)

    h1, qkv, attended, middle, h2 = attention_forward(x, packed, vec, seq_len)
    sent = place(h2.reshape(tokens, width))
    sent[0], cot_there[1] = tie(sent[0], cot_there[1])
    arrived = [exchange(sent[0])]
    sent[1], arrived[0] = tie(sent[1], arrived[0])
    arrived.append(exchange(sent[1]))

    weights = (expert_in, expert_in_bias, expert_out, expert_out_bias)
    first = expert_chunk(here, arrived[0], cot_there[0], weights, router, experts)
    back_first, arrived[1] = tie(first[0], arrived[1])
    back = [exchange(back_first)]
    second = expert_chunk(here, arrived[1], cot_there[1], weights, router, experts)
    back_second, back[0], *second = tie(second[0], back[0], *second[1:])
    back.append(exchange(back_second))
    gated, hiddens, inners, outers, logits, in_sums, out_sums = zip(first[1:], second)

    core_here = core.reshape(1).astype(jnp.int32)
    out_mine, out_other = out_grad(core_here, hiddens, outers)
    in_mine, in_other, router_grad = in_grad(core_here, arrived, inners, logits)
    back[1], out_mine, out_other, in_mine, in_other = tie(
        back[1], out_mine, out_other, in_mine, in_other
    )
    out_mine = add(out_mine, swap(out_other, "replica", 1))
    in_mine = add(in_mine, swap(in_other, "replica", 1))
    biases = jnp.concatenate([sum(in_sums)[0], sum(out_sums)[0]]).reshape(-1, width).astype(bf16)
    biases = over_chips(add(biases, swap(biases, "replica", 1)))
    out_mine = over_chips(out_mine)
    in_mine, out_mine = tie(in_mine, out_mine)
    in_mine = over_chips(in_mine)

    first_gated, back[1] = tie(gated[0], back[1])
    returned = [exchange(first_gated)]
    input_grad, mine, other = attention_backward(
        core_here,
        image_slots,
        x,
        cot,
        middle,
        qkv,
        packed,
        vec,
        h1,
        attended,
        router_grad,
        back,
        experts,
        seq_len,
    )
    mine, other, returned[0] = tie(mine, other, returned[0])
    mine = add(mine, swap(other, "replica", 1))
    mine, out_mine = tie(mine, out_mine)
    pieces = exchange(mine)
    second_gated, pieces = tie(gated[1], pieces)
    returned.append(exchange(second_gated))
    pieces = pieces.reshape(experts, width // experts, -1)
    mine = jnp.sum(pieces.astype(f32), 0).astype(bf16)
    mine = over_chips(mine)
    summed = join(mine, swap(mine, "replica", 1), core, 1).astype(f32)

    output = combine_output(image_slots, middle, returned)
    expert_out_grad = widen(core_here, out_mine, swap(out_mine, "replica", 1))[None]
    expert_in_grad = widen(core_here, in_mine, swap(in_mine, "replica", 1))[None]
    biases = biases.astype(f32).reshape(1, -1)
    hidden_width = expert_in_bias.shape[1]
    small_sum = summed[:, 4 * width :]
    vector_sums = small_sum[:, experts : experts + VECTORS].T
    return (
        output[:, :seq_len],
        input_grad[:, :seq_len],
        vector_sums[GAIN_ONE],
        vector_sums[SHIFT_ONE],
        summed[:, : 3 * width],
        vector_sums[QUERY_BIAS],
        vector_sums[VALUE_BIAS],
        summed[:, 3 * width : 4 * width],
        vector_sums[OUT_SHIFT],
        vector_sums[GAIN_TWO],
        vector_sums[SHIFT_TWO],
        small_sum[:, :experts],
        expert_in_grad,
        biases[:, :hidden_width],
        expert_out_grad,
        biases[:, hidden_width:],
    )


def solution(mesh):
    return jax.shard_map(
        per_device,
        mesh=mesh,
        in_specs=(
            P(("replica", "shard"), None, None),
            P(("replica", "shard"), None, None),
            P(("replica", "shard"), None, None),
            P("shard"),
            P("shard"),
            P("shard", None),
            P("shard"),
            P("shard"),
            P("shard", None),
            P("shard"),
            P("shard"),
            P("shard"),
            P("shard", None),
            P("shard", None, None),
            P("shard", None),
            P("shard", None, None),
            P("shard", None),
        ),
        out_specs=(
            P(("replica", "shard"), None, None),
            P(("replica", "shard"), None, None),
            P("shard"),
            P("shard"),
            P("shard", None),
            P("shard"),
            P("shard"),
            P("shard", None),
            P("shard"),
            P("shard"),
            P("shard"),
            P("shard", None),
            P("shard", None, None),
            P("shard", None),
            P("shard", None, None),
            P("shard", None),
        ),
        check_vma=False,
    )
```

time: 789 us -> 526 us (0.67)
  Pallas kernels: 0 us -> 223 us
  matrix products: 212 us -> 1.32 us
  waiting for transfers between devices: 349 us -> 180 us
  local copies, waits for them, and re-layouts: 110 us -> 18.9 us
  other arithmetic: 77.6 us -> 26.9 us
  starting transfers between devices: 19.9 us -> 53.3 us
    pallas_call x0 -> x13, Pallas kernels: none -> 223 us  [the longest x2 83.9 us: expert_chunk(): pl.pallas_call(functools.partial(expert_kernel, experts, tiles), grid_spe...]
    dot_general x25 -> x2, matrix products: 212 us -> 1.32 us  [the longest x1 1.05 us: dot_last(): lax.dot_general(left, right, (((1,), (1,)), ((), ())), preferred_element_...]
    all_gather x1, waiting for transfers between devices: 73.4 us -> 1.41 us  [per_device(): mine = lax.all_gather(mine, 'shard', axis=0, tiled=False)]
    convert_element_type x10 -> x1, local copies, waits for them, and re-layouts: 33.5 us -> 0.02 us  [per_device(): jnp.concatenate([sum(in_sums)[0], sum(out_sums)[0]]).reshape(-1, width)]
    all_to_all x4 -> x9, waiting for transfers between devices: 141 us -> 111 us  [exchange(): lax.all_to_all(blocks, 'shard', split_axis=0, concat_axis=0, tiled=True)]
    all_to_all x4 -> x9, starting transfers between devices: 17.5 us -> 46.8 us  [exchange(): lax.all_to_all(blocks, 'shard', split_axis=0, concat_axis=0, tiled=True)]
    psum x1 -> x0, waiting for transfers between devices: 27.9 us -> none  [per_device(): summed = lax.psum(owned, 'replica').astype(f32)]
    reshape x7 -> x1, local copies, waits for them, and re-layouts: 25 us -> 0.09 us  [per_device(): jnp.pad(routes, pad_rows, constant_values=-1).reshape(tokens, 2)]
  transfers between devices with their start and end apart: 13 -> 22, of which waited for: 8 -> 12; matrix products, arithmetic and copies ran while one was open for 30% -> 7% of each run, Pallas kernels for 0% -> 41%
where the time goes in v2:
time: 526 us; the launch traced here: 518 us
  Pallas kernels  223 us (42%)
  waiting for transfers between devices  180 us (34%)
  starting transfers between devices  53.3 us (10%)
  other arithmetic  26.9 us (5%)
  local copies, waits for them, and re-layouts  18.9 us (4%)
  between operations  14.6 us (3%)
    all_to_all x9, waiting for transfers between devices, exchange(): lax.all_to_all(blocks, 'shard', split_axis=0, concat_axis=0, tiled=True)  111 us
    pallas_call x2, Pallas kernels, expert_chunk(): pl.pallas_call(functools.partial(expert_kernel, experts, tiles), grid_spe...  83.9 us
    ppermute x12, waiting for transfers between devices, swap(): return lax.ppermute(value, axis, [(i, i ^ distance) for i in range(count)])  67.6 us
    all_to_all x9, starting transfers between devices, exchange(): lax.all_to_all(blocks, 'shard', split_axis=0, concat_axis=0, tiled=True)  46.8 us
    pallas_call x1, Pallas kernels, attention_backward(): pl.pallas_call(functools.partial(backward_kernel, seq_len, width, experts...  42.7 us
    pallas_call x4, Pallas kernels, dispatch(): pl.pallas_call(dispatch_kernel, in_specs=[whole(slots.shape), whole(rows....  19.1 us
    pallas_call x1, Pallas kernels, out_grad(): pl.pallas_call(functools.partial(out_grad_kernel, parts), grid_spec=pltpu...  19.1 us
    pallas_call x1, Pallas kernels, in_grad(): pl.pallas_call(functools.partial(in_grad_kernel, parts), grid_spec=pltpu....  18.1 us
  transfers between devices with their start and end apart: 22, of which 12 were waited for; matrix products, arithmetic and copies ran while one was open for 7% of the time, Pallas kernels for 41%

profile of v2, /device:TPU:0, one launch (start us, length us, event | category | flops | bytes accessed | tf_op | source)
XLA Modules:
  0.0 518.5 jit_solution(15834993794510276178)
XLA Ops:
  7.2 1.5 concatenate.17
  8.8 1.7 fusion.3
  10.6 0.7 copy.56
  11.4 1.4 copy.50
  12.8 1.1 pad.17.refs_2_
  14.3 0.6 pad_add_fusion.slot_ref
  14.9 4.8 dispatch.4
  19.7 7.4 %all-to-all-start = ((bf16[8,144,768]{2,1,0:T(8,128)(2,1)}), bf16[8,144,768]{2,1,0:T(8,128)(2,1)S(1)}, u32[]{:S(2)}, u32[]{:S(2)}) async-start(bf16[8,144,768]{2,1,0:T(8,128)(2,1)} %bitcast.59), calls=%async_computation | async-start | bytes 3538944 | tf_op jit(solution)/shard_map/all_to_all | solution.py:646
  27.6 1.2 pad.18.x_ref.refs_1_
  28.8 0.7 stack.63
  30.1 4.7 dispatch.5
  34.8 58.1 %all-to-all-done = bf16[8,144,768]{2,1,0:T(8,128)(2,1)S(1)} async-done(((bf16[8,144,768]{2,1,0:T(8,128)(2,1)}), bf16[8,144,768]{2,1,0:T(8,128)(2,1)S(1)}, u32[]{:S(2)}, u32[]{:S(2)}) %all-to-all-start) | async-done | bytes 1769504 | tf_op jit(solution)/shard_map/all_to_all | solution.py:646
  92.9 1.4 all-gather.3.cloned.1.call-done
  94.3 3.6 all-to-all-start.1
  97.9 1.4 collective-permute-done
  99.3 2.9 broadcast_select_fusion.1
  102.5 1.0 fusion.5.vec_ref.refs_6_
  103.6 1.1 copy-done
  104.7 16.5 %attention_forward.1 = (bf16[4,208,768]{2,1,0:T(8,128)(2,1)}, bf16[4,208,2304]{2,1,0:T(8,128)(2,1)}, bf16[4,208,768]{2,1,0:T(8,128)(2,1)}, f32[4,208,768]{2,1,0:T(8,128)}, bf16[4,208,768]{2,1,0:T(8,128)(2,1)}) custom-call(bf16[4,208,768]{2,1,0:T(8,128)(2,1)} %pad.18.x_ref.refs_1_, bf16[768,3200]{1,0:T(8,128)(2,1)} %bitcast.45, f32[8,768]{1,0:T(8,128)} %fusion.5.vec_ref.refs_6_), custom_call_target="tpu_custom_call" | custom-call | flops 1048576 | bytes 65536 | tf_op jit(solution)/shard_map/attention_forward/pallas_call | solution.py:125
  121.3 4.8 dispatch.7
  126.1 11.8 %all-to-all-done.1 = bf16[8,136,768]{2,1,0:T(8,128)(2,1)S(1)} async-done(((bf16[8,136,768]{2,1,0:T(8,128)(2,1)}), bf16[8,136,768]{2,1,0:T(8,128)(2,1)S(1)}, u32[]{:S(2)}, u32[]{:S(2)}) %all-to-all-start.1) | async-done | bytes 1671200 | tf_op jit(solution)/shard_map/all_to_all | solution.py:646
  137.9 1.2 copy-done.5
  139.0 3.6 all-to-all-start.2
  142.7 4.8 dispatch.6
  147.4 36.7 %all-to-all-done.2 = bf16[8,144,768]{2,1,0:T(8,128)(2,1)S(1)} async-done(((bf16[8,144,768]{2,1,0:T(8,128)(2,1)}), bf16[8,144,768]{2,1,0:T(8,128)(2,1)S(1)}, u32[]{:S(2)}, u32[]{:S(2)}) %all-to-all-start.2) | async-done | bytes 1769504 | tf_op jit(solution)/shard_map/all_to_all | solution.py:646
  184.1 3.9 all-to-all-start.3
  188.0 1.6 broadcast_select_fusion.4.router_ref
  189.6 42.9 %expert_chunk.2 = (bf16[1152,768]{1,0:T(8,128)(2,1)}, bf16[1152,768]{1,0:T(8,128)(2,1)}, bf16[1152,3072]{1,0:T(8,128)(2,1)}, bf16[1152,3072]{1,0:T(8,128)(2,1)},...) custom-call(s32[1]{0:T(128)} %bitcast.20.here_ref, ...), custom_call_target="tpu_custom_call" | custom-call | flops 1048576 | bytes 65536 | tf_op jit(solution)/shard_map/expert_chunk/pallas_call | solution.py:268
  232.6 6.4 %all-to-all-start.4 = ((bf16[8,144,768]{2,1,0:T(8,128)(2,1)}), bf16[8,144,768]{2,1,0:T(8,128)(2,1)S(1)}, u32[]{:S(2)}, u32[]{:S(2)}) async-start(bf16[8,144,768]{2,1,0:T(8,128)(2,1)} %bitcast.69), calls=%async_computation.4 | async-start | bytes 3538944 | tf_op jit(solution)/shard_map/all_to_all | solution.py:646
  239.0 40.9 %expert_chunk.3 = (bf16[1088,768]{1,0:T(8,128)(2,1)}, bf16[1088,768]{1,0:T(8,128)(2,1)}, bf16[1088,3072]{1,0:T(8,128)(2,1)}, bf16[1088,3072]{1,0:T(8,128)(2,1)},...) custom-call(s32[1]{0:T(128)} %bitcast.20.here_ref, ...), custom_call_target="tpu_custom_call" | custom-call | flops 1048576 | bytes 65536 | tf_op jit(solution)/shard_map/expert_chunk/pallas_call | solution.py:268
  280.0 6.0 %all-to-all-start.5 = ((bf16[8,136,768]{2,1,0:T(8,128)(2,1)}), bf16[8,136,768]{2,1,0:T(8,128)(2,1)S(1)}, u32[]{:S(2)}, u32[]{:S(2)}) async-start(bf16[8,136,768]{2,1,0:T(8,128)(2,1)} %bitcast.71), calls=%async_computation.5 | async-start | bytes 3342336 | tf_op jit(solution)/shard_map/all_to_all | solution.py:646
  286.0 19.1 %out_grad.1 = (bf16[1536,768]{1,0:T(8,128)(2,1)}, bf16[1536,768]{1,0:T(8,128)(2,1)}) custom-call(s32[1]{0:T(128)} %bitcast.14.core_ref, bf16[1152,3072]{1,0:T(8,128)(2,1)} %get-tuple-element.116.refs_0_, bf16[1088,3072]{1,0:T(8,128)(2,1)} %get-tuple-element.117.refs_1_, bf16[1152,768]{1,0:T(8,128)(2,1)} %get-tuple-element.118.refs_2_, ...), custom_call_target="tpu_custom_call" | custom-call | flops 1048576 | bytes 65536 | tf_op jit(solution)/shard_map/out_grad/pallas_call | solution.py:346
  305.1 18.1 %in_grad.1 = (bf16[384,3072]{1,0:T(8,128)(2,1)}, bf16[384,3072]{1,0:T(8,128)(2,1)}, f32[768,128]{1,0:T(8,128)}) custom-call(s32[1]{0:T(128)} %bitcast.14.core_ref, bf16[1152,768]{1,0:T(8,128)(2,1)} %bitcast.51, bf16[1088,768]{1,0:T(8,128)(2,1)} %bitcast.53, bf16[1152,3072]{1,0:T(8,128)(2,1)} %get-tuple-element.98.refs_2_, ...), custom_call_target="tpu_custom_call" | custom-call | flops 1048576 | bytes 65536 | tf_op jit(solution)/shard_map/in_grad/pallas_call | solution.py:397
  323.2 1.0 all-to-all-done.5
  324.2 5.1 all-to-all-start.6
  329.5 3.0 add_convert_fusion.3
  332.5 1.5 collective-permute-start.4
  334.0 42.7 %attention_backward.1 = (bf16[4,208,768]{2,1,0:T(8,128)(2,1)}, bf16[768,1664]{1,0:T(8,128)(2,1)}, bf16[768,1664]{1,0:T(8,128)(2,1)}) custom-call(s32[1]{0:T(128)} %bitcast.14.core_ref, s32[4,8,208]{2,1,0:T(8,128)} %bitcast.72, bf16[4,208,768]{2,1,0:T(8,128)(2,1)} %pad.18.x_ref.refs_1_, bf16[4,208,768]{2,1,0:T(8,128)(2,1)} %pad.17.refs_2_, ...), custom_call_target="tpu_custom_call" | custom-call | flops 1048576 | bytes 65536 | tf_op jit(solution)/shard_map/attention_backward/pallas_call | solution.py:608
  376.8 4.7 add_convert_fusion.4
  381.5 4.6 collective-permute-done.4
  386.1 3.7 add_convert_fusion.2.mine_ref
  389.8 2.1 add_convert_fusion
  391.9 6.0 %all-to-all-start.7 = ((bf16[8,96,1664]{2,1,0:T(8,128)(2,1)}), bf16[8,96,1664]{2,1,0:T(8,128)(2,1)S(1)}, u32[]{:S(2)}, u32[]{:S(2)}) async-start(bf16[8,96,1664]{2,1,0:T(8,128)(2,1)} %bitcast.54), calls=%async_computation.7 | async-start | bytes 5111808 | tf_op jit(solution)/shard_map/all_to_all | solution.py:646
  397.9 1.4 collective-permute-start.7
  399.4 51.4 %collective-permute-done.7 = bf16[384,3072]{1,0:T(8,128)(2,1)S(1)} collective-permute-done((bf16[384,3072]{1,0:T(8,128)(2,1)}, bf16[384,3072]{1,0:T(8,128)(2,1)S(1)}, u32[]{:S(2)}, u32[]{:S(2)}) %collective-permute-start.7) | collective-permute-done | bytes 2359328 | tf_op jit(solution)/shard_map/ppermute | solution.py:640
  450.7 4.0 add_convert_fusion.1.mine_ref
  454.7 1.2 all-to-all-done.7
  455.9 4.7 all-to-all-start.8
  461.1 1.5 collective-permute-start.5
  462.8 8.0 %collective-permute-done.5 = bf16[96,1664]{1,0:T(8,128)(2,1)S(1)} collective-permute-done((bf16[96,1664]{1,0:T(8,128)(2,1)S(1)}, bf16[96,1664]{1,0:T(8,128)(2,1)S(1)}, u32[]{:S(2)}, u32[]{:S(2)}) %collective-permute-start.5) | collective-permute-done | bytes 319520 | tf_op jit(solution)/shard_map/ppermute | solution.py:640
  471.0 1.5 collective-permute-start.10
  472.5 2.3 collective-permute-done.10
  475.9 1.4 slice.68
  477.3 1.5 copy.53
  478.8 7.9 %widen.3 = f32[3072,768]{1,0:T(8,128)} custom-call(s32[1]{0:T(128)} %bitcast.14.core_ref, bf16[1536,768]{1,0:T(8,128)(2,1)} %add_convert_fusion.2.mine_ref, bf16[1536,768]{1,0:T(8,128)(2,1)} %collective-permute-done.11.theirs_ref), custom_call_target="tpu_custom_call" | custom-call | flops 1048576 | bytes 65536 | tf_op jit(solution)/shard_map/widen/pallas_call | solution.py:439
  486.7 7.9 %widen.2 = f32[768,3072]{1,0:T(8,128)} custom-call(s32[1]{0:T(128)} %bitcast.14.core_ref, bf16[384,3072]{1,0:T(8,128)(2,1)} %add_convert_fusion.1.mine_ref, bf16[384,3072]{1,0:T(8,128)(2,1)} %collective-permute-done.8.theirs_ref), custom_call_target="tpu_custom_call" | custom-call | flops 1048576 | bytes 65536 | tf_op jit(solution)/shard_map/widen/pallas_call | solution.py:439
  494.6 0.7 copy.54
  495.4 1.0 slice.88
  496.4 0.9 slice_reduce_fusion
  497.3 0.7 maximum_convert_fusion.1
  498.0 2.5 all-to-all-done.8
  500.5 8.2 %combine_output.1 = bf16[4,208,768]{2,1,0:T(8,128)(2,1)} custom-call(s32[4,8,208]{2,1,0:T(8,128)} %bitcast.73, f32[4,208,768]{2,1,0:T(8,128)} %get-tuple-element.85.refs_3_.mid_ref, bf16[1152,768]{1,0:T(8,128)(2,1)} %bitcast.28.refs_0_, bf16[1088,768]{1,0:T(8,128)(2,1)} %bitcast.32.refs_1_), custom_call_target="tpu_custom_call" | custom-call | flops 1048576 | bytes 65536 | tf_op jit(solution)/shard_map/combine_output/pallas_call | solution.py:474
  508.6 1.3 slice-done
  509.9 1.5 copy.52
  (75 shorter events, 4.7 us)
Async XLA Ops:
  7.2 87.1 %all-gather.3.cloned.1.call-start = ((), (), s32[]{:S(2)}) async-start(), calls=%async_computation.9 | async-start | bytes 2764800 | tf_op jit(solution)/shard_map/all_gather | solution.py:715
  19.7 7.7 %copy-start.8 = (bf16[4,197,768]{2,0,1:T(4,128)(2,1)S(1)}, bf16[4,197,768]{2,0,1:T(4,128)(2,1)}, u32[]{:S(2)}) copy-start(bf16[4,197,768]{2,0,1:T(4,128)(2,1)} %param.17) | copy-start | bytes 3631108
  19.7 73.1 %all-to-all-start = ((bf16[8,144,768]{2,1,0:T(8,128)(2,1)}), bf16[8,144,768]{2,1,0:T(8,128)(2,1)S(1)}, u32[]{:S(2)}, u32[]{:S(2)}) async-start(bf16[8,144,768]{2,1,0:T(8,128)(2,1)} %bitcast.59), calls=%async_computation | async-start | bytes 3538944 | tf_op jit(solution)/shard_map/all_to_all | solution.py:646
  92.9 9.3 %copy-start.4 = (bf16[8,144,768]{2,1,0:T(8,128)(2,1)}, bf16[8,144,768]{2,1,0:T(8,128)(2,1)S(1)}, u32[]{:S(2)}) copy-start(bf16[8,144,768]{2,1,0:T(8,128)(2,1)S(1)} %all-to-all-done) | copy-start | bytes 5308420
  94.3 5.0 collective-permute-start
  94.3 43.5 %all-to-all-start.1 = ((bf16[8,136,768]{2,1,0:T(8,128)(2,1)}), bf16[8,136,768]{2,1,0:T(8,128)(2,1)S(1)}, u32[]{:S(2)}, u32[]{:S(2)}) async-start(bf16[8,136,768]{2,1,0:T(8,128)(2,1)} %bitcast.63), calls=%async_computation.1 | async-start | bytes 3342336 | tf_op jit(solution)/shard_map/all_to_all | solution.py:646
  102.5 2.2 copy-start
  137.8 1.2 copy-start.5
  139.0 45.1 %all-to-all-start.2 = ((bf16[8,144,768]{2,1,0:T(8,128)(2,1)}), bf16[8,144,768]{2,1,0:T(8,128)(2,1)S(1)}, u32[]{:S(2)}, u32[]{:S(2)}) async-start(bf16[8,144,768]{2,1,0:T(8,128)(2,1)} %bitcast.60), calls=%async_computation.2 | async-start | bytes 3538944 | tf_op jit(solution)/shard_map/all_to_all | solution.py:646
  184.1 5.5 %copy-start.1 = (bf16[8,144,768]{2,1,0:T(8,128)(2,1)}, bf16[8,144,768]{2,1,0:T(8,128)(2,1)S(1)}, u32[]{:S(2)}) copy-start(bf16[8,144,768]{2,1,0:T(8,128)(2,1)S(1)} %all-to-all-done.2) | copy-start | bytes 5308420
  184.1 48.5 %all-to-all-start.3 = ((bf16[8,136,768]{2,1,0:T(8,128)(2,1)}), bf16[8,136,768]{2,1,0:T(8,128)(2,1)S(1)}, u32[]{:S(2)}, u32[]{:S(2)}) async-start(bf16[8,136,768]{2,1,0:T(8,128)(2,1)} %bitcast.64), calls=%async_computation.3 | async-start | bytes 3342336 | tf_op jit(solution)/shard_map/all_to_all | solution.py:646
  232.6 6.5 %copy-start.2 = (bf16[8,136,768]{2,1,0:T(8,128)(2,1)}, bf16[8,136,768]{2,1,0:T(8,128)(2,1)S(1)}, u32[]{:S(2)}) copy-start(bf16[8,136,768]{2,1,0:T(8,128)(2,1)S(1)} %all-to-all-done.3) | copy-start | bytes 5013508
  232.6 47.4 %all-to-all-start.4 = ((bf16[8,144,768]{2,1,0:T(8,128)(2,1)}), bf16[8,144,768]{2,1,0:T(8,128)(2,1)S(1)}, u32[]{:S(2)}, u32[]{:S(2)}) async-start(bf16[8,144,768]{2,1,0:T(8,128)(2,1)} %bitcast.69), calls=%async_computation.4 | async-start | bytes 3538944 | tf_op jit(solution)/shard_map/all_to_all | solution.py:646
  280.0 25.1 %copy-start.3 = (bf16[8,144,768]{2,1,0:T(8,128)(2,1)}, bf16[8,144,768]{2,1,0:T(8,128)(2,1)S(1)}, u32[]{:S(2)}) copy-start(bf16[8,144,768]{2,1,0:T(8,128)(2,1)S(1)} %all-to-all-done.4) | copy-start | bytes 5308420
  280.0 44.2 %all-to-all-start.5 = ((bf16[8,136,768]{2,1,0:T(8,128)(2,1)}), bf16[8,136,768]{2,1,0:T(8,128)(2,1)S(1)}, u32[]{:S(2)}, u32[]{:S(2)}) async-start(bf16[8,136,768]{2,1,0:T(8,128)(2,1)} %bitcast.71), calls=%async_computation.5 | async-start | bytes 3342336 | tf_op jit(solution)/shard_map/all_to_all | solution.py:646
  324.2 5.3 %copy-start.6 = (bf16[8,136,768]{2,1,0:T(8,128)(2,1)}, bf16[8,136,768]{2,1,0:T(8,128)(2,1)S(1)}, u32[]{:S(2)}) copy-start(bf16[8,136,768]{2,1,0:T(8,128)(2,1)S(1)} %all-to-all-done.5) | copy-start | bytes 5013508
  324.2 5.3 %collective-permute-start.3 = (bf16[1536,768]{1,0:T(8,128)(2,1)}, bf16[1536,768]{1,0:T(8,128)(2,1)}, u32[]{:S(2)}, u32[]{:S(2)}) collective-permute-start(bf16[1536,768]{1,0:T(8,128)(2,1)} %get-tuple-element.136), channel_id=1, source_target_pairs={{0,8},{8,0},{16,24},{24,16},{1,9},{9,1},{17,25},{25,17},{2,10},{10... | collective-permute-start | bytes 7077896 | tf_op jit(solution)/shard_map/ppermute | solution.py:640
  324.2 52.5 %all-to-all-start.6 = ((bf16[8,144,768]{2,1,0:T(8,128)(2,1)}), bf16[8,144,768]{2,1,0:T(8,128)(2,1)}, u32[]{:S(2)}, u32[]{:S(2)}) async-start(bf16[8,144,768]{2,1,0:T(8,128)(2,1)} %bitcast.27), calls=%async_computation.6 | async-start | bytes 3538944 | tf_op jit(solution)/shard_map/all_to_all | solution.py:646
  329.3 47.5 %collective-permute-start.2 = (bf16[384,3072]{1,0:T(8,128)(2,1)}, bf16[384,3072]{1,0:T(8,128)(2,1)}, u32[]{:S(2)}, u32[]{:S(2)}) collective-permute-start(bf16[384,3072]{1,0:T(8,128)(2,1)} %get-tuple-element.134), channel_id=1, source_target_pairs={{0,8},{8,0},{16,24},{24,16},{1,9},{9,1},{17,25},{25,17},{2,10},{10... | collective-permute-start | bytes 7077896 | tf_op jit(solution)/shard_map/ppermute | solution.py:640
  332.5 53.6 %collective-permute-start.4 = (bf16[1536,768]{1,0:T(8,128)(2,1)S(1)}, bf16[1536,768]{1,0:T(8,128)(2,1)}, u32[]{:S(2)}, u32[]{:S(2)}) collective-permute-start(bf16[1536,768]{1,0:T(8,128)(2,1)S(1)} %add_convert_fusion.3), channel_id=1, source_target_pairs={{0,16},{8,24},{16,0},{24,8},{1,17},{9,25},{17,1},{25,9},{2,18},{10... | collective-permute-start | bytes 7077896 | tf_op jit(solution)/shard_map/ppermute | solution.py:640
  376.7 13.1 %collective-permute-start.1 = (bf16[768,1664]{1,0:T(8,128)(2,1)}, bf16[768,1664]{1,0:T(8,128)(2,1)S(1)}, u32[]{:S(2)}, u32[]{:S(2)}) collective-permute-start(bf16[768,1664]{1,0:T(8,128)(2,1)} %get-tuple-element.132), channel_id=1, source_target_pairs={{0,8},{8,0},{16,24},{24,16},{1,9},{9,1},{17,25},{25,17},{2,10},{10... | collective-permute-start | bytes 7667720 | tf_op jit(solution)/shard_map/ppermute | solution.py:640
  381.5 8.3 %copy-start.7 = (bf16[768,1664]{1,0:T(8,128)(2,1)S(1)}, bf16[768,1664]{1,0:T(8,128)(2,1)}, u32[]{:S(2)}) copy-start(bf16[768,1664]{1,0:T(8,128)(2,1)} %get-tuple-element.131) | copy-start | bytes 7667716
  391.9 63.9 %all-to-all-start.7 = ((bf16[8,96,1664]{2,1,0:T(8,128)(2,1)}), bf16[8,96,1664]{2,1,0:T(8,128)(2,1)S(1)}, u32[]{:S(2)}, u32[]{:S(2)}) async-start(bf16[8,96,1664]{2,1,0:T(8,128)(2,1)} %bitcast.54), calls=%async_computation.7 | async-start | bytes 5111808 | tf_op jit(solution)/shard_map/all_to_all | solution.py:646
  397.9 52.8 %collective-permute-start.7 = (bf16[384,3072]{1,0:T(8,128)(2,1)}, bf16[384,3072]{1,0:T(8,128)(2,1)S(1)}, u32[]{:S(2)}, u32[]{:S(2)}) collective-permute-start(bf16[384,3072]{1,0:T(8,128)(2,1)} %add_convert_fusion.4), channel_id=1, source_target_pairs={{0,16},{8,24},{16,0},{24,8},{1,17},{9,25},{17,1},{25,9},{2,18},{10... | collective-permute-start | bytes 7077896 | tf_op jit(solution)/shard_map/ppermute | solution.py:640
  399.4 79.4 %collective-permute-start.11 = (bf16[1536,768]{1,0:T(8,128)(2,1)}, bf16[1536,768]{1,0:T(8,128)(2,1)}, u32[]{:S(2)}, u32[]{:S(2)}) collective-permute-start(bf16[1536,768]{1,0:T(8,128)(2,1)} %add_convert_fusion.2.mine_ref), channel_id=1, source_target_pairs={{0,8},{8,0},{16,24},{24,16},{1,9},{9,1},{17,25},{25,17},{2,10},{10... | collective-permute-start | bytes 7077896 | tf_op jit(solution)/shard_map/ppermute | solution.py:640
  454.7 32.0 %collective-permute-start.8 = (bf16[384,3072]{1,0:T(8,128)(2,1)}, bf16[384,3072]{1,0:T(8,128)(2,1)}, u32[]{:S(2)}, u32[]{:S(2)}) collective-permute-start(bf16[384,3072]{1,0:T(8,128)(2,1)} %add_convert_fusion.1.mine_ref), channel_id=1, source_target_pairs={{0,8},{8,0},{16,24},{24,16},{1,9},{9,1},{17,25},{25,17},{2,10},{10... | collective-permute-start | bytes 7077896 | tf_op jit(solution)/shard_map/ppermute | solution.py:640
  455.9 6.7 %copy-start.11 = (f32[1,768]{1,0:T(1,128)S(1)}, f32[1,768]{1,0:T(1,128)}, u32[]{:S(2)}) copy-start(f32[1,768]{1,0:T(1,128)} %get-tuple-element.145) | copy-start | bytes 9220
  455.9 6.7 %copy-start.12 = (f32[1,768]{1,0:T(1,128)S(1)}, f32[1,768]{1,0:T(1,128)}, u32[]{:S(2)}) copy-start(f32[1,768]{1,0:T(1,128)} %get-tuple-element.146) | copy-start | bytes 9220
  455.9 6.7 %copy-start.9 = (f32[1,3072]{1,0:T(1,128)S(1)}, f32[1,3072]{1,0:T(1,128)}, u32[]{:S(2)}) copy-start(f32[1,3072]{1,0:T(1,128)} %get-tuple-element.143) | copy-start | bytes 36868
  455.9 6.7 %copy-start.10 = (f32[1,3072]{1,0:T(1,128)S(1)}, f32[1,3072]{1,0:T(1,128)}, u32[]{:S(2)}) copy-start(f32[1,3072]{1,0:T(1,128)} %get-tuple-element.144) | copy-start | bytes 36868
  455.9 44.6 %all-to-all-start.8 = ((bf16[8,136,768]{2,1,0:T(8,128)(2,1)}), bf16[8,136,768]{2,1,0:T(8,128)(2,1)}, u32[]{:S(2)}, u32[]{:S(2)}) async-start(bf16[8,136,768]{2,1,0:T(8,128)(2,1)} %bitcast.70), calls=%async_computation.8 | async-start | bytes 3342336 | tf_op jit(solution)/shard_map/all_to_all | solution.py:646
  461.1 9.7 %collective-permute-start.5 = (bf16[96,1664]{1,0:T(8,128)(2,1)S(1)}, bf16[96,1664]{1,0:T(8,128)(2,1)S(1)}, u32[]{:S(2)}, u32[]{:S(2)}) collective-permute-start(bf16[96,1664]{1,0:T(8,128)(2,1)S(1)} %reduce_sum.38), channel_id=1, source_target_pairs={{0,16},{8,24},{16,0},{24,8},{1,17},{9,25},{17,1},{25,9},{2,18},{10... | collective-permute-start | bytes 958472 | tf_op jit(solution)/shard_map/ppermute | solution.py:640
  462.7 8.2 %collective-permute-start.9 = (bf16[5,768]{1,0:T(8,128)(2,1)S(1)}, bf16[5,768]{1,0:T(8,128)(2,1)S(1)}, u32[]{:S(2)}, u32[]{:S(2)}) collective-permute-start(bf16[5,768]{1,0:T(8,128)(2,1)S(1)} %convert_element_type.113), channel_id=1, source_target_pairs={{0,8},{8,0},{16,24},{24,16},{1,9},{9,1},{17,25},{25,17},{2,10},{10... | collective-permute-start | bytes 23048 | tf_op jit(solution)/shard_map/ppermute | solution.py:640
  470.9 23.7 %collective-permute-start.6 = (bf16[96,1664]{1,0:T(8,128)(2,1)S(1)}, bf16[96,1664]{1,0:T(8,128)(2,1)S(1)}, u32[]{:S(2)}, u32[]{:S(2)}) collective-permute-start(bf16[96,1664]{1,0:T(8,128)(2,1)S(1)} %add_convert_fusion.5), channel_id=1, source_target_pairs={{0,8},{8,0},{16,24},{24,16},{1,9},{9,1},{17,25},{25,17},{2,10},{10... | collective-permute-start | bytes 958472 | tf_op jit(solution)/shard_map/ppermute | solution.py:640
  471.0 3.8 collective-permute-start.10
  508.6 1.3 slice-start
Sparse Core Ops, SparseCore 0:
  10.8 83.4 all-gather.2

commit v3 on v2

--- a/solution.py
+++ b/solution.py
@@ -185,20 +185,22 @@
     total_ref,
 ):
     phase, tile = pl.program_id(0), pl.program_id(1)
+    high = rows_ref.shape[0] // 4
+    blocks = [slice(i * high, (i + 1) * high) for i in range(4)]
 
     @pl.when(phase == 0)
     def _():
-        act = dot(rows_ref[...], in_ref[0]) + in_bias_ref[...].astype(f32)
-        square = act * act
         slant = 0.7978845608028654
-        bend = jnp.tanh(act * (slant + (slant * 0.044715) * square))
-        half = 0.5 + 0.5 * bend
-        hidden = (act * half).astype(bf16)
-        hidden_ref[...] = hidden
-        slope_ref[tile] = half + (0.5 * act) * (1.0 - bend * bend) * (
-            slant + (3.0 * slant * 0.044715) * square
-        )
-        part = dot(hidden, out_ref[0])
+        for block in blocks:
+            act = dot(rows_ref[block, :], in_ref[0]) + in_bias_ref[...].astype(f32)
+            square = act * act
+            bend = jnp.tanh(act * (slant + (slant * 0.044715) * square))
+            half = 0.5 + 0.5 * bend
+            hidden_ref[block, :] = (act * half).astype(bf16)
+            slope_ref[tile, block, :] = half + (0.5 * act) * (1.0 - bend * bend) * (
+                slant + (3.0 * slant * 0.044715) * square
+            )
+        part = dot(hidden_ref[...], out_ref[0])
 
         @pl.when(tile == 0)
         def _():
@@ -228,11 +230,15 @@
 
     @pl.when(phase == 1)
     def _():
-        hidden_grad = dot_last(outer_ref[...], out_ref[0])
-        inner = (hidden_grad * slope_ref[tile]).astype(bf16)
-        inner_ref[...] = inner
-        in_sum_ref[...] = jnp.sum(inner.astype(f32), 0, keepdims=True)
-        part = dot_last(inner, in_ref[0])
+        in_sum = None
+        for block in blocks:
+            hidden_grad = dot_last(outer_ref[block, :], out_ref[0])
+            inner = (hidden_grad * slope_ref[tile, block, :]).astype(bf16)
+            inner_ref[block, :] = inner
+            block_sum = jnp.sum(inner.astype(f32), 0, keepdims=True)
+            in_sum = block_sum if in_sum is None else in_sum + block_sum
+        in_sum_ref[...] = in_sum
+        part = dot_last(inner_ref[...], in_ref[0])
 
         @pl.when(tile == 0)
         def _():
@@ -664,8 +670,7 @@
     return jnp.concatenate([first, second], axis)
 
 
-def over_chips(value):
-    step = 2
+def over_chips(value, step=2):
     while step < lax.axis_size("replica"):
         value = add(value, swap(value, "replica", step))
         step *= 2
@@ -784,9 +789,7 @@
     in_mine = add(in_mine, swap(in_other, "replica", 1))
     biases = jnp.concatenate([sum(in_sums)[0], sum(out_sums)[0]]).reshape(-1, width).astype(bf16)
     biases = over_chips(add(biases, swap(biases, "replica", 1)))
-    out_mine = over_chips(out_mine)
-    in_mine, out_mine = tie(in_mine, out_mine)
-    in_mine = over_chips(in_mine)
+    out_theirs = swap(out_mine, "replica", 2)
 
     first_gated, back[1] = tie(gated[0], back[1])
     returned = [exchange(first_gated)]
@@ -806,19 +809,26 @@
         experts,
         seq_len,
     )
-    mine, other, returned[0] = tie(mine, other, returned[0])
-    mine = add(mine, swap(other, "replica", 1))
-    mine, out_mine = tie(mine, out_mine)
-    pieces = exchange(mine)
-    second_gated, pieces = tie(gated[1], pieces)
+    mine, other, returned[0], out_theirs = tie(mine, other, returned[0], out_theirs)
+    second_gated, returned[0] = tie(gated[1], returned[0])
     returned.append(exchange(second_gated))
-    pieces = pieces.reshape(experts, width // experts, -1)
-    mine = jnp.sum(pieces.astype(f32), 0).astype(bf16)
-    mine = over_chips(mine)
-    summed = join(mine, swap(mine, "replica", 1), core, 1).astype(f32)
-
+    mine = add(mine, swap(other, "replica", 1)).reshape(experts, width // experts, -1)
+    chip = lax.axis_index("replica") // 2 % 2
+    mine, other = halves(mine, chip, 1)
+    mine = add(mine, swap(other, "replica", 2))
+    out_mine = over_chips(add(out_mine, out_theirs), 4)
+    in_mine, mine = tie(in_mine, mine)
+    in_mine = over_chips(in_mine)
+    mine, returned[1] = tie(mine, returned[1])
+    pieces = lax.all_to_all(mine, "shard", split_axis=0, concat_axis=0, tiled=True)
     output = combine_output(image_slots, middle, returned)
     expert_out_grad = widen(core_here, out_mine, swap(out_mine, "replica", 1))[None]
+    pieces, output, expert_out_grad = tie(pieces, output, expert_out_grad)
+    mine = jnp.sum(pieces.astype(f32), 0).astype(bf16)
+    mine = over_chips(mine, 4)
+    mine = join(mine, swap(mine, "replica", 2), chip, 0)
+    summed = join(mine, swap(mine, "replica", 1), core, 1).astype(f32)
+
     expert_in_grad = widen(core_here, in_mine, swap(in_mine, "replica", 1))[None]
     biases = biases.astype(f32).reshape(1, -1)
     hidden_width = expert_in_bias.shape[1]

time: 526 us -> 517 us (0.983)
  waiting for transfers between devices: 180 us -> 174 us
    ppermute x12 -> x13, waiting for transfers between devices: 67.6 us -> 46.4 us  [swap(): return lax.ppermute(value, axis, [(i, i ^ distance) for i in range(count)])]
    all_to_all x0 -> x1, waiting for transfers between devices: none -> 14.6 us  [per_device(): lax.all_to_all(mine, 'shard', split_axis=0, concat_axis=0, tiled=True)]
    all_to_all x9 -> x8, starting transfers between devices: 46.8 us -> 42 us  [exchange(): lax.all_to_all(blocks, 'shard', split_axis=0, concat_axis=0, tiled=True)]
    all_to_all x9 -> x8, waiting for transfers between devices: 111 us -> 111 us  [exchange(): lax.all_to_all(blocks, 'shard', split_axis=0, concat_axis=0, tiled=True)]
  transfers between devices with their start and end apart: 22 -> 23, of which waited for: 12 -> 13; matrix products, arithmetic and copies ran while one was open for 7% -> 8% of each run, Pallas kernels for 41% -> 42%
where the time goes in v3:
time: 517 us; the launch traced here: 510 us
  Pallas kernels  223 us (43%)
  waiting for transfers between devices  174 us (34%)
  starting transfers between devices  54.7 us (11%)
  other arithmetic  27.7 us (5%)
  local copies, waits for them, and re-layouts  15.3 us (3%)
  between operations  14.7 us (3%)
    all_to_all x8, waiting for transfers between devices, exchange(): lax.all_to_all(blocks, 'shard', split_axis=0, concat_axis=0, tiled=True)  111 us
    pallas_call x2, Pallas kernels, expert_chunk(): pl.pallas_call(functools.partial(expert_kernel, experts, tiles), grid_spe...  83.3 us
    ppermute x13, waiting for transfers between devices, swap(): return lax.ppermute(value, axis, [(i, i ^ distance) for i in range(count)])  46.4 us
    pallas_call x1, Pallas kernels, attention_backward(): pl.pallas_call(functools.partial(backward_kernel, seq_len, width, experts...  42.5 us
    all_to_all x8, starting transfers between devices, exchange(): lax.all_to_all(blocks, 'shard', split_axis=0, concat_axis=0, tiled=True)  42 us
    pallas_call x4, Pallas kernels, dispatch(): pl.pallas_call(dispatch_kernel, in_specs=[whole(slots.shape), whole(rows....  19.1 us
    pallas_call x1, Pallas kernels, out_grad(): pl.pallas_call(functools.partial(out_grad_kernel, parts), grid_spec=pltpu...  19.1 us
    convert_element_type x7, other arithmetic, add(): return (left.astype(f32) + right.astype(f32)).astype(bf16)  18.4 us
  transfers between devices with their start and end apart: 23, of which 13 were waited for; matrix products, arithmetic and copies ran while one was open for 8% of the time, Pallas kernels for 42%

profile of v3, /device:TPU:0, one launch (start us, length us, event | category | flops | bytes accessed | tf_op | source)
XLA Modules:
  0.0 509.8 jit_solution(9438445238973550530)
XLA Ops:
  7.2 1.5 concatenate.20
  8.8 1.7 fusion.3
  10.6 0.7 copy.55
  11.4 1.4 copy.50
  12.8 1.1 pad.17.refs_2_
  14.3 0.6 pad_add_fusion.1.slot_ref
  14.9 4.8 dispatch.4
  19.8 7.4 %all-to-all-start = ((bf16[8,144,768]{2,1,0:T(8,128)(2,1)}), bf16[8,144,768]{2,1,0:T(8,128)(2,1)S(1)}, u32[]{:S(2)}, u32[]{:S(2)}) async-start(bf16[8,144,768]{2,1,0:T(8,128)(2,1)} %bitcast.58), calls=%async_computation | async-start | bytes 3538944 | tf_op jit(solution)/shard_map/all_to_all | solution.py:652
  27.3 1.2 pad.18.x_ref.refs_1_
  28.8 0.7 stack.63
  29.5 0.6 pad_add_fusion.slot_ref
  30.1 4.7 dispatch.5
  34.8 58.1 %all-to-all-done = bf16[8,144,768]{2,1,0:T(8,128)(2,1)S(1)} async-done(((bf16[8,144,768]{2,1,0:T(8,128)(2,1)}), bf16[8,144,768]{2,1,0:T(8,128)(2,1)S(1)}, u32[]{:S(2)}, u32[]{:S(2)}) %all-to-all-start) | async-done | bytes 1769504 | tf_op jit(solution)/shard_map/all_to_all | solution.py:652
  92.9 1.4 all-gather.3.cloned.1.call-done
  94.3 3.6 all-to-all-start.1
  97.9 1.4 collective-permute-done
  99.3 2.9 broadcast_select_fusion.1
  102.5 1.1 fusion.5.vec_ref.refs_6_
  103.5 1.1 copy-done
  104.7 16.6 %attention_forward.1 = (bf16[4,208,768]{2,1,0:T(8,128)(2,1)}, bf16[4,208,2304]{2,1,0:T(8,128)(2,1)}, bf16[4,208,768]{2,1,0:T(8,128)(2,1)}, f32[4,208,768]{2,1,0:T(8,128)}, bf16[4,208,768]{2,1,0:T(8,128)(2,1)}) custom-call(bf16[4,208,768]{2,1,0:T(8,128)(2,1)} %pad.18.x_ref.refs_1_, bf16[768,3200]{1,0:T(8,128)(2,1)} %bitcast.43, f32[8,768]{1,0:T(8,128)} %fusion.5.vec_ref.refs_6_), custom_call_target="tpu_custom_call" | custom-call | flops 1048576 | bytes 65536 | tf_op jit(solution)/shard_map/attention_forward/pallas_call | solution.py:125
  121.2 4.8 dispatch.7
  126.0 11.8 %all-to-all-done.1 = bf16[8,136,768]{2,1,0:T(8,128)(2,1)S(1)} async-done(((bf16[8,136,768]{2,1,0:T(8,128)(2,1)}), bf16[8,136,768]{2,1,0:T(8,128)(2,1)S(1)}, u32[]{:S(2)}, u32[]{:S(2)}) %all-to-all-start.1) | async-done | bytes 1671200 | tf_op jit(solution)/shard_map/all_to_all | solution.py:652
  137.8 3.6 all-to-all-start.2
  141.4 4.7 dispatch.6
  146.2 36.7 %all-to-all-done.2 = bf16[8,144,768]{2,1,0:T(8,128)(2,1)S(1)} async-done(((bf16[8,144,768]{2,1,0:T(8,128)(2,1)}), bf16[8,144,768]{2,1,0:T(8,128)(2,1)S(1)}, u32[]{:S(2)}, u32[]{:S(2)}) %all-to-all-start.2) | async-done | bytes 1769504 | tf_op jit(solution)/shard_map/all_to_all | solution.py:652
  182.9 3.9 all-to-all-start.3
  186.8 1.6 broadcast_select_fusion.4.router_ref
  188.4 42.8 %expert_chunk.2 = (bf16[1152,768]{1,0:T(8,128)(2,1)}, bf16[1152,768]{1,0:T(8,128)(2,1)}, bf16[1152,3072]{1,0:T(8,128)(2,1)}, bf16[1152,3072]{1,0:T(8,128)(2,1)},...) custom-call(s32[1]{0:T(128)} %bitcast.here_ref, ...), custom_call_target="tpu_custom_call" | custom-call | flops 1048576 | bytes 65536 | tf_op jit(solution)/shard_map/expert_chunk/pallas_call | solution.py:274
  231.2 6.4 %all-to-all-start.4 = ((bf16[8,144,768]{2,1,0:T(8,128)(2,1)}), bf16[8,144,768]{2,1,0:T(8,128)(2,1)S(1)}, u32[]{:S(2)}, u32[]{:S(2)}) async-start(bf16[8,144,768]{2,1,0:T(8,128)(2,1)} %bitcast.68), calls=%async_computation.4 | async-start | bytes 3538944 | tf_op jit(solution)/shard_map/all_to_all | solution.py:652
  237.7 40.5 %expert_chunk.3 = (bf16[1088,768]{1,0:T(8,128)(2,1)}, bf16[1088,768]{1,0:T(8,128)(2,1)}, bf16[1088,3072]{1,0:T(8,128)(2,1)}, bf16[1088,3072]{1,0:T(8,128)(2,1)},...) custom-call(s32[1]{0:T(128)} %bitcast.here_ref, ...), custom_call_target="tpu_custom_call" | custom-call | flops 1048576 | bytes 65536 | tf_op jit(solution)/shard_map/expert_chunk/pallas_call | solution.py:274
  278.4 5.8 %all-to-all-start.5 = ((bf16[8,136,768]{2,1,0:T(8,128)(2,1)}), bf16[8,136,768]{2,1,0:T(8,128)(2,1)S(1)}, u32[]{:S(2)}, u32[]{:S(2)}) async-start(bf16[8,136,768]{2,1,0:T(8,128)(2,1)} %bitcast.70), calls=%async_computation.5 | async-start | bytes 3342336 | tf_op jit(solution)/shard_map/all_to_all | solution.py:652
  284.2 19.1 %out_grad.1 = (bf16[1536,768]{1,0:T(8,128)(2,1)}, bf16[1536,768]{1,0:T(8,128)(2,1)}) custom-call(s32[1]{0:T(128)} %bitcast.26.core_ref, bf16[1152,3072]{1,0:T(8,128)(2,1)} %get-tuple-element.107.refs_0_, bf16[1088,3072]{1,0:T(8,128)(2,1)} %get-tuple-element.108.refs_1_, bf16[1152,768]{1,0:T(8,128)(2,1)} %get-tuple-element.109.refs_2_, ...), custom_call_target="tpu_custom_call" | custom-call | flops 1048576 | bytes 65536 | tf_op jit(solution)/shard_map/out_grad/pallas_call | solution.py:352
  303.3 18.1 %in_grad.1 = (bf16[384,3072]{1,0:T(8,128)(2,1)}, bf16[384,3072]{1,0:T(8,128)(2,1)}, f32[768,128]{1,0:T(8,128)}) custom-call(s32[1]{0:T(128)} %bitcast.26.core_ref, bf16[1152,768]{1,0:T(8,128)(2,1)} %bitcast.49, bf16[1088,768]{1,0:T(8,128)(2,1)} %bitcast.51, bf16[1152,3072]{1,0:T(8,128)(2,1)} %get-tuple-element.113.refs_2_, ...), custom_call_target="tpu_custom_call" | custom-call | flops 1048576 | bytes 65536 | tf_op jit(solution)/shard_map/in_grad/pallas_call | solution.py:403
  321.4 1.0 all-to-all-done.5
  322.4 5.3 %all-to-all-start.6 = ((bf16[8,144,768]{2,1,0:T(8,128)(2,1)}), bf16[8,144,768]{2,1,0:T(8,128)(2,1)}, u32[]{:S(2)}, u32[]{:S(2)}) async-start(bf16[8,144,768]{2,1,0:T(8,128)(2,1)} %bitcast.27), calls=%async_computation.6 | async-start | bytes 3538944 | tf_op jit(solution)/shard_map/all_to_all | solution.py:652
  327.8 3.0 add_convert_fusion.3
  330.7 1.5 collective-permute-start.3
  332.3 42.5 %attention_backward.1 = (bf16[4,208,768]{2,1,0:T(8,128)(2,1)}, bf16[768,1664]{1,0:T(8,128)(2,1)}, bf16[768,1664]{1,0:T(8,128)(2,1)}) custom-call(s32[1]{0:T(128)} %bitcast.26.core_ref, s32[4,8,208]{2,1,0:T(8,128)} %bitcast.71, bf16[4,208,768]{2,1,0:T(8,128)(2,1)} %pad.18.x_ref.refs_1_, bf16[4,208,768]{2,1,0:T(8,128)(2,1)} %pad.17.refs_2_, ...), custom_call_target="tpu_custom_call" | custom-call | flops 1048576 | bytes 65536 | tf_op jit(solution)/shard_map/attention_backward/pallas_call | solution.py:614
  374.8 9.5 %collective-permute-done.3 = bf16[1536,768]{1,0:T(8,128)(2,1)} collective-permute-done((bf16[1536,768]{1,0:T(8,128)(2,1)S(1)}, bf16[1536,768]{1,0:T(8,128)(2,1)}, u32[]{:S(2)}, u32[]{:S(2)}) %collective-permute-start.3) | collective-permute-done | bytes 2359328 | tf_op jit(solution)/shard_map/ppermute | solution.py:646
  384.8 6.0 %all-to-all-start.7 = ((bf16[8,136,768]{2,1,0:T(8,128)(2,1)}), bf16[8,136,768]{2,1,0:T(8,128)(2,1)}, u32[]{:S(2)}, u32[]{:S(2)}) async-start(bf16[8,136,768]{2,1,0:T(8,128)(2,1)} %bitcast.69), calls=%async_computation.7 | async-start | bytes 3342336 | tf_op jit(solution)/shard_map/all_to_all | solution.py:652
  390.8 3.1 add_convert_fusion
  394.0 1.5 collective-permute-start.5
  395.6 4.0 add_convert_fusion.4
  399.5 3.7 add_convert_fusion.2.mine_ref
  403.3 20.5 %collective-permute-done.5 = bf16[8,48,1664]{2,1,0:T(8,128)(2,1)S(1)} collective-permute-done((bf16[8,48,1664]{2,1,0:T(8,128)(2,1)S(1)}, bf16[8,48,1664]{2,1,0:T(8,128)(2,1)S(1)}, u32[]{:S(2)}, u32[]{:S(2)}) %collective-permute-start.5) | collective-permute-done | bytes 1277984 | tf_op jit(solution)/shard_map/ppermute | solution.py:646
  423.8 1.4 add_convert_fusion.5
  425.2 1.5 collective-permute-start.9
  426.7 3.4 all-to-all-done.7
  430.1 3.6 all-to-all-start.8
  434.0 7.9 %widen.2 = f32[3072,768]{1,0:T(8,128)} custom-call(s32[1]{0:T(128)} %bitcast.26.core_ref, bf16[1536,768]{1,0:T(8,128)(2,1)} %add_convert_fusion.2.mine_ref, bf16[1536,768]{1,0:T(8,128)(2,1)} %collective-permute-done.6.theirs_ref), custom_call_target="tpu_custom_call" | custom-call | flops 1048576 | bytes 65536 | tf_op jit(solution)/shard_map/widen/pallas_call | solution.py:445
  441.8 8.2 %combine_output.1 = bf16[4,208,768]{2,1,0:T(8,128)(2,1)} custom-call(s32[4,8,208]{2,1,0:T(8,128)} %bitcast.72, f32[4,208,768]{2,1,0:T(8,128)} %get-tuple-element.123.refs_3_.mid_ref, bf16[1152,768]{1,0:T(8,128)(2,1)} %bitcast.28.refs_0_, bf16[1088,768]{1,0:T(8,128)(2,1)} %bitcast.31.refs_1_), custom_call_target="tpu_custom_call" | custom-call | flops 1048576 | bytes 65536 | tf_op jit(solution)/shard_map/combine_output/pallas_call | solution.py:480
  450.0 14.6 %all-to-all-done.8 = bf16[8,48,1664]{2,1,0:T(8,128)(2,1)S(1)} async-done(((bf16[8,48,1664]{2,1,0:T(8,128)(2,1)}), bf16[8,48,1664]{2,1,0:T(8,128)(2,1)S(1)}, u32[]{:S(2)}, u32[]{:S(2)}) %all-to-all-start.8) | async-done | bytes 1277984 | tf_op jit(solution)/shard_map/all_to_all | solution.py:823
  464.8 1.5 collective-permute-start.7
  466.3 12.9 %collective-permute-done.9 = bf16[384,3072]{1,0:T(8,128)(2,1)} collective-permute-done((bf16[384,3072]{1,0:T(8,128)(2,1)}, bf16[384,3072]{1,0:T(8,128)(2,1)}, u32[]{:S(2)}, u32[]{:S(2)}) %collective-permute-start.9) | collective-permute-done | bytes 2359328 | tf_op jit(solution)/shard_map/ppermute | solution.py:646
  479.2 3.3 add_convert_fusion.1.mine_ref
  483.2 1.5 collective-permute-start.12
  484.8 2.2 collective-permute-done.12
  488.3 1.5 copy.53
  489.8 1.5 copy.52
  491.5 1.0 slice.87
  492.5 0.7 copy.54
  493.2 0.9 slice_reduce_fusion
  494.1 0.7 maximum_convert_fusion.1
  494.8 7.9 %widen.3 = f32[768,3072]{1,0:T(8,128)} custom-call(s32[1]{0:T(128)} %bitcast.26.core_ref, bf16[384,3072]{1,0:T(8,128)(2,1)} %copy-done.3, bf16[384,3072]{1,0:T(8,128)(2,1)} %collective-permute-done.10.theirs_ref), custom_call_target="tpu_custom_call" | custom-call | flops 1048576 | bytes 65536 | tf_op jit(solution)/shard_map/widen/pallas_call | solution.py:445
  (84 shorter events, 5.1 us)
Async XLA Ops:
  7.2 87.0 %all-gather.3.cloned.1.call-start = ((), (), s32[]{:S(2)}) async-start(), calls=%async_computation.9 | async-start | bytes 2764800 | tf_op jit(solution)/shard_map/all_gather | solution.py:720
  19.8 7.4 %copy-start.9 = (bf16[4,197,768]{2,0,1:T(4,128)(2,1)S(1)}, bf16[4,197,768]{2,0,1:T(4,128)(2,1)}, u32[]{:S(2)}) copy-start(bf16[4,197,768]{2,0,1:T(4,128)(2,1)} %param.17) | copy-start | bytes 3631108
  19.8 73.1 %all-to-all-start = ((bf16[8,144,768]{2,1,0:T(8,128)(2,1)}), bf16[8,144,768]{2,1,0:T(8,128)(2,1)S(1)}, u32[]{:S(2)}, u32[]{:S(2)}) async-start(bf16[8,144,768]{2,1,0:T(8,128)(2,1)} %bitcast.58), calls=%async_computation | async-start | bytes 3538944 | tf_op jit(solution)/shard_map/all_to_all | solution.py:652
  92.9 9.3 %copy-start.5 = (bf16[8,144,768]{2,1,0:T(8,128)(2,1)}, bf16[8,144,768]{2,1,0:T(8,128)(2,1)S(1)}, u32[]{:S(2)}) copy-start(bf16[8,144,768]{2,1,0:T(8,128)(2,1)S(1)} %all-to-all-done) | copy-start | bytes 5308420
  94.2 5.0 collective-permute-start
  94.3 43.5 %all-to-all-start.1 = ((bf16[8,136,768]{2,1,0:T(8,128)(2,1)}), bf16[8,136,768]{2,1,0:T(8,128)(2,1)S(1)}, u32[]{:S(2)}, u32[]{:S(2)}) async-start(bf16[8,136,768]{2,1,0:T(8,128)(2,1)} %bitcast.62), calls=%async_computation.1 | async-start | bytes 3342336 | tf_op jit(solution)/shard_map/all_to_all | solution.py:652
  102.5 2.2 copy-start
  137.8 8.4 %copy-start.6 = (bf16[8,136,768]{2,1,0:T(8,128)(2,1)}, bf16[8,136,768]{2,1,0:T(8,128)(2,1)S(1)}, u32[]{:S(2)}) copy-start(bf16[8,136,768]{2,1,0:T(8,128)(2,1)S(1)} %all-to-all-done.1) | copy-start | bytes 5013508
  137.8 45.1 %all-to-all-start.2 = ((bf16[8,144,768]{2,1,0:T(8,128)(2,1)}), bf16[8,144,768]{2,1,0:T(8,128)(2,1)S(1)}, u32[]{:S(2)}, u32[]{:S(2)}) async-start(bf16[8,144,768]{2,1,0:T(8,128)(2,1)} %bitcast.59), calls=%async_computation.2 | async-start | bytes 3538944 | tf_op jit(solution)/shard_map/all_to_all | solution.py:652
  182.9 5.5 %copy-start.1 = (bf16[8,144,768]{2,1,0:T(8,128)(2,1)}, bf16[8,144,768]{2,1,0:T(8,128)(2,1)S(1)}, u32[]{:S(2)}) copy-start(bf16[8,144,768]{2,1,0:T(8,128)(2,1)S(1)} %all-to-all-done.2) | copy-start | bytes 5308420
  182.9 48.3 %all-to-all-start.3 = ((bf16[8,136,768]{2,1,0:T(8,128)(2,1)}), bf16[8,136,768]{2,1,0:T(8,128)(2,1)S(1)}, u32[]{:S(2)}, u32[]{:S(2)}) async-start(bf16[8,136,768]{2,1,0:T(8,128)(2,1)} %bitcast.63), calls=%async_computation.3 | async-start | bytes 3342336 | tf_op jit(solution)/shard_map/all_to_all | solution.py:652
  231.2 6.5 %copy-start.2 = (bf16[8,136,768]{2,1,0:T(8,128)(2,1)}, bf16[8,136,768]{2,1,0:T(8,128)(2,1)S(1)}, u32[]{:S(2)}) copy-start(bf16[8,136,768]{2,1,0:T(8,128)(2,1)S(1)} %all-to-all-done.3) | copy-start | bytes 5013508
  231.2 47.2 %all-to-all-start.4 = ((bf16[8,144,768]{2,1,0:T(8,128)(2,1)}), bf16[8,144,768]{2,1,0:T(8,128)(2,1)S(1)}, u32[]{:S(2)}, u32[]{:S(2)}) async-start(bf16[8,144,768]{2,1,0:T(8,128)(2,1)} %bitcast.68), calls=%async_computation.4 | async-start | bytes 3538944 | tf_op jit(solution)/shard_map/all_to_all | solution.py:652
  278.4 24.9 %copy-start.4 = (bf16[8,144,768]{2,1,0:T(8,128)(2,1)}, bf16[8,144,768]{2,1,0:T(8,128)(2,1)S(1)}, u32[]{:S(2)}) copy-start(bf16[8,144,768]{2,1,0:T(8,128)(2,1)S(1)} %all-to-all-done.4) | copy-start | bytes 5308420
  278.4 44.0 %all-to-all-start.5 = ((bf16[8,136,768]{2,1,0:T(8,128)(2,1)}), bf16[8,136,768]{2,1,0:T(8,128)(2,1)S(1)}, u32[]{:S(2)}, u32[]{:S(2)}) async-start(bf16[8,136,768]{2,1,0:T(8,128)(2,1)} %bitcast.70), calls=%async_computation.5 | async-start | bytes 3342336 | tf_op jit(solution)/shard_map/all_to_all | solution.py:652
  322.4 5.3 %copy-start.7 = (bf16[8,136,768]{2,1,0:T(8,128)(2,1)}, bf16[8,136,768]{2,1,0:T(8,128)(2,1)S(1)}, u32[]{:S(2)}) copy-start(bf16[8,136,768]{2,1,0:T(8,128)(2,1)S(1)} %all-to-all-done.5) | copy-start | bytes 5013508
  322.4 5.3 %collective-permute-start.2 = (bf16[1536,768]{1,0:T(8,128)(2,1)}, bf16[1536,768]{1,0:T(8,128)(2,1)}, u32[]{:S(2)}, u32[]{:S(2)}) collective-permute-start(bf16[1536,768]{1,0:T(8,128)(2,1)} %get-tuple-element.136), channel_id=1, source_target_pairs={{0,8},{8,0},{16,24},{24,16},{1,9},{9,1},{17,25},{25,17},{2,10},{10... | collective-permute-start | bytes 7077896 | tf_op jit(solution)/shard_map/ppermute | solution.py:646
  322.4 52.4 %all-to-all-start.6 = ((bf16[8,144,768]{2,1,0:T(8,128)(2,1)}), bf16[8,144,768]{2,1,0:T(8,128)(2,1)}, u32[]{:S(2)}, u32[]{:S(2)}) async-start(bf16[8,144,768]{2,1,0:T(8,128)(2,1)} %bitcast.27), calls=%async_computation.6 | async-start | bytes 3538944 | tf_op jit(solution)/shard_map/all_to_all | solution.py:652
  330.7 53.5 %collective-permute-start.3 = (bf16[1536,768]{1,0:T(8,128)(2,1)S(1)}, bf16[1536,768]{1,0:T(8,128)(2,1)}, u32[]{:S(2)}, u32[]{:S(2)}) collective-permute-start(bf16[1536,768]{1,0:T(8,128)(2,1)S(1)} %add_convert_fusion.3), channel_id=1, source_target_pairs={{0,16},{8,24},{16,0},{24,8},{1,17},{9,25},{17,1},{25,9},{2,18},{10... | collective-permute-start | bytes 7077896 | tf_op jit(solution)/shard_map/ppermute | solution.py:646
  384.3 6.5 %collective-permute-start.4 = (bf16[768,1664]{1,0:T(8,128)(2,1)}, bf16[768,1664]{1,0:T(8,128)(2,1)}, u32[]{:S(2)}, u32[]{:S(2)}) collective-permute-start(bf16[768,1664]{1,0:T(8,128)(2,1)} %get-tuple-element.138), channel_id=1, source_target_pairs={{0,8},{8,0},{16,24},{24,16},{1,9},{9,1},{17,25},{25,17},{2,10},{10... | collective-permute-start | bytes 7667720 | tf_op jit(solution)/shard_map/ppermute | solution.py:646
  384.3 11.3 %collective-permute-start.1 = (bf16[384,3072]{1,0:T(8,128)(2,1)}, bf16[384,3072]{1,0:T(8,128)(2,1)}, u32[]{:S(2)}, u32[]{:S(2)}) collective-permute-start(bf16[384,3072]{1,0:T(8,128)(2,1)} %get-tuple-element.120), channel_id=1, source_target_pairs={{0,8},{8,0},{16,24},{24,16},{1,9},{9,1},{17,25},{25,17},{2,10},{10... | collective-permute-start | bytes 7077896 | tf_op jit(solution)/shard_map/ppermute | solution.py:646
  384.8 45.3 %all-to-all-start.7 = ((bf16[8,136,768]{2,1,0:T(8,128)(2,1)}), bf16[8,136,768]{2,1,0:T(8,128)(2,1)}, u32[]{:S(2)}, u32[]{:S(2)}) async-start(bf16[8,136,768]{2,1,0:T(8,128)(2,1)} %bitcast.69), calls=%async_computation.7 | async-start | bytes 3342336 | tf_op jit(solution)/shard_map/all_to_all | solution.py:652
  393.9 1.7 copy-start.8
  394.0 29.8 %collective-permute-start.5 = (bf16[8,48,1664]{2,1,0:T(8,128)(2,1)S(1)}, bf16[8,48,1664]{2,1,0:T(8,128)(2,1)S(1)}, u32[]{:S(2)}, u32[]{:S(2)}) collective-permute-start(bf16[8,48,1664]{2,1,0:T(8,128)(2,1)S(1)} %constant_dynamic-slice_fusion), channel_id=1, source_target_pairs={{0,16},{8,24},{16,0},{24,8},{1,17},{9,25},{17,1},{25,9},{2,18},{10... | collective-permute-start | bytes 3833864 | tf_op jit(solution)/shard_map/ppermute | solution.py:646
  403.2 30.5 %copy-start.13 = (f32[1,768]{1,0:T(1,128)S(1)}, f32[1,768]{1,0:T(1,128)}, u32[]{:S(2)}) copy-start(f32[1,768]{1,0:T(1,128)} %get-tuple-element.153) | copy-start | bytes 9220
  403.2 30.5 %copy-start.14 = (f32[1,768]{1,0:T(1,128)S(1)}, f32[1,768]{1,0:T(1,128)}, u32[]{:S(2)}) copy-start(f32[1,768]{1,0:T(1,128)} %get-tuple-element.154) | copy-start | bytes 9220
  403.2 30.5 %copy-start.11 = (f32[1,3072]{1,0:T(1,128)S(1)}, f32[1,3072]{1,0:T(1,128)}, u32[]{:S(2)}) copy-start(f32[1,3072]{1,0:T(1,128)} %get-tuple-element.151) | copy-start | bytes 36868
  403.2 30.6 %copy-start.12 = (f32[1,3072]{1,0:T(1,128)S(1)}, f32[1,3072]{1,0:T(1,128)}, u32[]{:S(2)}) copy-start(f32[1,3072]{1,0:T(1,128)} %get-tuple-element.152) | copy-start | bytes 36868
  403.2 30.7 %collective-permute-start.6 = (bf16[1536,768]{1,0:T(8,128)(2,1)}, bf16[1536,768]{1,0:T(8,128)(2,1)}, u32[]{:S(2)}, u32[]{:S(2)}) collective-permute-start(bf16[1536,768]{1,0:T(8,128)(2,1)} %add_convert_fusion.2.mine_ref), channel_id=1, source_target_pairs={{0,8},{8,0},{16,24},{24,16},{1,9},{9,1},{17,25},{25,17},{2,10},{10... | collective-permute-start | bytes 7077896 | tf_op jit(solution)/shard_map/ppermute | solution.py:646
  425.2 54.0 %collective-permute-start.9 = (bf16[384,3072]{1,0:T(8,128)(2,1)}, bf16[384,3072]{1,0:T(8,128)(2,1)}, u32[]{:S(2)}, u32[]{:S(2)}) collective-permute-start(bf16[384,3072]{1,0:T(8,128)(2,1)} %add_convert_fusion.4), channel_id=1, source_target_pairs={{0,16},{8,24},{16,0},{24,8},{1,17},{9,25},{17,1},{25,9},{2,18},{10... | collective-permute-start | bytes 7077896 | tf_op jit(solution)/shard_map/ppermute | solution.py:646
  430.1 34.5 %all-to-all-start.8 = ((bf16[8,48,1664]{2,1,0:T(8,128)(2,1)}), bf16[8,48,1664]{2,1,0:T(8,128)(2,1)S(1)}, u32[]{:S(2)}, u32[]{:S(2)}) async-start(bf16[8,48,1664]{2,1,0:T(8,128)(2,1)} %add_convert_fusion.5), calls=%async_computation.8 | async-start | bytes 2555904 | tf_op jit(solution)/shard_map/all_to_all | solution.py:823
  433.9 49.3 %collective-permute-start.11 = (bf16[5,768]{1,0:T(8,128)(2,1)S(1)}, bf16[5,768]{1,0:T(8,128)(2,1)S(1)}, u32[]{:S(2)}, u32[]{:S(2)}) collective-permute-start(bf16[5,768]{1,0:T(8,128)(2,1)S(1)} %convert_element_type.113), channel_id=1, source_target_pairs={{0,8},{8,0},{16,24},{24,16},{1,9},{9,1},{17,25},{25,17},{2,10},{10... | collective-permute-start | bytes 23048 | tf_op jit(solution)/shard_map/ppermute | solution.py:646
  464.8 23.4 %copy-start.10 = (bf16[4,208,768]{2,1,0:T(8,128)(2,1)S(1)}, bf16[4,208,768]{2,1,0:T(8,128)(2,1)}, u32[]{:S(2)}) copy-start(bf16[4,208,768]{2,1,0:T(8,128)(2,1)} %get-tuple-element.148) | copy-start | bytes 3833860
  464.8 17.8 %collective-permute-start.7 = (bf16[48,1664]{1,0:T(8,128)(2,1)S(1)}, bf16[48,1664]{1,0:T(8,128)(2,1)S(1)}, u32[]{:S(2)}, u32[]{:S(2)}) collective-permute-start(bf16[48,1664]{1,0:T(8,128)(2,1)S(1)} %reduce_sum.38), channel_id=1, source_target_pairs={{0,16},{8,24},{16,0},{24,8},{1,17},{9,25},{17,1},{25,9},{2,18},{10... | collective-permute-start | bytes 479240 | tf_op jit(solution)/shard_map/ppermute | solution.py:646
  482.5 7.3 %copy-start.3 = (bf16[384,3072]{1,0:T(8,128)(2,1)}, bf16[384,3072]{1,0:T(8,128)(2,1)S(1)}, u32[]{:S(2)}) copy-start(bf16[384,3072]{1,0:T(8,128)(2,1)S(1)} %add_convert_fusion.1.mine_ref) | copy-start | bytes 7077892
  482.5 12.3 %collective-permute-start.10 = (bf16[384,3072]{1,0:T(8,128)(2,1)S(1)}, bf16[384,3072]{1,0:T(8,128)(2,1)}, u32[]{:S(2)}, u32[]{:S(2)}) collective-permute-start(bf16[384,3072]{1,0:T(8,128)(2,1)S(1)} %add_convert_fusion.1.mine_ref), channel_id=1, source_target_pairs={{0,8},{8,0},{16,24},{24,16},{1,9},{9,1},{17,25},{25,17},{2,10},{10... | collective-permute-start | bytes 7077896 | tf_op jit(solution)/shard_map/ppermute | solution.py:646
  482.7 8.6 %collective-permute-start.8 = (bf16[96,1664]{1,0:T(8,128)(2,1)S(1)}, bf16[96,1664]{1,0:T(8,128)(2,1)S(1)}, u32[]{:S(2)}, u32[]{:S(2)}) collective-permute-start(bf16[96,1664]{1,0:T(8,128)(2,1)S(1)} %pad_maximum_fusion.1), channel_id=1, source_target_pairs={{0,8},{8,0},{16,24},{24,16},{1,9},{9,1},{17,25},{25,17},{2,10},{10... | collective-permute-start | bytes 958472 | tf_op jit(solution)/shard_map/ppermute | solution.py:646
  483.2 3.8 collective-permute-start.12
  488.3 1.5 slice-start
Sparse Core Ops, SparseCore 0:
  10.8 83.4 all-gather.2

commit v4 on v3

--- a/solution.py
+++ b/solution.py
@@ -419,7 +419,8 @@
     )(core, *arrived, *inners, *logits)
 
 
-def widen_kernel(core_ref, mine_ref, theirs_ref, out_ref):
+def widen_kernel(core_ref, mine_ref, theirs_ref, *refs):
+    out_ref = refs[-1]
     own = pl.program_id(0) == core_ref[0]
 
     @pl.when(own)
@@ -431,7 +432,7 @@
         out_ref[...] = theirs_ref[...].astype(f32)
 
 
-def widen(core, mine, theirs):
+def widen(core, mine, theirs, column=0, columns=1, kept=()):
     high, wide = mine.shape
     tile = high // 4
 
@@ -447,14 +448,16 @@
         grid_spec=pltpu.PrefetchScalarGridSpec(
             num_scalar_prefetch=1,
             grid=(2, 4),
-            in_specs=[block(True), block(False)],
-            out_specs=pl.BlockSpec((tile, wide), lambda h, i, _: (h * 4 + i, 0)),
+            in_specs=[block(True), block(False)]
+            + [pl.BlockSpec(memory_space=pl.ANY)] * len(kept),
+            out_specs=pl.BlockSpec((tile, wide), lambda h, i, _: (h * 4 + i, column)),
         ),
-        out_shape=jax.ShapeDtypeStruct((2 * high, wide), f32),
+        out_shape=jax.ShapeDtypeStruct((2 * high, columns * wide), f32),
+        input_output_aliases={3: 0} if kept else {},
         compiler_params=params(2),
         cost_estimate=cost(),
         name="widen",
-    )(core, mine, theirs)
+    )(core, mine, theirs, *kept)
 
 
 def collect(slots, rows):
@@ -818,18 +821,23 @@
     mine = add(mine, swap(other, "replica", 2))
     out_mine = over_chips(add(out_mine, out_theirs), 4)
     in_mine, mine = tie(in_mine, mine)
-    in_mine = over_chips(in_mine)
+    half_wide = in_mine.shape[1] // 2
+    in_first = over_chips(in_mine[:, :half_wide])
+    in_second, in_first = tie(in_mine[:, half_wide:], in_first)
+    in_second = over_chips(in_second)
     mine, returned[1] = tie(mine, returned[1])
     pieces = lax.all_to_all(mine, "shard", split_axis=0, concat_axis=0, tiled=True)
     output = combine_output(image_slots, middle, returned)
     expert_out_grad = widen(core_here, out_mine, swap(out_mine, "replica", 1))[None]
-    pieces, output, expert_out_grad = tie(pieces, output, expert_out_grad)
+    in_wide = widen(core_here, in_first, swap(in_first, "replica", 1), 0, 2)
+    pieces, output, expert_out_grad, in_wide = tie(pieces, output, expert_out_grad, in_wide)
     mine = jnp.sum(pieces.astype(f32), 0).astype(bf16)
     mine = over_chips(mine, 4)
     mine = join(mine, swap(mine, "replica", 2), chip, 0)
     summed = join(mine, swap(mine, "replica", 1), core, 1).astype(f32)
 
-    expert_in_grad = widen(core_here, in_mine, swap(in_mine, "replica", 1))[None]
+    in_theirs = swap(in_second, "replica", 1)
+    expert_in_grad = widen(core_here, in_second, in_theirs, 1, 2, (in_wide,))[None]
     biases = biases.astype(f32).reshape(1, -1)
     hidden_width = expert_in_bias.shape[1]
     small_sum = summed[:, 4 * width :]

time: 517 us -> 524 us (1.014)
  waiting for transfers between devices: 174 us -> 167 us
  local copies, waits for them, and re-layouts: 15.3 us -> 21 us
    all_to_all x1, waiting for transfers between devices: 14.6 us -> 0.01 us  [per_device(): lax.all_to_all(mine, 'shard', split_axis=0, concat_axis=0, tiled=True)]
    pallas_call x2 -> x3, Pallas kernels: 15.7 us -> 20.4 us  [widen(): pl.pallas_call(widen_kernel, grid_spec=pltpu.PrefetchScalarGridSpec(num_s...]
    ppermute x13 -> x15, waiting for transfers between devices: 46.4 us -> 50.8 us  [swap(): return lax.ppermute(value, axis, [(i, i ^ distance) for i in range(count)])]
    unnamed x38 -> x50, local copies, waits for them, and re-layouts: 7.19 us -> 10.7 us
    convert_element_type x7 -> x8, other arithmetic: 18.4 us -> 18.6 us  [add(): return (left.astype(f32) + right.astype(f32)).astype(bf16)]
  transfers between devices with their start and end apart: 23 -> 25, of which waited for: 13 -> 14; matrix products, arithmetic and copies ran while one was open for 8% -> 8% of each run, Pallas kernels for 42% -> 43%
where the time goes in v4:
time: 524 us; the launch traced here: 517 us
  Pallas kernels  227 us (43%)
  waiting for transfers between devices  167 us (32%)
  starting transfers between devices  56 us (11%)
  other arithmetic  29.2 us (6%)
  local copies, waits for them, and re-layouts  21 us (4%)
  between operations  14.8 us (3%)
    all_to_all x8, waiting for transfers between devices, exchange(): lax.all_to_all(blocks, 'shard', split_axis=0, concat_axis=0, tiled=True)  115 us
    pallas_call x2, Pallas kernels, expert_chunk(): pl.pallas_call(functools.partial(expert_kernel, experts, tiles), grid_spe...  83.3 us
    ppermute x15, waiting for transfers between devices, swap(): return lax.ppermute(value, axis, [(i, i ^ distance) for i in range(count)])  50.8 us
    pallas_call x1, Pallas kernels, attention_backward(): pl.pallas_call(functools.partial(backward_kernel, seq_len, width, experts...  42.5 us
    all_to_all x8, starting transfers between devices, exchange(): lax.all_to_all(blocks, 'shard', split_axis=0, concat_axis=0, tiled=True)  42 us
    pallas_call x3, Pallas kernels, widen(): pl.pallas_call(widen_kernel, grid_spec=pltpu.PrefetchScalarGridSpec(num_s...  20.4 us
    pallas_call x4, Pallas kernels, dispatch(): pl.pallas_call(dispatch_kernel, in_specs=[whole(slots.shape), whole(rows....  19.1 us
    pallas_call x1, Pallas kernels, out_grad(): pl.pallas_call(functools.partial(out_grad_kernel, parts), grid_spec=pltpu...  19.1 us
  transfers between devices with their start and end apart: 25, of which 14 were waited for; matrix products, arithmetic and copies ran while one was open for 8% of the time, Pallas kernels for 43%

profile of v4, /device:TPU:0, one launch (start us, length us, event | category | flops | bytes accessed | tf_op | source)
XLA Modules:
  0.0 516.6 jit_solution(6298874435953305103)
XLA Ops:
  7.2 1.5 concatenate.20
  8.8 1.7 fusion.3
  11.4 1.4 copy.51
  12.8 1.1 pad.17.refs_2_
  14.9 4.8 dispatch.4
  19.8 7.4 %all-to-all-start = ((bf16[8,144,768]{2,1,0:T(8,128)(2,1)}), bf16[8,144,768]{2,1,0:T(8,128)(2,1)S(1)}, u32[]{:S(2)}, u32[]{:S(2)}) async-start(bf16[8,144,768]{2,1,0:T(8,128)(2,1)} %bitcast.58), calls=%async_computation | async-start | bytes 3538944 | tf_op jit(solution)/shard_map/all_to_all | solution.py:655
  27.3 1.2 pad.18.x_ref.refs_1_
  30.1 4.7 dispatch.5
  34.8 58.1 %all-to-all-done = bf16[8,144,768]{2,1,0:T(8,128)(2,1)S(1)} async-done(((bf16[8,144,768]{2,1,0:T(8,128)(2,1)}), bf16[8,144,768]{2,1,0:T(8,128)(2,1)S(1)}, u32[]{:S(2)}, u32[]{:S(2)}) %all-to-all-start) | async-done | bytes 1769504 | tf_op jit(solution)/shard_map/all_to_all | solution.py:655
  92.9 1.4 all-gather.3.cloned.1.call-done
  94.3 3.6 all-to-all-start.1
  97.9 1.4 collective-permute-done
  99.3 2.9 broadcast_select_fusion.1
  102.5 1.0 fusion.5.vec_ref.refs_6_
  103.5 1.1 copy-done
  104.7 16.5 %attention_forward.1 = (bf16[4,208,768]{2,1,0:T(8,128)(2,1)}, bf16[4,208,2304]{2,1,0:T(8,128)(2,1)}, bf16[4,208,768]{2,1,0:T(8,128)(2,1)}, f32[4,208,768]{2,1,0:T(8,128)}, bf16[4,208,768]{2,1,0:T(8,128)(2,1)}) custom-call(bf16[4,208,768]{2,1,0:T(8,128)(2,1)} %pad.18.x_ref.refs_1_, bf16[768,3200]{1,0:T(8,128)(2,1)} %bitcast.43, f32[8,768]{1,0:T(8,128)} %fusion.5.vec_ref.refs_6_), custom_call_target="tpu_custom_call" | custom-call | flops 1048576 | bytes 65536 | tf_op jit(solution)/shard_map/attention_forward/pallas_call | solution.py:125
  121.2 4.8 dispatch.7
  126.0 11.8 %all-to-all-done.1 = bf16[8,136,768]{2,1,0:T(8,128)(2,1)S(1)} async-done(((bf16[8,136,768]{2,1,0:T(8,128)(2,1)}), bf16[8,136,768]{2,1,0:T(8,128)(2,1)S(1)}, u32[]{:S(2)}, u32[]{:S(2)}) %all-to-all-start.1) | async-done | bytes 1671200 | tf_op jit(solution)/shard_map/all_to_all | solution.py:655
  137.8 3.6 all-to-all-start.2
  141.4 4.7 dispatch.6
  146.2 36.7 %all-to-all-done.2 = bf16[8,144,768]{2,1,0:T(8,128)(2,1)S(1)} async-done(((bf16[8,144,768]{2,1,0:T(8,128)(2,1)}), bf16[8,144,768]{2,1,0:T(8,128)(2,1)S(1)}, u32[]{:S(2)}, u32[]{:S(2)}) %all-to-all-start.2) | async-done | bytes 1769504 | tf_op jit(solution)/shard_map/all_to_all | solution.py:655
  182.9 3.9 all-to-all-start.3
  186.8 1.6 broadcast_select_fusion.4.router_ref
  188.4 42.7 %expert_chunk.2 = (bf16[1152,768]{1,0:T(8,128)(2,1)}, bf16[1152,768]{1,0:T(8,128)(2,1)}, bf16[1152,3072]{1,0:T(8,128)(2,1)}, bf16[1152,3072]{1,0:T(8,128)(2,1)},...) custom-call(s32[1]{0:T(128)} %bitcast.here_ref, ...), custom_call_target="tpu_custom_call" | custom-call | flops 1048576 | bytes 65536 | tf_op jit(solution)/shard_map/expert_chunk/pallas_call | solution.py:274
  231.2 6.4 %all-to-all-start.4 = ((bf16[8,144,768]{2,1,0:T(8,128)(2,1)}), bf16[8,144,768]{2,1,0:T(8,128)(2,1)S(1)}, u32[]{:S(2)}, u32[]{:S(2)}) async-start(bf16[8,144,768]{2,1,0:T(8,128)(2,1)} %bitcast.68), calls=%async_computation.4 | async-start | bytes 3538944 | tf_op jit(solution)/shard_map/all_to_all | solution.py:655
  237.6 40.5 %expert_chunk.3 = (bf16[1088,768]{1,0:T(8,128)(2,1)}, bf16[1088,768]{1,0:T(8,128)(2,1)}, bf16[1088,3072]{1,0:T(8,128)(2,1)}, bf16[1088,3072]{1,0:T(8,128)(2,1)},...) custom-call(s32[1]{0:T(128)} %bitcast.here_ref, ...), custom_call_target="tpu_custom_call" | custom-call | flops 1048576 | bytes 65536 | tf_op jit(solution)/shard_map/expert_chunk/pallas_call | solution.py:274
  278.4 5.8 %all-to-all-start.5 = ((bf16[8,136,768]{2,1,0:T(8,128)(2,1)}), bf16[8,136,768]{2,1,0:T(8,128)(2,1)S(1)}, u32[]{:S(2)}, u32[]{:S(2)}) async-start(bf16[8,136,768]{2,1,0:T(8,128)(2,1)} %bitcast.69), calls=%async_computation.5 | async-start | bytes 3342336 | tf_op jit(solution)/shard_map/all_to_all | solution.py:655
  284.2 19.1 %out_grad.1 = (bf16[1536,768]{1,0:T(8,128)(2,1)}, bf16[1536,768]{1,0:T(8,128)(2,1)}) custom-call(s32[1]{0:T(128)} %bitcast.26.core_ref, bf16[1152,3072]{1,0:T(8,128)(2,1)} %get-tuple-element.110.refs_0_, bf16[1088,3072]{1,0:T(8,128)(2,1)} %get-tuple-element.111.refs_1_, bf16[1152,768]{1,0:T(8,128)(2,1)} %get-tuple-element.112.refs_2_, ...), custom_call_target="tpu_custom_call" | custom-call | flops 1048576 | bytes 65536 | tf_op jit(solution)/shard_map/out_grad/pallas_call | solution.py:352
  303.3 18.1 %in_grad.1 = (bf16[384,3072]{1,0:T(8,128)(2,1)}, bf16[384,3072]{1,0:T(8,128)(2,1)}, f32[768,128]{1,0:T(8,128)}) custom-call(s32[1]{0:T(128)} %bitcast.26.core_ref, bf16[1152,768]{1,0:T(8,128)(2,1)} %bitcast.50, bf16[1088,768]{1,0:T(8,128)(2,1)} %bitcast.52, bf16[1152,3072]{1,0:T(8,128)(2,1)} %get-tuple-element.116.refs_2_, ...), custom_call_target="tpu_custom_call" | custom-call | flops 1048576 | bytes 65536 | tf_op jit(solution)/shard_map/in_grad/pallas_call | solution.py:403
  321.4 1.1 all-to-all-done.5
  322.4 5.3 %all-to-all-start.6 = ((bf16[8,144,768]{2,1,0:T(8,128)(2,1)}), bf16[8,144,768]{2,1,0:T(8,128)(2,1)}, u32[]{:S(2)}, u32[]{:S(2)}) async-start(bf16[8,144,768]{2,1,0:T(8,128)(2,1)} %bitcast.27), calls=%async_computation.6 | async-start | bytes 3538944 | tf_op jit(solution)/shard_map/all_to_all | solution.py:655
  327.7 3.0 add_convert_fusion.2
  330.7 1.5 collective-permute-start.3
  332.2 42.5 %attention_backward.1 = (bf16[4,208,768]{2,1,0:T(8,128)(2,1)}, bf16[768,1664]{1,0:T(8,128)(2,1)}, bf16[768,1664]{1,0:T(8,128)(2,1)}) custom-call(s32[1]{0:T(128)} %bitcast.26.core_ref, s32[4,8,208]{2,1,0:T(8,128)} %bitcast.70, bf16[4,208,768]{2,1,0:T(8,128)(2,1)} %pad.18.x_ref.refs_1_, bf16[4,208,768]{2,1,0:T(8,128)(2,1)} %pad.17.refs_2_, ...), custom_call_target="tpu_custom_call" | custom-call | flops 1048576 | bytes 65536 | tf_op jit(solution)/shard_map/attention_backward/pallas_call | solution.py:617
  374.8 9.5 %collective-permute-done.3 = bf16[1536,768]{1,0:T(8,128)(2,1)} collective-permute-done((bf16[1536,768]{1,0:T(8,128)(2,1)S(1)}, bf16[1536,768]{1,0:T(8,128)(2,1)}, u32[]{:S(2)}, u32[]{:S(2)}) %collective-permute-start.3) | collective-permute-done | bytes 2359328 | tf_op jit(solution)/shard_map/ppermute | solution.py:649
  384.7 7.9 %collective-permute-done.4 = bf16[768,1664]{1,0:T(8,128)(2,1)S(1)} collective-permute-done((bf16[768,1664]{1,0:T(8,128)(2,1)}, bf16[768,1664]{1,0:T(8,128)(2,1)S(1)}, u32[]{:S(2)}, u32[]{:S(2)}) %collective-permute-start.4) | collective-permute-done | bytes 2555936 | tf_op jit(solution)/shard_map/ppermute | solution.py:649
  392.6 2.3 add_convert_fusion
  395.0 1.5 copy-done.3
  396.4 1.1 constant_dynamic-slice_fusion
  397.6 1.5 collective-permute-start.5
  399.0 6.0 %all-to-all-start.7 = ((bf16[8,136,768]{2,1,0:T(8,128)(2,1)}), bf16[8,136,768]{2,1,0:T(8,128)(2,1)}, u32[]{:S(2)}, u32[]{:S(2)}) async-start(bf16[8,136,768]{2,1,0:T(8,128)(2,1)} %bitcast.30), calls=%async_computation.7 | async-start | bytes 3342336 | tf_op jit(solution)/shard_map/all_to_all | solution.py:655
  405.1 3.4 add_convert_fusion.3
  408.5 19.5 %collective-permute-done.5 = bf16[8,48,1664]{2,1,0:T(8,128)(2,1)} collective-permute-done((bf16[8,48,1664]{2,1,0:T(8,128)(2,1)}, bf16[8,48,1664]{2,1,0:T(8,128)(2,1)}, u32[]{:S(2)}, u32[]{:S(2)}) %collective-permute-start.5) | collective-permute-done | bytes 1277984 | tf_op jit(solution)/shard_map/ppermute | solution.py:649
  428.0 2.7 add_convert_fusion.4
  430.7 1.2 fusion.16
  431.9 1.5 collective-permute-start.7
  433.4 3.7 add_convert_fusion.1.mine_ref
  437.1 7.1 %all-to-all-done.7 = bf16[8,136,768]{2,1,0:T(8,128)(2,1)} async-done(((bf16[8,136,768]{2,1,0:T(8,128)(2,1)}), bf16[8,136,768]{2,1,0:T(8,128)(2,1)}, u32[]{:S(2)}, u32[]{:S(2)}) %all-to-all-start.7) | async-done | bytes 1671200 | tf_op jit(solution)/shard_map/all_to_all | solution.py:655
  444.2 4.3 all-to-all-start.8
  448.5 10.7 %collective-permute-done.7 = bf16[384,1536]{1,0:T(8,128)(2,1)} collective-permute-done((bf16[384,1536]{1,0:T(8,128)(2,1)S(1)}, bf16[384,1536]{1,0:T(8,128)(2,1)}, u32[]{:S(2)}, u32[]{:S(2)}) %collective-permute-start.7) | collective-permute-done | bytes 1179680 | tf_op jit(solution)/shard_map/ppermute | solution.py:649
  459.2 1.6 add_convert_fusion.6.mine_ref
  461.0 1.6 collective-permute-start.11
  462.9 1.0 collective-permute-done.13
  463.8 1.5 collective-permute-start.14
  465.3 7.9 %widen.3 = f32[3072,768]{1,0:T(8,128)} custom-call(s32[1]{0:T(128)} %bitcast.26.core_ref, bf16[1536,768]{1,0:T(8,128)(2,1)} %add_convert_fusion.1.mine_ref, bf16[1536,768]{1,0:T(8,128)(2,1)} %collective-permute-done.6.theirs_ref), custom_call_target="tpu_custom_call" | custom-call | flops 1048576 | bytes 65536 | tf_op jit(solution)/shard_map/widen/pallas_call | solution.py:446
  473.2 8.2 %combine_output.1 = bf16[4,208,768]{2,1,0:T(8,128)(2,1)} custom-call(s32[4,8,208]{2,1,0:T(8,128)} %bitcast.71, f32[4,208,768]{2,1,0:T(8,128)} %get-tuple-element.126.refs_3_.mid_ref, bf16[1152,768]{1,0:T(8,128)(2,1)} %bitcast.28.refs_0_, bf16[1088,768]{1,0:T(8,128)(2,1)} %bitcast.31.refs_1_), custom_call_target="tpu_custom_call" | custom-call | flops 1048576 | bytes 65536 | tf_op jit(solution)/shard_map/combine_output/pallas_call | solution.py:483
  481.4 1.0 copy-done.15
  482.4 6.3 %widen.4.refs_0_ = f32[768,3072]{1,0:T(8,128)} custom-call(s32[1]{0:T(128)} %bitcast.26.core_ref, bf16[384,1536]{1,0:T(8,128)(2,1)} %copy-done.11, bf16[384,1536]{1,0:T(8,128)(2,1)} %copy-done.15), custom_call_target="tpu_custom_call" | custom-call | flops 1048576 | bytes 65536 | tf_op jit(solution)/shard_map/widen/pallas_call | solution.py:446
  488.7 1.6 reduce_sum.38
  492.3 1.5 copy.54
  493.8 1.5 copy.53
  496.3 1.9 add_convert_fusion.5.mine_ref
  502.3 1.0 copy-done.16
  503.3 6.3 %widen.5 = f32[768,3072]{1,0:T(8,128)} custom-call(s32[1]{0:T(128)} %bitcast.26.core_ref, bf16[384,1536]{1,0:T(8,128)(2,1)} %copy-done.12, bf16[384,1536]{1,0:T(8,128)(2,1)} %copy-done.16, f32[768,3072]{1,0:T(8,128)} %widen.4.refs_0_), custom_call_target="tpu_custom_call", output_to_operand_aliasing={{}: (3, {})} | custom-call | flops 1048576 | bytes 65536 | tf_op jit(solution)/shard_map/widen/pallas_call | solution.py:446
  (103 shorter events, 12.4 us)
Async XLA Ops:
  7.2 87.1 %all-gather.3.cloned.1.call-start = ((), (), s32[]{:S(2)}) async-start(), calls=%async_computation.9 | async-start | bytes 2764800 | tf_op jit(solution)/shard_map/all_gather | solution.py:723
  19.8 7.4 %copy-start.13 = (bf16[4,197,768]{2,0,1:T(4,128)(2,1)S(1)}, bf16[4,197,768]{2,0,1:T(4,128)(2,1)}, u32[]{:S(2)}) copy-start(bf16[4,197,768]{2,0,1:T(4,128)(2,1)} %param.17) | copy-start | bytes 3631108
  19.8 73.1 %all-to-all-start = ((bf16[8,144,768]{2,1,0:T(8,128)(2,1)}), bf16[8,144,768]{2,1,0:T(8,128)(2,1)S(1)}, u32[]{:S(2)}, u32[]{:S(2)}) async-start(bf16[8,144,768]{2,1,0:T(8,128)(2,1)} %bitcast.58), calls=%async_computation | async-start | bytes 3538944 | tf_op jit(solution)/shard_map/all_to_all | solution.py:655
  92.9 9.3 %copy-start.8 = (bf16[8,144,768]{2,1,0:T(8,128)(2,1)}, bf16[8,144,768]{2,1,0:T(8,128)(2,1)S(1)}, u32[]{:S(2)}) copy-start(bf16[8,144,768]{2,1,0:T(8,128)(2,1)S(1)} %all-to-all-done) | copy-start | bytes 5308420
  94.2 5.0 collective-permute-start
  94.3 43.5 %all-to-all-start.1 = ((bf16[8,136,768]{2,1,0:T(8,128)(2,1)}), bf16[8,136,768]{2,1,0:T(8,128)(2,1)S(1)}, u32[]{:S(2)}, u32[]{:S(2)}) async-start(bf16[8,136,768]{2,1,0:T(8,128)(2,1)} %bitcast.62), calls=%async_computation.1 | async-start | bytes 3342336 | tf_op jit(solution)/shard_map/all_to_all | solution.py:655
  102.5 2.2 copy-start
  137.8 8.4 %copy-start.9 = (bf16[8,136,768]{2,1,0:T(8,128)(2,1)}, bf16[8,136,768]{2,1,0:T(8,128)(2,1)S(1)}, u32[]{:S(2)}) copy-start(bf16[8,136,768]{2,1,0:T(8,128)(2,1)S(1)} %all-to-all-done.1) | copy-start | bytes 5013508
  137.8 45.1 %all-to-all-start.2 = ((bf16[8,144,768]{2,1,0:T(8,128)(2,1)}), bf16[8,144,768]{2,1,0:T(8,128)(2,1)S(1)}, u32[]{:S(2)}, u32[]{:S(2)}) async-start(bf16[8,144,768]{2,1,0:T(8,128)(2,1)} %bitcast.59), calls=%async_computation.2 | async-start | bytes 3538944 | tf_op jit(solution)/shard_map/all_to_all | solution.py:655
  182.9 5.5 %copy-start.1 = (bf16[8,144,768]{2,1,0:T(8,128)(2,1)}, bf16[8,144,768]{2,1,0:T(8,128)(2,1)S(1)}, u32[]{:S(2)}) copy-start(bf16[8,144,768]{2,1,0:T(8,128)(2,1)S(1)} %all-to-all-done.2) | copy-start | bytes 5308420
  182.9 48.3 %all-to-all-start.3 = ((bf16[8,136,768]{2,1,0:T(8,128)(2,1)}), bf16[8,136,768]{2,1,0:T(8,128)(2,1)S(1)}, u32[]{:S(2)}, u32[]{:S(2)}) async-start(bf16[8,136,768]{2,1,0:T(8,128)(2,1)} %bitcast.63), calls=%async_computation.3 | async-start | bytes 3342336 | tf_op jit(solution)/shard_map/all_to_all | solution.py:655
  231.2 6.5 %copy-start.2 = (bf16[8,136,768]{2,1,0:T(8,128)(2,1)}, bf16[8,136,768]{2,1,0:T(8,128)(2,1)S(1)}, u32[]{:S(2)}) copy-start(bf16[8,136,768]{2,1,0:T(8,128)(2,1)S(1)} %all-to-all-done.3) | copy-start | bytes 5013508
  231.2 47.2 %all-to-all-start.4 = ((bf16[8,144,768]{2,1,0:T(8,128)(2,1)}), bf16[8,144,768]{2,1,0:T(8,128)(2,1)S(1)}, u32[]{:S(2)}, u32[]{:S(2)}) async-start(bf16[8,144,768]{2,1,0:T(8,128)(2,1)} %bitcast.68), calls=%async_computation.4 | async-start | bytes 3538944 | tf_op jit(solution)/shard_map/all_to_all | solution.py:655
  278.4 24.9 %copy-start.7 = (bf16[8,144,768]{2,1,0:T(8,128)(2,1)}, bf16[8,144,768]{2,1,0:T(8,128)(2,1)S(1)}, u32[]{:S(2)}) copy-start(bf16[8,144,768]{2,1,0:T(8,128)(2,1)S(1)} %all-to-all-done.4) | copy-start | bytes 5308420
  278.4 44.0 %all-to-all-start.5 = ((bf16[8,136,768]{2,1,0:T(8,128)(2,1)}), bf16[8,136,768]{2,1,0:T(8,128)(2,1)S(1)}, u32[]{:S(2)}, u32[]{:S(2)}) async-start(bf16[8,136,768]{2,1,0:T(8,128)(2,1)} %bitcast.69), calls=%async_computation.5 | async-start | bytes 3342336 | tf_op jit(solution)/shard_map/all_to_all | solution.py:655
  322.4 5.3 %copy-start.10 = (bf16[8,136,768]{2,1,0:T(8,128)(2,1)}, bf16[8,136,768]{2,1,0:T(8,128)(2,1)S(1)}, u32[]{:S(2)}) copy-start(bf16[8,136,768]{2,1,0:T(8,128)(2,1)S(1)} %all-to-all-done.5) | copy-start | bytes 5013508
  322.4 5.3 %collective-permute-start.2 = (bf16[1536,768]{1,0:T(8,128)(2,1)}, bf16[1536,768]{1,0:T(8,128)(2,1)}, u32[]{:S(2)}, u32[]{:S(2)}) collective-permute-start(bf16[1536,768]{1,0:T(8,128)(2,1)} %get-tuple-element.139), channel_id=1, source_target_pairs={{0,8},{8,0},{16,24},{24,16},{1,9},{9,1},{17,25},{25,17},{2,10},{10... | collective-permute-start | bytes 7077896 | tf_op jit(solution)/shard_map/ppermute | solution.py:649
  322.4 52.3 %all-to-all-start.6 = ((bf16[8,144,768]{2,1,0:T(8,128)(2,1)}), bf16[8,144,768]{2,1,0:T(8,128)(2,1)}, u32[]{:S(2)}, u32[]{:S(2)}) async-start(bf16[8,144,768]{2,1,0:T(8,128)(2,1)} %bitcast.27), calls=%async_computation.6 | async-start | bytes 3538944 | tf_op jit(solution)/shard_map/all_to_all | solution.py:655
  330.7 44.0 %copy-start.5 = (bf16[1536,768]{1,0:T(8,128)(2,1)}, bf16[1536,768]{1,0:T(8,128)(2,1)S(1)}, u32[]{:S(2)}) copy-start(bf16[1536,768]{1,0:T(8,128)(2,1)S(1)} %add_convert_fusion.2) | copy-start | bytes 7077892
  330.7 53.5 %collective-permute-start.3 = (bf16[1536,768]{1,0:T(8,128)(2,1)S(1)}, bf16[1536,768]{1,0:T(8,128)(2,1)}, u32[]{:S(2)}, u32[]{:S(2)}) collective-permute-start(bf16[1536,768]{1,0:T(8,128)(2,1)S(1)} %add_convert_fusion.2), channel_id=1, source_target_pairs={{0,16},{8,24},{16,0},{24,8},{1,17},{9,25},{17,1},{25,9},{2,18},{10... | collective-permute-start | bytes 7077896 | tf_op jit(solution)/shard_map/ppermute | solution.py:649
  384.2 8.4 %collective-permute-start.4 = (bf16[768,1664]{1,0:T(8,128)(2,1)}, bf16[768,1664]{1,0:T(8,128)(2,1)S(1)}, u32[]{:S(2)}, u32[]{:S(2)}) collective-permute-start(bf16[768,1664]{1,0:T(8,128)(2,1)} %get-tuple-element.141), channel_id=1, source_target_pairs={{0,8},{8,0},{16,24},{24,16},{1,9},{9,1},{17,25},{25,17},{2,10},{10... | collective-permute-start | bytes 7667720 | tf_op jit(solution)/shard_map/ppermute | solution.py:649
  384.2 20.8 %collective-permute-start.1 = (bf16[384,3072]{1,0:T(8,128)(2,1)}, bf16[384,3072]{1,0:T(8,128)(2,1)}, u32[]{:S(2)}, u32[]{:S(2)}) collective-permute-start(bf16[384,3072]{1,0:T(8,128)(2,1)} %get-tuple-element.123), channel_id=1, source_target_pairs={{0,8},{8,0},{16,24},{24,16},{1,9},{9,1},{17,25},{25,17},{2,10},{10... | collective-permute-start | bytes 7077896 | tf_op jit(solution)/shard_map/ppermute | solution.py:649
  395.0 1.5 copy-start.3
  397.6 30.4 %collective-permute-start.5 = (bf16[8,48,1664]{2,1,0:T(8,128)(2,1)}, bf16[8,48,1664]{2,1,0:T(8,128)(2,1)}, u32[]{:S(2)}, u32[]{:S(2)}) collective-permute-start(bf16[8,48,1664]{2,1,0:T(8,128)(2,1)} %constant_dynamic-slice_fusion), channel_id=1, source_target_pairs={{0,16},{8,24},{16,0},{24,8},{1,17},{9,25},{17,1},{25,9},{2,18},{10... | collective-permute-start | bytes 3833864 | tf_op jit(solution)/shard_map/ppermute | solution.py:649
  399.0 45.2 %all-to-all-start.7 = ((bf16[8,136,768]{2,1,0:T(8,128)(2,1)}), bf16[8,136,768]{2,1,0:T(8,128)(2,1)}, u32[]{:S(2)}, u32[]{:S(2)}) async-start(bf16[8,136,768]{2,1,0:T(8,128)(2,1)} %bitcast.30), calls=%async_computation.7 | async-start | bytes 3342336 | tf_op jit(solution)/shard_map/all_to_all | solution.py:655
  405.0 23.0 %copy-start.4 = (bf16[768,1664]{1,0:T(8,128)(2,1)S(1)}, bf16[768,1664]{1,0:T(8,128)(2,1)}, u32[]{:S(2)}) copy-start(bf16[768,1664]{1,0:T(8,128)(2,1)} %copy-done.3) | copy-start | bytes 7667716
  430.7 2.7 copy-start.6
  431.9 27.3 %collective-permute-start.7 = (bf16[384,1536]{1,0:T(8,128)(2,1)S(1)}, bf16[384,1536]{1,0:T(8,128)(2,1)}, u32[]{:S(2)}, u32[]{:S(2)}) collective-permute-start(bf16[384,1536]{1,0:T(8,128)(2,1)S(1)} %get-tuple-element.231), channel_id=1, source_target_pairs={{0,16},{8,24},{16,0},{24,8},{1,17},{9,25},{17,1},{25,9},{2,18},{10... | collective-permute-start | bytes 3538952 | tf_op jit(solution)/shard_map/ppermute | solution.py:649
  437.1 28.2 %collective-permute-start.6 = (bf16[1536,768]{1,0:T(8,128)(2,1)}, bf16[1536,768]{1,0:T(8,128)(2,1)}, u32[]{:S(2)}, u32[]{:S(2)}) collective-permute-start(bf16[1536,768]{1,0:T(8,128)(2,1)} %add_convert_fusion.1.mine_ref), channel_id=1, source_target_pairs={{0,8},{8,0},{16,24},{24,16},{1,9},{9,1},{17,25},{25,17},{2,10},{10... | collective-permute-start | bytes 7077896 | tf_op jit(solution)/shard_map/ppermute | solution.py:649
  444.2 44.5 %all-to-all-start.8 = ((bf16[8,48,1664]{2,1,0:T(8,128)(2,1)}), bf16[8,48,1664]{2,1,0:T(8,128)(2,1)}, u32[]{:S(2)}, u32[]{:S(2)}) async-start(bf16[8,48,1664]{2,1,0:T(8,128)(2,1)} %add_convert_fusion.4), calls=%async_computation.8 | async-start | bytes 2555904 | tf_op jit(solution)/shard_map/all_to_all | solution.py:829
  448.5 12.4 %copy-start.19 = (f32[1,768]{1,0:T(1,128)S(1)}, f32[1,768]{1,0:T(1,128)}, u32[]{:S(2)}) copy-start(f32[1,768]{1,0:T(1,128)} %get-tuple-element.159) | copy-start | bytes 9220
  448.5 12.4 %copy-start.20 = (f32[1,768]{1,0:T(1,128)S(1)}, f32[1,768]{1,0:T(1,128)}, u32[]{:S(2)}) copy-start(f32[1,768]{1,0:T(1,128)} %get-tuple-element.160) | copy-start | bytes 9220
  448.5 12.4 %copy-start.17 = (f32[1,3072]{1,0:T(1,128)S(1)}, f32[1,3072]{1,0:T(1,128)}, u32[]{:S(2)}) copy-start(f32[1,3072]{1,0:T(1,128)} %get-tuple-element.157) | copy-start | bytes 36868
  448.5 12.4 %copy-start.18 = (f32[1,3072]{1,0:T(1,128)S(1)}, f32[1,3072]{1,0:T(1,128)}, u32[]{:S(2)}) copy-start(f32[1,3072]{1,0:T(1,128)} %get-tuple-element.158) | copy-start | bytes 36868
  460.8 12.4 %copy-start.11 = (bf16[384,1536]{1,0:T(8,128)(2,1)}, bf16[384,1536]{1,0:T(8,128)(2,1)S(1)}, u32[]{:S(2)}) copy-start(bf16[384,1536]{1,0:T(8,128)(2,1)S(1)} %add_convert_fusion.6.mine_ref) | copy-start | bytes 3538948
  460.8 20.5 %collective-permute-start.8 = (bf16[384,1536]{1,0:T(8,128)(2,1)S(1)}, bf16[384,1536]{1,0:T(8,128)(2,1)S(1)}, u32[]{:S(2)}, u32[]{:S(2)}) collective-permute-start(bf16[384,1536]{1,0:T(8,128)(2,1)S(1)} %add_convert_fusion.6.mine_ref), channel_id=1, source_target_pairs={{0,8},{8,0},{16,24},{24,16},{1,9},{9,1},{17,25},{25,17},{2,10},{10... | collective-permute-start | bytes 3538952 | tf_op jit(solution)/shard_map/ppermute | solution.py:649
  461.0 35.3 %collective-permute-start.11 = (bf16[384,1536]{1,0:T(8,128)(2,1)}, bf16[384,1536]{1,0:T(8,128)(2,1)}, u32[]{:S(2)}, u32[]{:S(2)}) collective-permute-start(bf16[384,1536]{1,0:T(8,128)(2,1)} %get-tuple-element.155), channel_id=1, source_target_pairs={{0,16},{8,24},{16,0},{24,8},{1,17},{9,25},{17,1},{25,9},{2,18},{10... | collective-permute-start | bytes 3538952 | tf_op jit(solution)/shard_map/ppermute | solution.py:649
  462.6 1.2 collective-permute-start.13
  463.8 27.1 %collective-permute-start.14 = (bf16[5,768]{1,0:T(8,128)(2,1)S(1)}, bf16[5,768]{1,0:T(8,128)(2,1)S(1)}, u32[]{:S(2)}, u32[]{:S(2)}) collective-permute-start(bf16[5,768]{1,0:T(8,128)(2,1)S(1)} %add_convert_fusion.8), channel_id=1, source_target_pairs={{0,16},{8,24},{16,0},{24,8},{1,17},{9,25},{17,1},{25,9},{2,18},{10... | collective-permute-start | bytes 23048 | tf_op jit(solution)/shard_map/ppermute | solution.py:649
  481.4 1.0 copy-start.15
  488.6 3.5 copy-start.14
  490.3 5.9 %collective-permute-start.9 = (bf16[48,1664]{1,0:T(8,128)(2,1)S(1)}, bf16[48,1664]{1,0:T(8,128)(2,1)S(1)}, u32[]{:S(2)}, u32[]{:S(2)}) collective-permute-start(bf16[48,1664]{1,0:T(8,128)(2,1)S(1)} %reduce_sum.38), channel_id=1, source_target_pairs={{0,16},{8,24},{16,0},{24,8},{1,17},{9,25},{17,1},{25,9},{2,18},{10... | collective-permute-start | bytes 479240 | tf_op jit(solution)/shard_map/ppermute | solution.py:649
  492.3 1.5 slice-start
  496.2 2.6 collective-permute-start.10
  498.2 1.8 copy-start.12
  498.2 4.1 collective-permute-start.12
  502.3 1.0 copy-start.16
Sparse Core Ops, SparseCore 0:
  10.8 83.4 all-gather.2
